TPU v7x, 256 devices: a whole 4x4x8 slice. The times are simulated.
256 devices in a mesh: slab: 128 (over x, y_lo, z, core), member: 2 (over y_hi).
Axes of the slice: x: 4, y: 4 (y_hi: 2, y_lo: 2; y = y_hi * 2 + y_lo), z: 8, core: 2. Of those that a mesh axis runs over, the one named last changes fastest.
Arguments:
- density: bfloat16 [256, 512, 256], P('slab', 'member'), parts along dimension 1, may hold values from -6 to 6
- amplitudes: bfloat16 [256, 512, 256], P('slab', 'member'), parts along dimension 1, may hold values from 0.25 to 4
- support: int32 [256, 512, 256], P('slab', 'member'), parts along dimension 1, may hold values 0 or 1
Outputs:
- updated: bfloat16 [256, 512, 256], P('slab', 'member'), parts along dimension 1
There are 2 independent parts, one for each index of `member`. A program takes and returns all parts, laid end to end along the dimension named above; each array names one. Nothing has to cross between parts.
Inputs may be any that keep to these rules, and one draw needn't show every extreme that they name: support holds only 0 and 1.
All inputs are finite; a program needn't handle non-finite values. No bound on the sum of `support` on one device may be relied on, other than what follows from the above.
Results may differ from a plain program's by a relative error of at most 0.0011.
Values may be sent and summed in bfloat16 or wider, within the bound.
No kernel may reach another device: no remote copies, remote signals or barrier semaphores. Data moves between devices by JAX's collectives and lax.ppermute only.
A program may use at most 64 MiB of HBM per device.

v0:
```python
import math

import jax
import jax.numpy as jnp
from jax import lax
from jax.sharding import PartitionSpec as P

modulus_floor = 0.25


def phase_pair(first, second, period):
    product = first[:, None] * second[None, :] % period
    angle = product.astype(jnp.float32) * (2.0 * math.pi / period)
    return (jnp.cos(angle), jnp.sin(angle))


def einsum_high(spec, left, right):
    return jnp.einsum(
        spec, left, right, precision=lax.Precision.HIGHEST, preferred_element_type=jnp.float32
    )


def contract(spec, data, table):
    data_real, data_imag = data
    table_cos, table_sin = table
    out_real = einsum_high(spec, data_real, table_cos)
    out_imag = einsum_high(spec, data_real, table_sin)
    out_real = out_real - einsum_high(spec, data_imag, table_sin)
    out_imag = out_imag + einsum_high(spec, data_imag, table_cos)
    return (out_real, out_imag)


def twiddle(data, table_cos, table_sin):
    data_real, data_imag = data
    if data_imag is None:
        return (data_real * table_cos, data_real * table_sin)
    return (
        data_real * table_cos - data_imag * table_sin,
        data_real * table_sin + data_imag * table_cos,
    )


def shift_tables(length, axis, ndim):
    positions = jnp.arange(length, dtype=jnp.int32)
    angle = ((length - 1) * positions % (2 * length)).astype(jnp.float32) * (math.pi / length)
    shape = [1] * ndim
    shape[axis] = length
    return (jnp.cos(angle).reshape(shape), jnp.sin(angle).reshape(shape))


def forward_axis(data, axis, kept):
    shape = data[0].shape
    length = shape[axis]
    radix = 16
    second = length // radix
    outer = math.prod(shape[:axis])
    inner = math.prod(shape[axis + 1 :])
    shift_cos, shift_sin = shift_tables(length, axis, len(shape))
    data_real, data_imag = twiddle(data, shift_cos, shift_sin)
    data_real = data_real.reshape(outer, radix, second, inner)
    data_imag = data_imag.reshape(outer, radix, second, inner)
    small = jnp.arange(radix, dtype=jnp.int32)
    first_cos, first_sin = phase_pair(small, small, radix)
    sectioned = contract("pabq,ka->pkbq", (data_real, data_imag), (first_cos, -first_sin))
    turn_cos, turn_sin = phase_pair(small, jnp.arange(second, dtype=jnp.int32), length)
    sectioned = twiddle(sectioned, turn_cos[None, :, :, None], -turn_sin[None, :, :, None])
    last_cos, last_sin = phase_pair(
        jnp.arange(kept, dtype=jnp.int32), jnp.arange(second, dtype=jnp.int32), second
    )
    out_real, out_imag = contract("pkbq,jb->pjkq", sectioned, (last_cos, -last_sin))
    new_shape = list(shape)
    new_shape[axis] = kept * radix
    scale = 1.0 / math.sqrt(length)
    return (out_real.reshape(new_shape) * scale, out_imag.reshape(new_shape) * scale)


def inverse_axis(data, axis, length, real_only):
    shape = data[0].shape
    radix = 16
    second = length // radix
    kept = shape[axis] // radix
    outer = math.prod(shape[:axis])
    inner = math.prod(shape[axis + 1 :])
    data_real = data[0].reshape(outer, kept, radix, inner)
    data_imag = data[1].reshape(outer, kept, radix, inner)
    first_cos, first_sin = phase_pair(
        jnp.arange(second, dtype=jnp.int32), jnp.arange(kept, dtype=jnp.int32), second
    )
    sectioned = contract("pjkq,bj->pkbq", (data_real, data_imag), (first_cos, first_sin))
    small = jnp.arange(radix, dtype=jnp.int32)
    turn_cos, turn_sin = phase_pair(small, jnp.arange(second, dtype=jnp.int32), length)
    sectioned = twiddle(sectioned, turn_cos[None, :, :, None], turn_sin[None, :, :, None])
    last_cos, last_sin = phase_pair(small, small, radix)
    out_real, out_imag = contract("pkbq,ak->pabq", sectioned, (last_cos, last_sin))
    new_shape = list(shape)
    new_shape[axis] = length
    scale = 1.0 / math.sqrt(length)
    out_real = out_real.reshape(new_shape) * scale
    out_imag = out_imag.reshape(new_shape) * scale
    shift_cos, shift_sin = shift_tables(length, axis, len(shape))
    if real_only:
        return out_real * shift_cos + out_imag * shift_sin
    return twiddle((out_real, out_imag), shift_cos, -shift_sin)


def shards(density, amplitudes, support):
    length = density.shape[2]
    second = length // 16
    fold = 1.0
    rho = density.astype(jnp.float32)
    spectrum = forward_axis((rho, None), 2, second)
    spectrum = forward_axis(spectrum, 1, second)
    spectrum = forward_axis(
        (
            lax.all_to_all(spectrum[0], "slab", split_axis=1, concat_axis=0, tiled=True),
            lax.all_to_all(spectrum[1], "slab", split_axis=1, concat_axis=0, tiled=True),
        ),
        0,
        second,
    )
    direct = amplitudes
    mirrored = amplitudes[:, ::-1, ::-1]
    direct, mirrored = (
        lax.all_to_all(direct, "slab", split_axis=1, concat_axis=0, tiled=True),
        lax.all_to_all(mirrored, "slab", split_axis=1, concat_axis=0, tiled=True),
    )
    target = 0.5 * (direct.astype(jnp.float32) + mirrored[::-1].astype(jnp.float32))
    spec_real, spec_imag = spectrum
    magnitude = jnp.sqrt(spec_real * spec_real + spec_imag * spec_imag)
    ratio = target / jnp.maximum(magnitude, modulus_floor)
    projected = inverse_axis((spec_real * ratio, spec_imag * ratio), 0, length, False)
    projected = inverse_axis(
        (
            lax.all_to_all(projected[0], "slab", split_axis=0, concat_axis=1, tiled=True),
            lax.all_to_all(projected[1], "slab", split_axis=0, concat_axis=1, tiled=True),
        ),
        1,
        length,
        False,
    )
    moduled = fold * inverse_axis(projected, 2, length, True)
    mask = support.astype(jnp.float32)
    updated = rho + mask * (2.0 * moduled - rho) - moduled
    return updated.astype(jnp.bfloat16)


def solution(mesh):
    in_specs = (P("slab", "member", None), P("slab", "member", None), P("slab", "member", None))
    out_specs = P("slab", "member", None)
    return jax.shard_map(shards, mesh=mesh, in_specs=in_specs, out_specs=out_specs, check_vma=False)
```

profile of v0, /device:TPU:1, one launch (start us, length us, event | category | flops | bytes accessed | tf_op | source)
XLA Modules:
  0.0 231.5 jit_solution(1350726113099511981)
XLA Ops:
  0.0 1.9 copy.235
  1.9 3.5 %rev.6 = bf16[2,256,256]{2,0,1:T(2,128)(2,1)} reverse(bf16[2,256,256]{2,0,1:T(2,128)(2,1)} %copy.235), dimensions={1,2} | reverse | bytes 524288 | tf_op jit(solution)/shard_map/rev | solution.py:122
  5.4 15.1 %all-to-all-start.3 = ((bf16[2,256,256]{2,0,1:T(2,128)(2,1)}), bf16[2,256,256]{2,0,1:T(2,128)(2,1)S(1)}, u32[]{:S(2)}, u32[]{:S(2)}) async-start(bf16[2,256,256]{2,0,1:T(2,128)(2,1)} %rev.6), calls=%async_computation.3 | async-start | bytes 524288 | tf_op jit(solution)/shard_map/all_to_all | solution.py:125
  20.6 1.0 convert_multiply_fusion
  25.8 1.0 add_bitcast_fusion.3
  29.4 3.7 %copy.206 = f32[512,16,16,1]{2,1,0,3:T(8,128)} copy(f32[512,16,16,1]{0,1,2,3:T(8,128)S(1)} %fusion.17) | data formatting | bytes 1048576 | tf_op jit(solution)/shard_map/sub | solution.py:28
  33.1 3.5 %reshape.377 = f32[2,16,16,256]{3,2,1,0:T(8,128)S(1)} reshape(f32[512,16,16,1]{2,1,0,3:T(8,128)} %copy.206) | data formatting | bytes 1048576 | tf_op jit(solution)/shard_map/reshape | solution.py:74
  37.4 3.7 %copy.209 = f32[512,16,16,1]{2,1,0,3:T(8,128)} copy(f32[512,16,16,1]{0,1,2,3:T(8,128)S(1)} %fusion.16) | data formatting | bytes 1048576 | tf_op jit(solution)/shard_map/add | solution.py:29
  41.2 3.9 %reshape.378 = f32[2,16,16,256]{3,2,1,0:T(8,128)S(1)} reshape(f32[512,16,16,1]{2,1,0,3:T(8,128)} %copy.209) | data formatting | bytes 1048576 | tf_op jit(solution)/shard_map/reshape | solution.py:74
  47.8 12.3 %all-to-all-start.2 = ((bf16[2,256,256]{2,0,1:T(2,128)(2,1)}), bf16[2,256,256]{2,0,1:T(2,128)(2,1)S(1)}, u32[]{:S(2)}, u32[]{:S(2)}) async-start(bf16[2,256,256]{2,0,1:T(2,128)(2,1)} %copy.235), calls=%async_computation.2 | async-start | bytes 524288 | tf_op jit(solution)/shard_map/all_to_all | solution.py:124
  60.2 1.0 add_bitcast_fusion.2
  63.2 1.2 copy.219
  64.4 10.4 %all-to-all-done.2 = bf16[2,256,256]{2,0,1:T(2,128)(2,1)S(1)} async-done(((bf16[2,256,256]{2,0,1:T(2,128)(2,1)}), bf16[2,256,256]{2,0,1:T(2,128)(2,1)S(1)}, u32[]{:S(2)}, u32[]{:S(2)}) %all-to-all-start.2) | async-done | bytes 262176 | tf_op jit(solution)/shard_map/all_to_all | solution.py:124
  74.8 5.5 %all-to-all-start = ((f32[2,256,256]{2,0,1:T(2,128)}), f32[2,256,256]{2,0,1:T(2,128)S(1)}, u32[]{:S(2)}, u32[]{:S(2)}) async-start(f32[2,256,256]{2,0,1:T(2,128)} %copy.219), calls=%async_computation | async-start | bytes 1048576 | tf_op jit(solution)/shard_map/all_to_all | solution.py:115
  82.4 1.2 copy.224
  83.6 16.8 %all-to-all-done = f32[2,256,256]{2,0,1:T(2,128)S(1)} async-done(((f32[2,256,256]{2,0,1:T(2,128)}), f32[2,256,256]{2,0,1:T(2,128)S(1)}, u32[]{:S(2)}, u32[]{:S(2)}) %all-to-all-start) | async-done | bytes 524320 | tf_op jit(solution)/shard_map/all_to_all | solution.py:115
  100.5 5.5 %all-to-all-start.1 = ((f32[2,256,256]{2,0,1:T(2,128)}), f32[2,256,256]{2,0,1:T(2,128)S(1)}, u32[]{:S(2)}, u32[]{:S(2)}) async-start(f32[2,256,256]{2,0,1:T(2,128)} %copy.224), calls=%async_computation.1 | async-start | bytes 1048576 | tf_op jit(solution)/shard_map/all_to_all | solution.py:116
  107.2 18.4 %all-to-all-done.1 = f32[2,256,256]{2,0,1:T(2,128)S(1)} async-done(((f32[2,256,256]{2,0,1:T(2,128)}), f32[2,256,256]{2,0,1:T(2,128)S(1)}, u32[]{:S(2)}, u32[]{:S(2)}) %all-to-all-start.1) | async-done | bytes 524320 | tf_op jit(solution)/shard_map/all_to_all | solution.py:116
  129.1 1.0 multiply_add_fusion.3
  134.8 1.2 fusion.412
  140.1 1.0 add_bitcast_fusion.1
  145.9 1.7 multiply_add_fusion.2
  147.6 25.0 %all_to_all.93 = f32[256,2,256]{2,1,0:T(2,128)S(1)} all-to-all(f32[256,2,256]{2,1,0:T(2,128)S(1)} %get-tuple-element.26), channel_id=1, replica_groups=mesh['slab'=128,'member'=2] {'slab'}, dimensions={0} | all-to-all | bytes 1048576 | tf_op jit(solution)/shard_map/all_to_all | solution.py:134
  172.6 5.5 %all-to-all-start.5 = ((f32[256,2,256]{2,1,0:T(2,128)}), f32[256,2,256]{2,1,0:T(2,128)S(1)}, u32[]{:S(2)}, u32[]{:S(2)}) async-start(f32[256,2,256]{2,1,0:T(2,128)} %get-tuple-element.25), calls=%async_computation.5 | async-start | bytes 1048576 | tf_op jit(solution)/shard_map/all_to_all | solution.py:135
  180.1 17.8 %all-to-all-done.5 = f32[256,2,256]{2,1,0:T(2,128)S(1)} async-done(((f32[256,2,256]{2,1,0:T(2,128)}), f32[256,2,256]{2,1,0:T(2,128)S(1)}, u32[]{:S(2)}, u32[]{:S(2)}) %all-to-all-start.5) | async-done | bytes 524320 | tf_op jit(solution)/shard_map/all_to_all | solution.py:135
  199.1 1.0 multiply_add_fusion.1
  202.6 4.4 %copy.283 = f32[2,16,16,256]{2,1,0,3:T(8,128)} copy(f32[2,16,16,256]{3,1,2,0:T(8,128)S(1)} %fusion.5) | data formatting | bytes 1048576 | tf_op jit(solution)/shard_map/reshape | solution.py:98
  207.0 4.5 %reshape.401 = f32[512,16,16]{0,2,1:T(8,128)S(1)} reshape(f32[2,16,16,256]{2,1,0,3:T(8,128)} %copy.283) | data formatting | bytes 1048576 | tf_op jit(solution)/shard_map/reshape | solution.py:98
  212.3 4.4 %copy.284 = f32[2,16,16,256]{2,1,0,3:T(8,128)} copy(f32[2,16,16,256]{3,1,2,0:T(8,128)S(1)} %fusion.4) | data formatting | bytes 1048576 | tf_op jit(solution)/shard_map/reshape | solution.py:99
  216.7 4.7 %reshape.402 = f32[512,16,16]{0,2,1:T(8,128)S(1)} reshape(f32[2,16,16,256]{2,1,0,3:T(8,128)} %copy.284) | data formatting | bytes 1048576 | tf_op jit(solution)/shard_map/reshape | solution.py:99
  224.2 1.0 add_bitcast_fusion
  230.4 0.9 fusion.22
  (94 shorter events, 46.9 us)
Async XLA Ops:
  5.4 42.4 %all-to-all-start.3 = ((bf16[2,256,256]{2,0,1:T(2,128)(2,1)}), bf16[2,256,256]{2,0,1:T(2,128)(2,1)S(1)}, u32[]{:S(2)}, u32[]{:S(2)}) async-start(bf16[2,256,256]{2,0,1:T(2,128)(2,1)} %rev.6), calls=%async_computation.3 | async-start | bytes 524288 | tf_op jit(solution)/shard_map/all_to_all | solution.py:125
  47.8 27.0 %all-to-all-start.2 = ((bf16[2,256,256]{2,0,1:T(2,128)(2,1)}), bf16[2,256,256]{2,0,1:T(2,128)(2,1)S(1)}, u32[]{:S(2)}, u32[]{:S(2)}) async-start(bf16[2,256,256]{2,0,1:T(2,128)(2,1)} %copy.235), calls=%async_computation.2 | async-start | bytes 524288 | tf_op jit(solution)/shard_map/all_to_all | solution.py:124
  74.8 25.6 %all-to-all-start = ((f32[2,256,256]{2,0,1:T(2,128)}), f32[2,256,256]{2,0,1:T(2,128)S(1)}, u32[]{:S(2)}, u32[]{:S(2)}) async-start(f32[2,256,256]{2,0,1:T(2,128)} %copy.219), calls=%async_computation | async-start | bytes 1048576 | tf_op jit(solution)/shard_map/all_to_all | solution.py:115
  100.5 25.2 %all-to-all-start.1 = ((f32[2,256,256]{2,0,1:T(2,128)}), f32[2,256,256]{2,0,1:T(2,128)S(1)}, u32[]{:S(2)}, u32[]{:S(2)}) async-start(f32[2,256,256]{2,0,1:T(2,128)} %copy.224), calls=%async_computation.1 | async-start | bytes 1048576 | tf_op jit(solution)/shard_map/all_to_all | solution.py:116
  172.6 25.4 %all-to-all-start.5 = ((f32[256,2,256]{2,1,0:T(2,128)}), f32[256,2,256]{2,1,0:T(2,128)S(1)}, u32[]{:S(2)}, u32[]{:S(2)}) async-start(f32[256,2,256]{2,1,0:T(2,128)} %get-tuple-element.25), calls=%async_computation.5 | async-start | bytes 1048576 | tf_op jit(solution)/shard_map/all_to_all | solution.py:135
  227.7 2.7 %copy-start = (bf16[2,256,256]{2,1,0:T(8,128)(2,1)S(1)}, bf16[2,256,256]{2,1,0:T(8,128)(2,1)}, u32[]{:S(2)}) copy-start(bf16[2,256,256]{2,1,0:T(8,128)(2,1)} %param.3) | copy-start | bytes 786436
  227.7 2.7 %copy-start.1 = (s32[2,256,256]{2,1,0:T(8,128)S(1)}, s32[2,256,256]{2,1,0:T(8,128)}, u32[]{:S(2)}) copy-start(s32[2,256,256]{2,1,0:T(8,128)} %param.5) | copy-start | bytes 1572868
where the time goes:
time: 235 us; the launch traced here: 231 us
  waiting for transfers between devices  63.5 us (27%)
  local copies, waits for them, and re-layouts  50.6 us (22%)
  starting transfers between devices  43.9 us (19%)
  matrix products  41.5 us (18%)
  blocking collectives  25 us (11%)
  other arithmetic  6.08 us (3%)
    dot_general x48, matrix products, einsum_high(): jnp.einsum(spec, left, right, precision=lax.Precision.HIGHEST, preferred_...  41.5 us
    all_to_all x1, blocking collectives, shards(): lax.all_to_all(projected[0], 'slab', split_axis=0, concat_axis=1, tiled=T...  25 us
    all_to_all x1, waiting for transfers between devices, shards(): lax.all_to_all(spectrum[1], 'slab', split_axis=1, concat_axis=0, tiled=True)  18.4 us
    all_to_all x1, waiting for transfers between devices, shards(): lax.all_to_all(projected[1], 'slab', split_axis=0, concat_axis=1, tiled=T...  17.8 us
    all_to_all x1, waiting for transfers between devices, shards(): lax.all_to_all(spectrum[0], 'slab', split_axis=1, concat_axis=0, tiled=True)  16.8 us
    all_to_all x1, starting transfers between devices, shards(): lax.all_to_all(mirrored, 'slab', split_axis=1, concat_axis=0, tiled=True)  15.1 us
    all_to_all x1, starting transfers between devices, shards(): lax.all_to_all(direct, 'slab', split_axis=1, concat_axis=0, tiled=True)  12.3 us
    all_to_all x1, waiting for transfers between devices, shards(): lax.all_to_all(direct, 'slab', split_axis=1, concat_axis=0, tiled=True)  10.4 us
  transfers between devices with their start and end apart: 5, of which 4 were waited for; matrix products, arithmetic and copies ran while one was open for 16% of the time, Pallas kernels for 0%

commit v1 on v0

v1 whole, which is shorter than its diff:
```python
import functools

import jax
import jax.numpy as jnp
import ml_dtypes
import numpy as np
from jax import lax
from jax.experimental import pallas as pl
from jax.experimental.pallas import tpu as pltpu
from jax.sharding import PartitionSpec as P

N = 256
CHIPS = 64
HALF = N // 2
QUARTER = N // 4
FLOOR = 0.25
FULL = 8190.0
FORWARD_LOW = -4
INVERSE_LOW = -9
AMP_UNIT = 512.0


def angles(k, position):
    turns = np.outer(2 * np.asarray(k) - (N - 1), np.asarray(position)) % (2 * N)
    return turns * (np.pi / N)


def split(table):
    high = table.astype(ml_dtypes.bfloat16)
    low = (table - high.astype(np.float64)).astype(ml_dtypes.bfloat16)
    return high, low


def two(tables):
    highs, lows = zip(*(split(t) for t in tables))
    return np.stack(highs), np.stack(lows)


@functools.cache
def constants():
    out = {}
    scale = 1.0 / np.sqrt(N)
    every = np.arange(N)
    half = np.arange(HALF)
    forward, inverse = [], []
    for core in range(2):
        kx = np.tile(np.arange(QUARTER) + QUARTER * core, 2)
        a = angles(kx, every)
        forward.append(np.concatenate([np.cos(a), -np.sin(a)], 0).T * scale)
        inverse.append(np.concatenate([np.cos(a), -np.sin(a)], 0) * (2.0 * scale))
    out["tx"] = two(forward)
    out["txi"] = two(inverse)
    a = angles(half, every)
    out["ty"] = split(np.concatenate([np.cos(a), np.sin(a)], 0) * scale)
    out["tyi"] = split(np.concatenate([np.cos(a), np.sin(a)], 0).T * scale)
    forward, inverse = [], []
    for core in range(2):
        planes = [0, 1, 2, 3] if core == 0 else [2, 3, 0, 1]
        z = np.concatenate([4 * np.arange(CHIPS) + p for p in planes])
        a = angles(z, z)
        forward.append(np.concatenate([np.cos(a), np.sin(a)], 0) * scale)
        inverse.append(np.concatenate([np.cos(a.T), np.sin(a.T)], 0) * scale)
    out["tz"] = two(forward)
    out["tzi"] = two(inverse)
    picks = []
    for core in range(2):
        pick = np.zeros((2 * N, 2 * HALF))
        for h in range(2):
            for j in range(QUARTER):
                kx = QUARTER * core + j
                pick[N * h + kx, QUARTER * h + j] = 1
                pick[N * (1 - h) + N - 1 - kx, HALF + QUARTER * h + j] = 1
        picks.append(pick)
    out["pick"] = np.stack(picks).astype(ml_dtypes.bfloat16)
    out["rev_half"] = np.eye(HALF)[::-1].astype(ml_dtypes.bfloat16)
    out["rev_all"] = np.eye(N)[::-1].astype(ml_dtypes.bfloat16)
    return out


def mm(a, b):
    return jnp.dot(a, b, preferred_element_type=jnp.float32)


def cut(x):
    high = x.astype(jnp.bfloat16)
    return high, (x - high.astype(jnp.float32)).astype(jnp.bfloat16)


def left3(high, low, x):
    xh, xl = cut(x)
    return mm(high, xh) + (mm(high, xl) + mm(low, xh))


def right3(x, high, low):
    xh, xl = cut(x)
    return mm(xh, high) + (mm(xl, high) + mm(xh, low))


def pack(re, im, low):
    m = jnp.maximum(jnp.maximum(jnp.abs(re), jnp.abs(im)), 1e-30)
    e = jnp.clip(jnp.floor(jnp.log2(m)) + (1.0 - low), 0.0, 15.0)
    s = jnp.exp2(-(e + low)) * FULL
    a = jnp.floor(re * s + 0.5).astype(jnp.int32)
    b = jnp.floor(im * s + 0.5).astype(jnp.int32)
    return (a << 18) | ((b & 0x3FFF) << 4) | e.astype(jnp.int32)


def unpack(word, low):
    s = jnp.exp2((word & 15).astype(jnp.float32) + low) * (1.0 / FULL)
    re = (word >> 18).astype(jnp.float32) * s
    im = ((word << 14) >> 18).astype(jnp.float32) * s
    return re, im


def signs(y_axis_len):
    y = lax.broadcasted_iota(jnp.int32, (y_axis_len, 2 * HALF), 0)
    lane = lax.broadcasted_iota(jnp.int32, (y_axis_len, 2 * HALF), 1)
    odd = (y & 1) * ((lane >> 6) & 1)
    return (1 - 2 * odd).astype(jnp.float32)


def forward_kernel(core_ref, own, other, amp_own, amp_other, txh, txl, tyh, tyl, pick, rev, out):
    core = core_ref[0]
    sign = signs(N)
    table_high, table_low = txh[core], txl[core]
    chosen = pick[core]
    for p in range(4):
        rho = (own if p < 2 else other)[p % 2]
        a = (mm(rho, table_high) + mm(rho, table_low)) * sign
        u = left3(tyh[...], tyl[...], a)
        re = u[:HALF, :HALF] + u[HALF:, HALF:]
        im = u[:HALF, HALF:] - u[HALF:, :HALF]
        word = pack(re, im, FORWARD_LOW)
        amp = (amp_own if p < 2 else amp_other)[p % 2]
        both = mm(jnp.concatenate([amp[:HALF], amp[HALF:]], 1), chosen)
        direct = both[:, :HALF]
        mirror = mm(rev[...], both[:, HALF:].astype(jnp.bfloat16))
        coded = ((direct * AMP_UNIT).astype(jnp.int32) << 16) | (mirror * AMP_UNIT).astype(jnp.int32)
        for r in range(2):
            rows = slice(CHIPS * r, CHIPS * (r + 1))
            out[pl.ds(2 * p + r, CHIPS, stride=16), :] = word[rows]
            out[pl.ds(8 + 2 * p + r, CHIPS, stride=16), :] = coded[rows]


def middle_kernel(core_ref, msg, tzh, tzl, tzih, tzil, rev, out):
    core = core_ref[0]

    def gather(first):
        return jnp.concatenate(
            [
                jnp.concatenate(
                    [msg[pl.ds(first + 2 * p + r, CHIPS, stride=16), :] for p in range(4)], 0
                )
                for r in range(2)
            ],
            1,
        )

    re, im = unpack(gather(0), FORWARD_LOW)
    u = left3(tzh[core], tzl[core], jnp.concatenate([re, im], 1))
    re = u[:N, :N] + u[N:, N:]
    im = u[:N, N:] - u[N:, :N]
    coded = gather(8)
    direct = (coded >> 16).astype(jnp.float32)
    mirror = mm(rev[...], (coded & 0xFFFF).astype(jnp.float32).astype(jnp.bfloat16))
    target = (direct + mirror) * (0.5 / AMP_UNIT)
    ratio = target / jnp.maximum(jnp.sqrt(re * re + im * im), FLOOR)
    u = left3(tzih[core], tzil[core], jnp.concatenate([re * ratio, im * ratio], 1))
    word = pack(u[:N, :N] - u[N:, N:], u[:N, N:] + u[N:, :N], INVERSE_LOW)
    for p in range(4):
        for r in range(2):
            out[pl.ds(2 * p + r, CHIPS, stride=8), :] = word[
                CHIPS * p : CHIPS * (p + 1), HALF * r : HALF * (r + 1)
            ]


def inverse_kernel(core_ref, own, other, rho_ref, support, tyh, tyl, txh, txl, out):
    core = core_ref[0]
    sign = signs(N)
    for q in range(2):
        moduled = None
        for part, (ref, first, c) in enumerate(((own, 2 * q, core), (other, 4 + 2 * q, 1 - core))):
            word = jnp.concatenate(
                [ref[pl.ds(first + r, CHIPS, stride=8), :] for r in range(2)], 0
            )
            re, im = unpack(word, INVERSE_LOW)
            g = jnp.concatenate(
                [jnp.concatenate([re, im], 1), jnp.concatenate([-im, re], 1)], 0
            )
            lines = left3(tyh[...], tyl[...], g) * sign
            term = right3(lines, txh[c], txl[c])
            moduled = term if moduled is None else moduled + term
        rho = rho_ref[q].astype(jnp.float32)
        mask = support[q].astype(jnp.float32)
        out[q] = (rho + mask * (2.0 * moduled - rho) - moduled).astype(jnp.bfloat16)


def call(kernel, out_shape, core, *operands):
    return pl.pallas_call(
        kernel,
        out_shape=out_shape,
        in_specs=[pl.BlockSpec(memory_space=pltpu.SMEM)]
        + [pl.BlockSpec(memory_space=pltpu.VMEM)] * len(operands),
        out_specs=pl.BlockSpec(memory_space=pltpu.VMEM),
        compiler_params=pltpu.CompilerParams(vmem_limit_bytes=48 * 2**20),
    )(core, *operands)


def shards(density, amplitudes, support):
    c = {k: jax.tree.map(jnp.asarray, v) for k, v in constants().items()}
    swap = [(i, i ^ 1) for i in range(2 * CHIPS)]
    same_core = [list(range(core, 2 * CHIPS, 2)) for core in range(2)]
    core = (lax.axis_index("slab") % 2).astype(jnp.int32).reshape(1)

    def exchange(x):
        return lax.all_to_all(
            x, "slab", split_axis=0, concat_axis=0, tiled=True, axis_index_groups=same_core
        )

    density_other = lax.ppermute(density, "slab", swap)
    amplitudes_other = lax.ppermute(amplitudes, "slab", swap)
    sent = call(
        forward_kernel,
        jax.ShapeDtypeStruct((CHIPS * 16, HALF), jnp.int32),
        core, density, density_other, amplitudes, amplitudes_other,
        *c["tx"], *c["ty"], c["pick"], c["rev_half"],
    )
    lines = exchange(sent.reshape(CHIPS, 16, HALF)).reshape(CHIPS * 16, HALF)
    sent = call(
        middle_kernel,
        jax.ShapeDtypeStruct((CHIPS * 8, HALF), jnp.int32),
        core, lines, *c["tz"], *c["tzi"], c["rev_all"],
    )
    planes = exchange(sent.reshape(CHIPS, 8, HALF)).reshape(CHIPS * 8, HALF)
    planes_other = lax.ppermute(planes, "slab", swap)
    return call(
        inverse_kernel,
        jax.ShapeDtypeStruct(density.shape, jnp.bfloat16),
        core, planes, planes_other, density, support, *c["tyi"], *c["txi"],
    )


def solution(mesh):
    spec = P("slab", "member", None)
    return jax.shard_map(
        shards, mesh=mesh, in_specs=(spec, spec, spec), out_specs=spec, check_vma=False
    )
```

time: 235 us -> 68.2 us (0.29); the launches traced: 231 us -> 67.8 us
  waiting for transfers between devices: 63.5 us -> 2.91 us
  local copies, waits for them, and re-layouts: 50.6 us -> 6.72 us
  matrix products: 41.5 us -> 0 us
  starting transfers between devices: 43.9 us -> 6.75 us
  blocking collectives: 25 us -> 44.9 us
  Pallas kernels: 0 us -> 6.44 us
  other arithmetic: 6.08 us -> 0 us
    all_to_all x5 -> x0, waiting for transfers between devices: 63.5 us -> none  [the longest x1 18.4 us: shards(): lax.all_to_all(spectrum[1], 'slab', split_axis=1, concat_axis=0, tiled=True)]
    all_to_all x5 -> x0, starting transfers between devices: 43.9 us -> none  [the longest x1 15.1 us: shards(): lax.all_to_all(mirrored, 'slab', split_axis=1, concat_axis=0, tiled=True)]
    dot_general x48 -> x0, matrix products: 41.5 us -> none  [einsum_high(): jnp.einsum(spec, left, right, precision=lax.Precision.HIGHEST, preferred_...]
    reshape x13 -> x0, local copies, waits for them, and re-layouts: 27.5 us -> none  [the longest x5 9.95 us: inverse_axis(): out_imag = out_imag.reshape(new_shape) * scale]
    all_to_all x1 -> x2, blocking collectives: 25 us -> 44.9 us  [exchange(): lax.all_to_all(x, 'slab', split_axis=0, concat_axis=0, tiled=True, axis_i...]
    ppermute x0 -> x3, starting transfers between devices: none -> 6.75 us  [the longest x1 3.5 us: shards(): planes_other = lax.ppermute(planes, 'slab', swap)]
    pallas_call x0 -> x3, Pallas kernels: none -> 6.44 us  [call(): pl.pallas_call(kernel, out_shape=out_shape, in_specs=[pl.BlockSpec(memory...]
    mul x10 -> x0, local copies, waits for them, and re-layouts: 4.81 us -> none  [the longest x4 2.18 us: forward_axis(): out_real.reshape(new_shape) * scale]
  transfers between devices with their start and end apart: 5 -> 3, of which waited for: 4 -> 3; matrix products, arithmetic and copies ran while one was open for 16% -> 0% of each run, Pallas kernels for 0% -> 0%
where the time goes in v1:
time: 68.2 us; the launch traced here: 67.8 us
  blocking collectives  44.9 us (66%)
  starting transfers between devices  6.75 us (10%)
  local copies, waits for them, and re-layouts  6.72 us (10%)
  Pallas kernels  6.44 us (9%)
  waiting for transfers between devices  2.91 us (4%)
    all_to_all x2, blocking collectives, exchange(): lax.all_to_all(x, 'slab', split_axis=0, concat_axis=0, tiled=True, axis_i...  44.9 us
    unnamed x38, local copies, waits for them, and re-layouts  6.72 us
    pallas_call x3, Pallas kernels, call(): pl.pallas_call(kernel, out_shape=out_shape, in_specs=[pl.BlockSpec(memory...  6.44 us
    ppermute x1, starting transfers between devices, shards(): planes_other = lax.ppermute(planes, 'slab', swap)  3.5 us
    ppermute x1, starting transfers between devices, shards(): amplitudes_other = lax.ppermute(amplitudes, 'slab', swap)  3.24 us
    ppermute x1, waiting for transfers between devices, shards(): amplitudes_other = lax.ppermute(amplitudes, 'slab', swap)  1.37 us
  transfers between devices with their start and end apart: 3, of which 3 were waited for; matrix products, arithmetic and copies ran while one was open for 0% of the time, Pallas kernels for 0%

profile of v1, /device:TPU:1, one launch (start us, length us, event | category | flops | bytes accessed | tf_op | source)
XLA Modules:
  0.0 67.8 jit_solution(11824504014716994942)
XLA Ops:
  0.0 3.2 %collective-permute-start.1 = (bf16[2,256,256]{2,1,0:T(8,128)(2,1)}, bf16[2,256,256]{2,1,0:T(8,128)(2,1)S(1)}, u32[]{:S(2)}, u32[]{:S(2)}) collective-permute-start(bf16[2,256,256]{2,1,0:T(8,128)(2,1)} %amp_own.1), channel_id=1, source_target_pairs={{0,2},{2,0},{4,6},{6,4},{8,10},{10,8},{12,14},{14,12},{16,18},{18,... | collective-permute-start | bytes 786440 | tf_op jit(solution)/shard_map/ppermute | solution.py:221
  3.2 0.0 collective-permute-start
  3.2 1.4 %collective-permute-done.1.amp_other = bf16[2,256,256]{2,1,0:T(8,128)(2,1)S(1)} collective-permute-done((bf16[2,256,256]{2,1,0:T(8,128)(2,1)}, bf16[2,256,256]{2,1,0:T(8,128)(2,1)S(1)}, u32[]{:S(2)}, u32[]{:S(2)}) %collective-permute-start.1) | collective-permute-done | bytes 262176 | tf_op jit(solution)/shard_map/ppermute | solution.py:221
  4.6 0.4 collective-permute-done.other
  5.0 0.0 copy-done.18
  5.0 0.9 %copy-done = bf16[2,256,256]{2,1,0:T(8,128)(2,1)S(1)} copy-done((bf16[2,256,256]{2,1,0:T(8,128)(2,1)S(1)}, bf16[2,256,256]{2,1,0:T(8,128)(2,1)}, u32[]{:S(2)}) %copy-start) | copy-done | bytes 262168
  5.9 1.0 %copy-done.7 = bf16[2,512,256]{2,1,0:T(8,128)(2,1)S(1)} copy-done((bf16[2,512,256]{2,1,0:T(8,128)(2,1)S(1)}, bf16[2,512,256]{2,1,0:T(8,128)(2,1)}, u32[]{:S(2)}) %copy-start.7) | copy-done | bytes 524312
  7.0 0.9 %copy-done.8 = bf16[2,256,256]{2,1,0:T(8,128)(2,1)S(1)} copy-done((bf16[2,256,256]{2,1,0:T(8,128)(2,1)S(1)}, bf16[2,256,256]{2,1,0:T(8,128)(2,1)}, u32[]{:S(2)}) %copy-start.8) | copy-done | bytes 262168
  7.9 0.9 %copy-done.11 = bf16[2,256,256]{2,1,0:T(8,128)(2,1)S(1)} copy-done((bf16[2,256,256]{2,1,0:T(8,128)(2,1)S(1)}, bf16[2,256,256]{2,1,0:T(8,128)(2,1)}, u32[]{:S(2)}) %copy-start.11) | copy-done | bytes 262168
  8.9 0.9 %copy-done.12 = bf16[2,256,256]{2,1,0:T(8,128)(2,1)S(1)} copy-done((bf16[2,256,256]{2,1,0:T(8,128)(2,1)S(1)}, bf16[2,256,256]{2,1,0:T(8,128)(2,1)}, u32[]{:S(2)}) %copy-start.12) | copy-done | bytes 262168
  9.8 0.9 %copy-done.16 = bf16[256,256]{1,0:T(8,128)(2,1)S(1)} copy-done((bf16[256,256]{1,0:T(8,128)(2,1)S(1)}, bf16[256,256]{1,0:T(8,128)(2,1)}, u32[]{:S(2)}) %copy-start.16) | copy-done | bytes 131096
  10.7 0.9 %copy-done.17 = bf16[256,256]{1,0:T(8,128)(2,1)S(1)} copy-done((bf16[256,256]{1,0:T(8,128)(2,1)S(1)}, bf16[256,256]{1,0:T(8,128)(2,1)}, u32[]{:S(2)}) %copy-start.17) | copy-done | bytes 131096
  11.7 2.1 %shard_map.172 = s32[1024,128]{1,0:T(8,128)S(1)} custom-call(s32[1]{0:T(128)} %bitcast.core_ref, bf16[2,256,256]{2,1,0:T(8,128)(2,1)S(1)} %copy-done, bf16[2,256,256]{2,1,0:T(8,128)(2,1)S(1)} %collective-permute-done.other, bf16[2,256,256]{2,1,0:T(8,128)(2,1)S(1)} %copy-done.8, bf16[2,256,256]{2,1,0:T(8,128)(2,1)S(1)} %collective-permute-done.1.amp_other, ...), custom_call_target="tpu_custom_call" | custom-call | tf_op jit(solution)/shard_map/pallas_call | solution.py:199
  13.8 0.0 copy-start.3
  13.8 0.0 copy-start.4
  13.8 27.1 %all_to_all.10 = s32[64,16,128]{2,1,0:T(8,128)S(1)} all-to-all(s32[64,16,128]{2,1,0:T(8,128)S(1)} %bitcast.5), channel_id=1, replica_groups={{0,4,8,12,16,20,24,28,32,36,40,44,48,52,56,60,64,68,72,76,80,84,88,92,9..., dimensions={0} | all-to-all | bytes 1048576 | tf_op jit(solution)/shard_map/all_to_all | solution.py:216
  40.9 0.0 copy-done.3
  41.0 0.0 copy-done.4
  41.0 0.0 copy-start.2
  41.0 0.0 copy-start.10
  41.0 0.0 copy-start.13
  41.0 0.0 copy-start.14
  41.0 2.3 %shard_map.173 = s32[512,128]{1,0:T(8,128)S(1)} custom-call(s32[1]{0:T(128)} %bitcast.core_ref, s32[1024,128]{1,0:T(8,128)S(1)} %bitcast.6, bf16[2,512,256]{2,1,0:T(8,128)(2,1)S(1)} %copy-done.6, bf16[2,512,256]{2,1,0:T(8,128)(2,1)S(1)} %copy-done.5, bf16[2,512,256]{2,1,0:T(8,128)(2,1)S(1)} %copy-done.4, bf16[2,512,256]{2,1,0:T(8,128)(2,1)S(1)} %copy-done.3, ...), custom_call_target="tpu_custom_call" | custom-call | tf_op jit(solution)/shard_map/pallas_call | solution.py:199
  43.3 0.0 copy-start.1
  43.4 0.0 copy-start.9
  43.4 17.8 %all_to_all.11 = s32[64,8,128]{2,1,0:T(8,128)S(1)} all-to-all(s32[64,8,128]{2,1,0:T(8,128)S(1)} %bitcast.9), channel_id=1, replica_groups={{0,4,8,12,16,20,24,28,32,36,40,44,48,52,56,60,64,68,72,76,80,84,88,92,9..., dimensions={0} | all-to-all | bytes 524288 | tf_op jit(solution)/shard_map/all_to_all | solution.py:216
  61.1 3.5 %collective-permute-start.2 = (s32[512,128]{1,0:T(8,128)S(1)}, s32[512,128]{1,0:T(8,128)S(1)}, u32[]{:S(2)}, u32[]{:S(2)}) collective-permute-start(s32[512,128]{1,0:T(8,128)S(1)} %bitcast.7), channel_id=1, source_target_pairs={{0,2},{2,0},{4,6},{6,4},{8,10},{10,8},{12,14},{14,12},{16,18},{18,... | collective-permute-start | bytes 786440 | tf_op jit(solution)/shard_map/ppermute | solution.py:235
  64.6 1.2 %collective-permute-done.2.other = s32[512,128]{1,0:T(8,128)S(1)} collective-permute-done((s32[512,128]{1,0:T(8,128)S(1)}, s32[512,128]{1,0:T(8,128)S(1)}, u32[]{:S(2)}, u32[]{:S(2)}) %collective-permute-start.2) | collective-permute-done | bytes 262176 | tf_op jit(solution)/shard_map/ppermute | solution.py:235
  65.8 0.0 copy-done.2
  65.8 0.0 copy-done.1
  65.8 0.0 copy-done.9
  65.8 2.0 %shard_map.174 = bf16[2,256,256]{2,1,0:T(8,128)(2,1)} custom-call(s32[1]{0:T(128)} %bitcast.core_ref, s32[512,128]{1,0:T(8,128)S(1)} %bitcast.8, s32[512,128]{1,0:T(8,128)S(1)} %collective-permute-done.2.other, bf16[2,256,256]{2,1,0:T(8,128)(2,1)S(1)} %copy-done.1, s32[2,256,256]{2,1,0:T(8,128)S(1)} %copy-done.2, bf16[256,256]{1,0:T(8,128)(2,1)S(1)} %copy-done.14, ...), custom_call_target="tpu_custom_call" | custom-call | tf_op jit(solution)/shard_map/pallas_call | solution.py:199
  (17 shorter events, 0.0 us)
Async XLA Ops:
  0.0 5.0 %copy-start.18 = (bf16[128,128]{1,0:T(8,128)(2,1)S(1)}, bf16[128,128]{1,0:T(8,128)(2,1)}, u32[]{:S(2)}) copy-start(bf16[128,128]{1,0:T(8,128)(2,1)} %constant.62.clone.rev) | copy-start | bytes 98308
  0.0 4.6 %collective-permute-start.1 = (bf16[2,256,256]{2,1,0:T(8,128)(2,1)}, bf16[2,256,256]{2,1,0:T(8,128)(2,1)S(1)}, u32[]{:S(2)}, u32[]{:S(2)}) collective-permute-start(bf16[2,256,256]{2,1,0:T(8,128)(2,1)} %amp_own.1), channel_id=1, source_target_pairs={{0,2},{2,0},{4,6},{6,4},{8,10},{10,8},{12,14},{14,12},{16,18},{18,... | collective-permute-start | bytes 786440 | tf_op jit(solution)/shard_map/ppermute | solution.py:221
  3.2 1.7 %collective-permute-start = (bf16[2,256,256]{2,1,0:T(8,128)(2,1)}, bf16[2,256,256]{2,1,0:T(8,128)(2,1)S(1)}, u32[]{:S(2)}, u32[]{:S(2)}) collective-permute-start(bf16[2,256,256]{2,1,0:T(8,128)(2,1)} %rho_ref.1), channel_id=1, source_target_pairs={{0,2},{2,0},{4,6},{6,4},{8,10},{10,8},{12,14},{14,12},{16,18},{18,... | collective-permute-start | bytes 786440 | tf_op jit(solution)/shard_map/ppermute | solution.py:220
  5.0 1.0 %copy-start = (bf16[2,256,256]{2,1,0:T(8,128)(2,1)S(1)}, bf16[2,256,256]{2,1,0:T(8,128)(2,1)}, u32[]{:S(2)}) copy-start(bf16[2,256,256]{2,1,0:T(8,128)(2,1)} %rho_ref.1) | copy-start | bytes 786436
  5.9 1.0 %copy-start.7 = (bf16[2,512,256]{2,1,0:T(8,128)(2,1)S(1)}, bf16[2,512,256]{2,1,0:T(8,128)(2,1)}, u32[]{:S(2)}) copy-start(bf16[2,512,256]{2,1,0:T(8,128)(2,1)} %constant.61.clone.pick) | copy-start | bytes 1572868
  7.0 0.9 %copy-start.8 = (bf16[2,256,256]{2,1,0:T(8,128)(2,1)S(1)}, bf16[2,256,256]{2,1,0:T(8,128)(2,1)}, u32[]{:S(2)}) copy-start(bf16[2,256,256]{2,1,0:T(8,128)(2,1)} %amp_own.1) | copy-start | bytes 786436
  7.9 0.9 %copy-start.11 = (bf16[2,256,256]{2,1,0:T(8,128)(2,1)S(1)}, bf16[2,256,256]{2,1,0:T(8,128)(2,1)}, u32[]{:S(2)}) copy-start(bf16[2,256,256]{2,1,0:T(8,128)(2,1)} %constant.50.clone.txl) | copy-start | bytes 786436
  8.9 0.9 %copy-start.12 = (bf16[2,256,256]{2,1,0:T(8,128)(2,1)S(1)}, bf16[2,256,256]{2,1,0:T(8,128)(2,1)}, u32[]{:S(2)}) copy-start(bf16[2,256,256]{2,1,0:T(8,128)(2,1)} %constant.49.clone.txh) | copy-start | bytes 786436
  9.8 0.9 %copy-start.16 = (bf16[256,256]{1,0:T(8,128)(2,1)S(1)}, bf16[256,256]{1,0:T(8,128)(2,1)}, u32[]{:S(2)}) copy-start(bf16[256,256]{1,0:T(8,128)(2,1)} %constant.54.clone.tyl) | copy-start | bytes 393220
  10.7 0.9 %copy-start.17 = (bf16[256,256]{1,0:T(8,128)(2,1)S(1)}, bf16[256,256]{1,0:T(8,128)(2,1)}, u32[]{:S(2)}) copy-start(bf16[256,256]{1,0:T(8,128)(2,1)} %constant.53.clone.tyh) | copy-start | bytes 393220
  11.6 29.3 %copy-start.5 = (bf16[2,512,256]{2,1,0:T(8,128)(2,1)S(1)}, bf16[2,512,256]{2,1,0:T(8,128)(2,1)}, u32[]{:S(2)}) copy-start(bf16[2,512,256]{2,1,0:T(8,128)(2,1)} %constant.58.clone.tzl) | copy-start | bytes 1572868
  11.7 29.3 %copy-start.6 = (bf16[2,512,256]{2,1,0:T(8,128)(2,1)S(1)}, bf16[2,512,256]{2,1,0:T(8,128)(2,1)}, u32[]{:S(2)}) copy-start(bf16[2,512,256]{2,1,0:T(8,128)(2,1)} %constant.57.clone.tzh) | copy-start | bytes 1572868
  11.7 29.3 %copy-start.15 = (bf16[256,256]{1,0:T(8,128)(2,1)S(1)}, bf16[256,256]{1,0:T(8,128)(2,1)}, u32[]{:S(2)}) copy-start(bf16[256,256]{1,0:T(8,128)(2,1)} %constant.63.clone.rev) | copy-start | bytes 393220
  13.8 27.2 %copy-start.3 = (bf16[2,512,256]{2,1,0:T(8,128)(2,1)S(1)}, bf16[2,512,256]{2,1,0:T(8,128)(2,1)}, u32[]{:S(2)}) copy-start(bf16[2,512,256]{2,1,0:T(8,128)(2,1)} %constant.60.clone.tzil) | copy-start | bytes 1572868
  13.8 27.2 %copy-start.4 = (bf16[2,512,256]{2,1,0:T(8,128)(2,1)S(1)}, bf16[2,512,256]{2,1,0:T(8,128)(2,1)}, u32[]{:S(2)}) copy-start(bf16[2,512,256]{2,1,0:T(8,128)(2,1)} %constant.59.clone.tzih) | copy-start | bytes 1572868
  41.0 24.9 %copy-start.2 = (s32[2,256,256]{2,1,0:T(8,128)S(1)}, s32[2,256,256]{2,1,0:T(8,128)}, u32[]{:S(2)}) copy-start(s32[2,256,256]{2,1,0:T(8,128)} %support.1) | copy-start | bytes 1572868
  41.0 24.8 %copy-start.10 = (bf16[2,256,256]{2,1,0:T(8,128)(2,1)S(1)}, bf16[2,256,256]{2,1,0:T(8,128)(2,1)}, u32[]{:S(2)}) copy-start(bf16[2,256,256]{2,1,0:T(8,128)(2,1)} %constant.51.clone.txh) | copy-start | bytes 786436
  41.0 24.8 %copy-start.13 = (bf16[256,256]{1,0:T(8,128)(2,1)S(1)}, bf16[256,256]{1,0:T(8,128)(2,1)}, u32[]{:S(2)}) copy-start(bf16[256,256]{1,0:T(8,128)(2,1)} %constant.56.clone.tyl) | copy-start | bytes 393220
  41.0 24.8 %copy-start.14 = (bf16[256,256]{1,0:T(8,128)(2,1)S(1)}, bf16[256,256]{1,0:T(8,128)(2,1)}, u32[]{:S(2)}) copy-start(bf16[256,256]{1,0:T(8,128)(2,1)} %constant.55.clone.tyh) | copy-start | bytes 393220
  43.3 22.5 %copy-start.1 = (bf16[2,256,256]{2,1,0:T(8,128)(2,1)S(1)}, bf16[2,256,256]{2,1,0:T(8,128)(2,1)}, u32[]{:S(2)}) copy-start(bf16[2,256,256]{2,1,0:T(8,128)(2,1)} %rho_ref.1) | copy-start | bytes 786436
  43.4 22.5 %copy-start.9 = (bf16[2,256,256]{2,1,0:T(8,128)(2,1)S(1)}, bf16[2,256,256]{2,1,0:T(8,128)(2,1)}, u32[]{:S(2)}) copy-start(bf16[2,256,256]{2,1,0:T(8,128)(2,1)} %constant.52.clone.txl) | copy-start | bytes 786436
  61.1 4.7 %collective-permute-start.2 = (s32[512,128]{1,0:T(8,128)S(1)}, s32[512,128]{1,0:T(8,128)S(1)}, u32[]{:S(2)}, u32[]{:S(2)}) collective-permute-start(s32[512,128]{1,0:T(8,128)S(1)} %bitcast.7), channel_id=1, source_target_pairs={{0,2},{2,0},{4,6},{6,4},{8,10},{10,8},{12,14},{14,12},{16,18},{18,... | collective-permute-start | bytes 786440 | tf_op jit(solution)/shard_map/ppermute | solution.py:235

commit v2 on v1

v2 whole, which is shorter than its diff:
```python
import functools

import jax
import jax.numpy as jnp
import ml_dtypes
import numpy as np
from jax import lax
from jax.experimental import pallas as pl
from jax.experimental.pallas import tpu as pltpu
from jax.sharding import PartitionSpec as P

N = 256
CHIPS = 64
HALF = N // 2
QUARTER = N // 4
FLOOR = 0.25
FULL = 16380.0
FORWARD_LOW = -20
INVERSE_LOW = -25
AMP_UNIT = 512.0


def angles(k, position):
    turns = np.outer(2 * np.asarray(k) - (N - 1), np.asarray(position)) % (2 * N)
    return turns * (np.pi / N)


def split(table):
    high = table.astype(ml_dtypes.bfloat16)
    low = (table - high.astype(np.float64)).astype(ml_dtypes.bfloat16)
    return high, low


def two(tables):
    highs, lows = zip(*(split(t) for t in tables))
    return np.stack(highs), np.stack(lows)


@functools.cache
def constants():
    out = {}
    scale = 1.0 / np.sqrt(N)
    every = np.arange(N)
    half = np.arange(HALF)
    forward, inverse = [], []
    for core in range(2):
        kx = np.tile(np.arange(QUARTER) + QUARTER * core, 2)
        a = angles(kx, every)
        forward.append(np.concatenate([np.cos(a), -np.sin(a)], 0).T * scale)
        inverse.append(np.concatenate([np.cos(a), -np.sin(a)], 0) * (2.0 * scale))
    out["tx"] = np.stack([np.concatenate(split(t), 1) for t in forward])
    out["txi"] = two(inverse)
    a = angles(half, every)
    out["ty"] = np.concatenate(split(np.concatenate([np.cos(a), np.sin(a)], 0) * scale), 0)
    out["tyi"] = split(np.concatenate([np.cos(a), np.sin(a)], 0).T * scale)
    forward, inverse = [], []
    for core in range(2):
        planes = [0, 1, 2, 3] if core == 0 else [2, 3, 0, 1]
        z = np.concatenate([4 * np.arange(CHIPS) + p for p in planes])
        a = angles(z, z)
        forward.append(np.concatenate([np.cos(a), np.sin(a)], 0) * scale)
        inverse.append(np.concatenate([np.cos(a.T), np.sin(a.T)], 0) * scale)
    out["tz"] = two(forward)
    out["tzi"] = two(inverse)
    picks = []
    for core in range(2):
        pick = np.zeros((2 * N, 2 * HALF))
        for h in range(2):
            for j in range(QUARTER):
                kx = QUARTER * core + j
                pick[N * h + kx, QUARTER * h + j] = 1
                pick[N * (1 - h) + N - 1 - kx, HALF + QUARTER * h + j] = 1
        picks.append(pick)
    out["pick"] = np.stack(picks).astype(ml_dtypes.bfloat16)
    out["rev_half"] = np.eye(HALF)[::-1].astype(ml_dtypes.bfloat16)
    out["rev_all"] = np.eye(N)[::-1].astype(ml_dtypes.bfloat16)
    return out


def mm(a, b):
    return jnp.dot(a, b, preferred_element_type=jnp.float32)


def cut(x):
    high = x.astype(jnp.bfloat16)
    return high, (x - high.astype(jnp.float32)).astype(jnp.bfloat16)


def left3(high, low, x):
    xh, xl = cut(x)
    return mm(high, xh) + (mm(high, xl) + mm(low, xh))


def right3(x, high, low):
    xh, xl = cut(x)
    return mm(xh, high) + (mm(xl, high) + mm(xh, low))


def pack(re0, im0, re1, im1, low):
    m = jnp.maximum(jnp.maximum(jnp.abs(re0), jnp.abs(im0)), jnp.maximum(jnp.abs(re1), jnp.abs(im1)))
    e = jnp.clip(jnp.floor(jnp.log2(jnp.maximum(m, 1e-30))) + (1.0 - low), 0.0, 31.0)
    s = jnp.exp2(-(e + low)) * FULL
    e = e.astype(jnp.int32)

    def code(x, factor):
        return jnp.floor(x * factor + 0.5).astype(jnp.int32)

    word0 = (code(re0, s) << 17) | ((code(im0, s) & 0x7FFF) << 2) | (e & 3)
    word1 = (code(re1, s) << 17) | ((code(im1, 0.5 * s) & 0x3FFF) << 3) | (e >> 2)
    return word0, word1


def unpack(word0, word1, low):
    e = (word0 & 3) | ((word1 & 7) << 2)
    s = jnp.exp2(e.astype(jnp.float32) + low) * (1.0 / FULL)
    re0 = (word0 >> 17).astype(jnp.float32) * s
    im0 = ((word0 << 15) >> 17).astype(jnp.float32) * s
    re1 = (word1 >> 17).astype(jnp.float32) * s
    im1 = ((word1 << 15) >> 18).astype(jnp.float32) * (2.0 * s)
    return re0, im0, re1, im1


def signs(y_axis_len):
    y = lax.broadcasted_iota(jnp.int32, (y_axis_len, 2 * HALF), 0)
    lane = lax.broadcasted_iota(jnp.int32, (y_axis_len, 2 * HALF), 1)
    odd = (y & 1) * ((lane >> 6) & 1)
    return (1 - 2 * odd).astype(jnp.float32)


def forward_planes(first, rho_ref, amp_ref, tx, ty, pick, rev, out, ready):
    sign = signs(N)
    ready("rho", "tx")
    lines = []
    for q in range(2):
        a = mm(rho_ref[q], tx[...])
        lines.append((a[:, :N] + a[:, N:]) * sign)
    ready("ty")
    parts = []
    for a in lines:
        u = left3(ty[:N], ty[N:], a)
        parts += [u[:HALF, :HALF] + u[HALF:, HALF:], u[:HALF, HALF:] - u[HALF:, :HALF]]
    words = pack(*parts, FORWARD_LOW)
    ready("amp", "pick", "rev")
    for q in range(2):
        amp = amp_ref[q]
        both = mm(jnp.concatenate([amp[:HALF], amp[HALF:]], 1), pick[...])
        direct = both[:, :HALF]
        mirror = mm(rev[...], both[:, HALF:].astype(jnp.bfloat16))
        coded = ((direct * AMP_UNIT).astype(jnp.int32) << 16) | (mirror * AMP_UNIT).astype(jnp.int32)
        for r in range(2):
            rows = slice(CHIPS * r, CHIPS * (r + 1))
            slot = 2 * (first + q) + r
            out[pl.ds(slot, CHIPS, stride=16), :] = words[q][rows]
            out[pl.ds(8 + slot, CHIPS, stride=16), :] = coded[rows]


def first_kernel(core_ref, rho_hbm, amp_hbm, tx_hbm, ty_hbm, pick_hbm, rev_hbm,
                 out, tx, ty, pick, rev, rho, amp, sems):
    core = core_ref[0]
    copies = {}
    for i, (name, source, target) in enumerate((
        ("rho", rho_hbm, rho),
        ("tx", tx_hbm.at[core], tx),
        ("ty", ty_hbm, ty),
        ("amp", amp_hbm, amp),
        ("pick", pick_hbm.at[core], pick),
        ("rev", rev_hbm, rev),
    )):
        copies[name] = pltpu.make_async_copy(source, target, sems.at[i])
        copies[name].start()

    def ready(*names):
        for name in names:
            copies[name].wait()

    forward_planes(0, rho, amp, tx, ty, pick, rev, out, ready)


def second_kernel(sent, rho, amp, tx, ty, pick, rev, out):
    forward_planes(2, rho, amp, tx, ty, pick, rev, out, lambda *names: None)


def middle_kernel(core_ref, msg, tzh, tzl, tzih, tzil, rev, out):
    core = core_ref[0]
    for r in range(2):

        def rows(slot):
            return msg[pl.ds(slot + r, CHIPS, stride=16), :]

        re, im = [], []
        for p in (0, 2):
            re0, im0, re1, im1 = unpack(rows(2 * p), rows(2 * p + 2), FORWARD_LOW)
            re += [re0, re1]
            im += [im0, im1]
        lines = jnp.concatenate([jnp.concatenate(re, 0), jnp.concatenate(im, 0)], 1)
        u = left3(tzh[core], tzl[core], lines)
        re = u[:N, :HALF] + u[N:, HALF:]
        im = u[:N, HALF:] - u[N:, :HALF]
        coded = jnp.concatenate([rows(8 + 2 * p) for p in range(4)], 0)
        direct = (coded >> 16).astype(jnp.float32)
        mirror = mm(rev[...], (coded & 0xFFFF).astype(jnp.float32).astype(jnp.bfloat16))
        target = (direct + mirror) * (0.5 / AMP_UNIT)
        ratio = target / jnp.maximum(jnp.sqrt(re * re + im * im), FLOOR)
        u = left3(tzih[core], tzil[core], jnp.concatenate([re * ratio, im * ratio], 1))
        re = u[:N, :HALF] - u[N:, HALF:]
        im = u[:N, HALF:] + u[N:, :HALF]
        for p in (0, 2):
            planes = [slice(CHIPS * i, CHIPS * (i + 1)) for i in (p, p + 1)]
            words = pack(re[planes[0]], im[planes[0]], re[planes[1]], im[planes[1]], INVERSE_LOW)
            for i in range(2):
                out[pl.ds(2 * (p + i) + r, CHIPS, stride=8), :] = words[i]


def half_planes(ref, first, tyh, tyl, txh, txl):
    sign = signs(N)
    words = [
        jnp.concatenate([ref[pl.ds(2 * p + r, CHIPS, stride=8), :] for r in range(2)], 0)
        for p in (first, first + 1)
    ]
    parts = unpack(*words, INVERSE_LOW)
    out = []
    for q in range(2):
        re, im = parts[2 * q : 2 * q + 2]
        g = jnp.concatenate([jnp.concatenate([re, im], 1), jnp.concatenate([-im, re], 1)], 0)
        out.append(right3(left3(tyh[...], tyl[...], g) * sign, txh, txl))
    return out


def own_kernel(core_ref, own, tyh, tyl, txh, txl, out):
    core = core_ref[0]
    for q, term in enumerate(half_planes(own, 0, tyh, tyl, txh[core], txl[core])):
        out[q] = term


def update_kernel(core_ref, partial, other, rho_ref, support, tyh, tyl, txh, txl, out):
    core = 1 - core_ref[0]
    for q, term in enumerate(half_planes(other, 2, tyh, tyl, txh[core], txl[core])):
        moduled = partial[q] + term
        rho = rho_ref[q].astype(jnp.float32)
        mask = support[q].astype(jnp.float32)
        out[q] = (rho + mask * (2.0 * moduled - rho) - moduled).astype(jnp.bfloat16)


SMEM = pl.BlockSpec(memory_space=pltpu.SMEM)
VMEM = pl.BlockSpec(memory_space=pltpu.VMEM)
HBM = pl.BlockSpec(memory_space=pltpu.HBM)


def call(kernel, out_shape, operands, in_specs, flops, **more):
    return pl.pallas_call(
        kernel,
        out_shape=out_shape,
        in_specs=in_specs,
        out_specs=jax.tree.map(lambda _: VMEM, out_shape),
        compiler_params=pltpu.CompilerParams(vmem_limit_bytes=40 * 2**20),
        cost_estimate=pl.CostEstimate(
            flops=int(flops), bytes_accessed=2 * 2**20, transcendentals=0
        ),
        **more,
    )(*operands)


def shards(density, amplitudes, support):
    c = {k: jax.tree.map(jnp.asarray, v) for k, v in constants().items()}
    swap = [(i, i ^ 1) for i in range(2 * CHIPS)]
    same_core = [list(range(core, 2 * CHIPS, 2)) for core in range(2)]
    core = (lax.axis_index("slab") % 2).astype(jnp.int32).reshape(1)

    def exchange(x):
        return lax.all_to_all(
            x, "slab", split_axis=0, concat_axis=0, tiled=True, axis_index_groups=same_core
        )

    def shape(dims, kind):
        return jax.ShapeDtypeStruct(dims, kind)

    density_other = lax.ppermute(density, "slab", swap)
    amplitudes_other = lax.ppermute(amplitudes, "slab", swap)
    message = shape((CHIPS * 16, HALF), jnp.int32)
    kept = [
        shape(c["tx"].shape[1:], jnp.bfloat16),
        shape(c["ty"].shape, jnp.bfloat16),
        shape(c["pick"].shape[1:], jnp.bfloat16),
        shape(c["rev_half"].shape, jnp.bfloat16),
    ]
    sent, *tables = call(
        first_kernel,
        [message, *kept],
        (core, density, amplitudes, c["tx"], c["ty"], c["pick"], c["rev_half"]),
        [SMEM] + [HBM] * 6,
        400e6,
        scratch_shapes=[
            pltpu.VMEM(density.shape, jnp.bfloat16),
            pltpu.VMEM(density.shape, jnp.bfloat16),
            pltpu.SemaphoreType.DMA((6,)),
        ],
    )
    sent = call(
        second_kernel,
        message,
        (sent, density_other, amplitudes_other, *tables),
        [VMEM] * 7,
        400e6,
        input_output_aliases={0: 0},
    )
    lines = exchange(sent.reshape(CHIPS, 16, HALF)).reshape(CHIPS * 16, HALF)
    sent = call(
        middle_kernel,
        shape((CHIPS * 8, HALF), jnp.int32),
        (core, lines, *c["tz"], *c["tzi"], c["rev_all"]),
        [SMEM] + [VMEM] * 6,
        800e6,
    )
    planes = exchange(sent.reshape(CHIPS, 8, HALF)).reshape(CHIPS * 8, HALF)
    planes_other = lax.ppermute(planes, "slab", swap)
    tables = (*c["tyi"], *c["txi"])
    partial = call(
        own_kernel,
        shape(density.shape, jnp.float32),
        (core, planes, *tables),
        [SMEM] + [VMEM] * 5,
        400e6,
    )
    return call(
        update_kernel,
        shape(density.shape, jnp.bfloat16),
        (core, partial, planes_other, density, support, *tables),
        [SMEM] + [VMEM] * 8,
        400e6,
    )


def solution(mesh):
    spec = P("slab", "member", None)
    return jax.shard_map(
        shards, mesh=mesh, in_specs=(spec, spec, spec), out_specs=spec, check_vma=False
    )
```

time: 68.2 us -> 64.6 us (0.947)
  waiting for transfers between devices: 2.91 us -> 0.3 us
  local copies, waits for them, and re-layouts: 6.72 us -> 5 us
  Pallas kernels: 6.44 us -> 7.22 us
    unnamed x38 -> x34, local copies, waits for them, and re-layouts: 6.72 us -> 5 us
    ppermute x1, waiting for transfers between devices: 1.37 us -> 0.01 us  [shards(): amplitudes_other = lax.ppermute(amplitudes, 'slab', swap)]
    ppermute x1, waiting for transfers between devices: 1.16 us -> 0.29 us  [shards(): planes_other = lax.ppermute(planes, 'slab', swap)]
    pallas_call x3 -> x5, Pallas kernels: 6.44 us -> 7.22 us  [call(): pl.pallas_call(kernel, out_shape=out_shape, in_specs=in_specs, out_specs=...]
  transfers between devices with their start and end apart: 3 -> 3, of which waited for: 3 -> 1; matrix products, arithmetic and copies ran while one was open for 0% -> 0% of each run, Pallas kernels for 0% -> 4%
where the time goes in v2:
time: 64.6 us; the launch traced here: 64.2 us
  blocking collectives  44.7 us (69%)
  Pallas kernels  7.22 us (11%)
  starting transfers between devices  6.82 us (11%)
  local copies, waits for them, and re-layouts  5 us (8%)
    all_to_all x2, blocking collectives, exchange(): lax.all_to_all(x, 'slab', split_axis=0, concat_axis=0, tiled=True, axis_i...  44.7 us
    pallas_call x5, Pallas kernels, call(): pl.pallas_call(kernel, out_shape=out_shape, in_specs=in_specs, out_specs=...  7.22 us
    unnamed x34, local copies, waits for them, and re-layouts  5 us
    ppermute x1, starting transfers between devices, shards(): planes_other = lax.ppermute(planes, 'slab', swap)  3.58 us
    ppermute x1, starting transfers between devices, shards(): amplitudes_other = lax.ppermute(amplitudes, 'slab', swap)  3.24 us
  transfers between devices with their start and end apart: 3, of which 1 were waited for; matrix products, arithmetic and copies ran while one was open for 0% of the time, Pallas kernels for 4%

profile of v2, /device:TPU:1, one launch (start us, length us, event | category | flops | bytes accessed | tf_op | source)
XLA Modules:
  0.0 64.2 jit_solution(933206154964364598)
XLA Ops:
  0.0 3.2 %collective-permute-start.1 = (bf16[2,256,256]{2,1,0:T(8,128)(2,1)}, bf16[2,256,256]{2,1,0:T(8,128)(2,1)S(1)}, u32[]{:S(2)}, u32[]{:S(2)}) collective-permute-start(bf16[2,256,256]{2,1,0:T(8,128)(2,1)} %amp_hbm.1), channel_id=1, source_target_pairs={{0,2},{2,0},{4,6},{6,4},{8,10},{10,8},{12,14},{14,12},{16,18},{18,... | collective-permute-start | bytes 786440 | tf_op jit(solution)/shard_map/ppermute | solution.py:278
  3.2 0.0 collective-permute-start
  3.2 0.0 copy-done.16
  3.3 0.9 %copy-done = bf16[2,256,256]{2,1,0:T(8,128)(2,1)S(1)} copy-done((bf16[2,256,256]{2,1,0:T(8,128)(2,1)S(1)}, bf16[2,256,256]{2,1,0:T(8,128)(2,1)}, u32[]{:S(2)}) %copy-start) | copy-done | bytes 262168
  4.2 1.0 %copy-done.11 = bf16[2,512,256]{2,1,0:T(8,128)(2,1)S(1)} copy-done((bf16[2,512,256]{2,1,0:T(8,128)(2,1)S(1)}, bf16[2,512,256]{2,1,0:T(8,128)(2,1)}, u32[]{:S(2)}) %copy-start.11) | copy-done | bytes 524312
  5.2 1.0 %copy-done.12 = bf16[2,256,512]{2,1,0:T(8,128)(2,1)S(1)} copy-done((bf16[2,256,512]{2,1,0:T(8,128)(2,1)S(1)}, bf16[2,256,512]{2,1,0:T(8,128)(2,1)}, u32[]{:S(2)}) %copy-start.12) | copy-done | bytes 524312
  6.3 0.9 %copy-done.13 = bf16[2,256,256]{2,1,0:T(8,128)(2,1)S(1)} copy-done((bf16[2,256,256]{2,1,0:T(8,128)(2,1)S(1)}, bf16[2,256,256]{2,1,0:T(8,128)(2,1)}, u32[]{:S(2)}) %copy-start.13) | copy-done | bytes 262168
  7.2 0.9 %copy-done.14 = bf16[512,256]{1,0:T(8,128)(2,1)S(1)} copy-done((bf16[512,256]{1,0:T(8,128)(2,1)S(1)}, bf16[512,256]{1,0:T(8,128)(2,1)}, u32[]{:S(2)}) %copy-start.14) | copy-done | bytes 262168
  8.2 1.7 %shard_map.154 = (s32[1024,128]{1,0:T(8,128)S(1)}, bf16[256,512]{1,0:T(8,128)(2,1)S(1)}, bf16[512,256]{1,0:T(8,128)(2,1)S(1)}, bf16[512,256]{1,0:T(8,128)(2,1)S(1)}, bf16[128,128]{1,0:T(8,128)(2,1)S(1)}) custom-call(s32[1]{0:T(128)} %bitcast.core_ref, bf16[2,256,256]{2,1,0:T(8,128)(2,1)S(1)} %copy-done, bf16[2,256,256]{2,1,0:T(8,128)(2,1)S(1)} %copy-done.13, ...), custom_call_target="tpu_custom_call" | custom-call | flops 400000000 | bytes 2097152 | tf_op jit(solution)/shard_map/pallas_call | solution.py:250
  9.9 0.0 collective-permute-done.1.amp
  9.9 0.0 collective-permute-done.rho
  9.9 0.0 copy-start.6
  9.9 0.0 copy-start.7
  9.9 0.0 copy-start.15
  9.9 1.1 %shard_map.155 = s32[1024,128]{1,0:T(8,128)S(1)} custom-call(s32[1024,128]{1,0:T(8,128)S(1)} %get-tuple-element.10.sent, bf16[2,256,256]{2,1,0:T(8,128)(2,1)S(1)} %collective-permute-done.rho, bf16[2,256,256]{2,1,0:T(8,128)(2,1)S(1)} %collective-permute-done.1.amp, bf16[256,512]{1,0:T(8,128)(2,1)S(1)} %get-tuple-element.11.tx, ...), custom_call_target="tpu_custom_call", output_to_operand_aliasing={{}: (0, {})} | custom-call | flops 400000000 | bytes 2097152 | tf_op jit(solution)/shard_map/pallas_call | solution.py:250
  11.1 0.0 copy-start.4
  11.1 0.0 copy-start.5
  11.1 26.9 %all_to_all.10 = s32[64,16,128]{2,1,0:T(8,128)S(1)} all-to-all(s32[64,16,128]{2,1,0:T(8,128)S(1)} %bitcast.6), channel_id=1, replica_groups={{0,4,8,12,16,20,24,28,32,36,40,44,48,52,56,60,64,68,72,76,80,84,88,92,9..., dimensions={0} | all-to-all | bytes 1048576 | tf_op jit(solution)/shard_map/all_to_all | solution.py:270
  38.0 0.0 copy-done.6
  38.0 0.0 copy-done.7
  38.0 0.0 copy-done.15
  38.0 0.0 copy-start.8
  38.0 0.0 copy-start.9
  38.0 2.0 %shard_map.156 = s32[512,128]{1,0:T(8,128)S(1)} custom-call(s32[1]{0:T(128)} %bitcast.core_ref, s32[1024,128]{1,0:T(8,128)S(1)} %bitcast.5, bf16[2,512,256]{2,1,0:T(8,128)(2,1)S(1)} %copy-done.7, bf16[2,512,256]{2,1,0:T(8,128)(2,1)S(1)} %copy-done.6, bf16[2,512,256]{2,1,0:T(8,128)(2,1)S(1)} %copy-done.5, bf16[2,512,256]{2,1,0:T(8,128)(2,1)S(1)} %copy-done.4, ...), custom_call_target="tpu_custom_call" | custom-call | flops 800000000 | bytes 2097152 | tf_op jit(solution)/shard_map/pallas_call | solution.py:250
  40.0 0.0 copy-start.2
  40.0 0.0 copy-start.3
  40.0 17.8 %all_to_all.11 = s32[64,8,128]{2,1,0:T(8,128)S(1)} all-to-all(s32[64,8,128]{2,1,0:T(8,128)S(1)} %bitcast.7), channel_id=1, replica_groups={{0,4,8,12,16,20,24,28,32,36,40,44,48,52,56,60,64,68,72,76,80,84,88,92,9..., dimensions={0} | all-to-all | bytes 524288 | tf_op jit(solution)/shard_map/all_to_all | solution.py:270
  57.8 3.6 %collective-permute-start.2 = (s32[512,128]{1,0:T(8,128)S(1)}, s32[512,128]{1,0:T(8,128)S(1)}, u32[]{:S(2)}, u32[]{:S(2)}) collective-permute-start(s32[512,128]{1,0:T(8,128)S(1)} %bitcast.8), channel_id=1, source_target_pairs={{0,2},{2,0},{4,6},{6,4},{8,10},{10,8},{12,14},{14,12},{16,18},{18,... | collective-permute-start | bytes 786440 | tf_op jit(solution)/shard_map/ppermute | solution.py:315
  61.4 0.0 copy-done.8
  61.4 0.8 %shard_map.157.partial = f32[2,256,256]{2,1,0:T(8,128)S(1)} custom-call(s32[1]{0:T(128)} %bitcast.core_ref, s32[512,128]{1,0:T(8,128)S(1)} %bitcast.9, bf16[256,256]{1,0:T(8,128)(2,1)S(1)} %copy-done.9, bf16[256,256]{1,0:T(8,128)(2,1)S(1)} %copy-done.8, bf16[2,256,256]{2,1,0:T(8,128)(2,1)S(1)} %copy-done.3, bf16[2,256,256]{2,1,0:T(8,128)(2,1)S(1)} %copy-done.2), custom_call_target="tpu_custom_call" | custom-call | flops 400000000 | bytes 2097152 | tf_op jit(solution)/shard_map/pallas_call | solution.py:250
  62.3 0.3 collective-permute-done.2.other
  62.6 1.6 %shard_map.158 = bf16[2,256,256]{2,1,0:T(8,128)(2,1)} custom-call(s32[1]{0:T(128)} %bitcast.core_ref, f32[2,256,256]{2,1,0:T(8,128)S(1)} %shard_map.157.partial, s32[512,128]{1,0:T(8,128)S(1)} %collective-permute-done.2.other, bf16[2,256,256]{2,1,0:T(8,128)(2,1)S(1)} %copy-done.1, s32[2,256,256]{2,1,0:T(8,128)S(1)} %copy-done.10, ...), custom_call_target="tpu_custom_call" | custom-call | flops 400000000 | bytes 2097152 | tf_op jit(solution)/shard_map/pallas_call | solution.py:250
  (15 shorter events, 0.0 us)
Async XLA Ops:
  0.0 3.2 %copy-start.16 = (bf16[128,128]{1,0:T(8,128)(2,1)S(1)}, bf16[128,128]{1,0:T(8,128)(2,1)}, u32[]{:S(2)}) copy-start(bf16[128,128]{1,0:T(8,128)(2,1)} %constant.56.clone.rev_hbm) | copy-start | bytes 98308
  0.0 9.9 %collective-permute-start.1 = (bf16[2,256,256]{2,1,0:T(8,128)(2,1)}, bf16[2,256,256]{2,1,0:T(8,128)(2,1)S(1)}, u32[]{:S(2)}, u32[]{:S(2)}) collective-permute-start(bf16[2,256,256]{2,1,0:T(8,128)(2,1)} %amp_hbm.1), channel_id=1, source_target_pairs={{0,2},{2,0},{4,6},{6,4},{8,10},{10,8},{12,14},{14,12},{16,18},{18,... | collective-permute-start | bytes 786440 | tf_op jit(solution)/shard_map/ppermute | solution.py:278
  3.2 6.6 %collective-permute-start = (bf16[2,256,256]{2,1,0:T(8,128)(2,1)}, bf16[2,256,256]{2,1,0:T(8,128)(2,1)S(1)}, u32[]{:S(2)}, u32[]{:S(2)}) collective-permute-start(bf16[2,256,256]{2,1,0:T(8,128)(2,1)} %rho_ref.1), channel_id=1, source_target_pairs={{0,2},{2,0},{4,6},{6,4},{8,10},{10,8},{12,14},{14,12},{16,18},{18,... | collective-permute-start | bytes 786440 | tf_op jit(solution)/shard_map/ppermute | solution.py:277
  3.2 1.0 %copy-start = (bf16[2,256,256]{2,1,0:T(8,128)(2,1)S(1)}, bf16[2,256,256]{2,1,0:T(8,128)(2,1)}, u32[]{:S(2)}) copy-start(bf16[2,256,256]{2,1,0:T(8,128)(2,1)} %rho_ref.1) | copy-start | bytes 786436
  4.2 1.0 %copy-start.11 = (bf16[2,512,256]{2,1,0:T(8,128)(2,1)S(1)}, bf16[2,512,256]{2,1,0:T(8,128)(2,1)}, u32[]{:S(2)}) copy-start(bf16[2,512,256]{2,1,0:T(8,128)(2,1)} %constant.55.clone.pick_hbm) | copy-start | bytes 1572868
  5.2 1.0 %copy-start.12 = (bf16[2,256,512]{2,1,0:T(8,128)(2,1)S(1)}, bf16[2,256,512]{2,1,0:T(8,128)(2,1)}, u32[]{:S(2)}) copy-start(bf16[2,256,512]{2,1,0:T(8,128)(2,1)} %constant.45.clone.tx_hbm) | copy-start | bytes 1572868
  6.3 0.9 %copy-start.13 = (bf16[2,256,256]{2,1,0:T(8,128)(2,1)S(1)}, bf16[2,256,256]{2,1,0:T(8,128)(2,1)}, u32[]{:S(2)}) copy-start(bf16[2,256,256]{2,1,0:T(8,128)(2,1)} %amp_hbm.1) | copy-start | bytes 786436
  7.2 0.9 %copy-start.14 = (bf16[512,256]{1,0:T(8,128)(2,1)S(1)}, bf16[512,256]{1,0:T(8,128)(2,1)}, u32[]{:S(2)}) copy-start(bf16[512,256]{1,0:T(8,128)(2,1)} %constant.48.clone.ty_hbm) | copy-start | bytes 786436
  9.9 28.1 %copy-start.6 = (bf16[2,512,256]{2,1,0:T(8,128)(2,1)S(1)}, bf16[2,512,256]{2,1,0:T(8,128)(2,1)}, u32[]{:S(2)}) copy-start(bf16[2,512,256]{2,1,0:T(8,128)(2,1)} %constant.52.clone.tzl) | copy-start | bytes 1572868
  9.9 28.1 %copy-start.7 = (bf16[2,512,256]{2,1,0:T(8,128)(2,1)S(1)}, bf16[2,512,256]{2,1,0:T(8,128)(2,1)}, u32[]{:S(2)}) copy-start(bf16[2,512,256]{2,1,0:T(8,128)(2,1)} %constant.51.clone.tzh) | copy-start | bytes 1572868
  9.9 28.1 %copy-start.15 = (bf16[256,256]{1,0:T(8,128)(2,1)S(1)}, bf16[256,256]{1,0:T(8,128)(2,1)}, u32[]{:S(2)}) copy-start(bf16[256,256]{1,0:T(8,128)(2,1)} %constant.57.clone.rev) | copy-start | bytes 393220
  11.1 26.9 %copy-start.4 = (bf16[2,512,256]{2,1,0:T(8,128)(2,1)S(1)}, bf16[2,512,256]{2,1,0:T(8,128)(2,1)}, u32[]{:S(2)}) copy-start(bf16[2,512,256]{2,1,0:T(8,128)(2,1)} %constant.54.clone.tzil) | copy-start | bytes 1572868
  11.1 26.9 %copy-start.5 = (bf16[2,512,256]{2,1,0:T(8,128)(2,1)S(1)}, bf16[2,512,256]{2,1,0:T(8,128)(2,1)}, u32[]{:S(2)}) copy-start(bf16[2,512,256]{2,1,0:T(8,128)(2,1)} %constant.53.clone.tzih) | copy-start | bytes 1572868
  38.0 23.4 %copy-start.8 = (bf16[256,256]{1,0:T(8,128)(2,1)S(1)}, bf16[256,256]{1,0:T(8,128)(2,1)}, u32[]{:S(2)}) copy-start(bf16[256,256]{1,0:T(8,128)(2,1)} %constant.50.clone.tyl) | copy-start | bytes 393220
  38.0 23.4 %copy-start.9 = (bf16[256,256]{1,0:T(8,128)(2,1)S(1)}, bf16[256,256]{1,0:T(8,128)(2,1)}, u32[]{:S(2)}) copy-start(bf16[256,256]{1,0:T(8,128)(2,1)} %constant.49.clone.tyh) | copy-start | bytes 393220
  40.0 21.4 %copy-start.2 = (bf16[2,256,256]{2,1,0:T(8,128)(2,1)S(1)}, bf16[2,256,256]{2,1,0:T(8,128)(2,1)}, u32[]{:S(2)}) copy-start(bf16[2,256,256]{2,1,0:T(8,128)(2,1)} %constant.47.clone.txl) | copy-start | bytes 786436
  40.0 21.4 %copy-start.3 = (bf16[2,256,256]{2,1,0:T(8,128)(2,1)S(1)}, bf16[2,256,256]{2,1,0:T(8,128)(2,1)}, u32[]{:S(2)}) copy-start(bf16[2,256,256]{2,1,0:T(8,128)(2,1)} %constant.46.clone.txh) | copy-start | bytes 786436
  57.8 4.8 %copy-start.1 = (bf16[2,256,256]{2,1,0:T(8,128)(2,1)S(1)}, bf16[2,256,256]{2,1,0:T(8,128)(2,1)}, u32[]{:S(2)}) copy-start(bf16[2,256,256]{2,1,0:T(8,128)(2,1)} %rho_ref.1) | copy-start | bytes 786436
  57.8 4.8 %copy-start.10 = (s32[2,256,256]{2,1,0:T(8,128)S(1)}, s32[2,256,256]{2,1,0:T(8,128)}, u32[]{:S(2)}) copy-start(s32[2,256,256]{2,1,0:T(8,128)} %support.1) | copy-start | bytes 1572868
  57.8 4.7 %collective-permute-start.2 = (s32[512,128]{1,0:T(8,128)S(1)}, s32[512,128]{1,0:T(8,128)S(1)}, u32[]{:S(2)}, u32[]{:S(2)}) collective-permute-start(s32[512,128]{1,0:T(8,128)S(1)} %bitcast.8), channel_id=1, source_target_pairs={{0,2},{2,0},{4,6},{6,4},{8,10},{10,8},{12,14},{14,12},{16,18},{18,... | collective-permute-start | bytes 786440 | tf_op jit(solution)/shard_map/ppermute | solution.py:315

commit v3 on v2

--- a/solution.py
+++ b/solution.py
@@ -18,6 +18,7 @@
 FORWARD_LOW = -20
 INVERSE_LOW = -25
 AMP_UNIT = 512.0
+ORDER = np.arange(CHIPS) ^ 44
 
 
 def angles(k, position):
@@ -48,15 +49,15 @@
         a = angles(kx, every)
         forward.append(np.concatenate([np.cos(a), -np.sin(a)], 0).T * scale)
         inverse.append(np.concatenate([np.cos(a), -np.sin(a)], 0) * (2.0 * scale))
-    out["tx"] = np.stack([np.concatenate(split(t), 1) for t in forward])
+    tx = forward
     out["txi"] = two(inverse)
     a = angles(half, every)
-    out["ty"] = np.concatenate(split(np.concatenate([np.cos(a), np.sin(a)], 0) * scale), 0)
+    ty = np.concatenate([np.cos(a), np.sin(a)], 0) * scale
     out["tyi"] = split(np.concatenate([np.cos(a), np.sin(a)], 0).T * scale)
     forward, inverse = [], []
     for core in range(2):
         planes = [0, 1, 2, 3] if core == 0 else [2, 3, 0, 1]
-        z = np.concatenate([4 * np.arange(CHIPS) + p for p in planes])
+        z = np.concatenate([4 * ORDER + p for p in planes])
         a = angles(z, z)
         forward.append(np.concatenate([np.cos(a), np.sin(a)], 0) * scale)
         inverse.append(np.concatenate([np.cos(a.T), np.sin(a.T)], 0) * scale)
@@ -71,8 +72,14 @@
                 pick[N * h + kx, QUARTER * h + j] = 1
                 pick[N * (1 - h) + N - 1 - kx, HALF + QUARTER * h + j] = 1
         picks.append(pick)
-    out["pick"] = np.stack(picks).astype(ml_dtypes.bfloat16)
-    out["rev_half"] = np.eye(HALF)[::-1].astype(ml_dtypes.bfloat16)
+    rev = np.zeros((HALF, N))
+    rev[:, :HALF] = np.eye(HALF)[::-1]
+    out["first"] = np.stack(
+        [
+            np.concatenate([*split(tx[core]), *split(ty), picks[core], rev], 0).astype(ml_dtypes.bfloat16)
+            for core in range(2)
+        ]
+    )
     out["rev_all"] = np.eye(N)[::-1].astype(ml_dtypes.bfloat16)
     return out
 
@@ -127,25 +134,19 @@
     return (1 - 2 * odd).astype(jnp.float32)
 
 
-def forward_planes(first, rho_ref, amp_ref, tx, ty, pick, rev, out, ready):
+def forward_planes(first, rho_ref, amp_ref, table, out):
     sign = signs(N)
-    ready("rho", "tx")
-    lines = []
+    parts = []
     for q in range(2):
-        a = mm(rho_ref[q], tx[...])
-        lines.append((a[:, :N] + a[:, N:]) * sign)
-    ready("ty")
-    parts = []
-    for a in lines:
-        u = left3(ty[:N], ty[N:], a)
+        a = mm(rho_ref[q], table[:N]) + mm(rho_ref[q], table[N : 2 * N])
+        u = left3(table[2 * N : 3 * N], table[3 * N : 4 * N], a * sign)
         parts += [u[:HALF, :HALF] + u[HALF:, HALF:], u[:HALF, HALF:] - u[HALF:, :HALF]]
     words = pack(*parts, FORWARD_LOW)
-    ready("amp", "pick", "rev")
     for q in range(2):
         amp = amp_ref[q]
-        both = mm(jnp.concatenate([amp[:HALF], amp[HALF:]], 1), pick[...])
+        both = mm(jnp.concatenate([amp[:HALF], amp[HALF:]], 1), table[4 * N : 6 * N])
         direct = both[:, :HALF]
-        mirror = mm(rev[...], both[:, HALF:].astype(jnp.bfloat16))
+        mirror = mm(table[6 * N :, :HALF], both[:, HALF:].astype(jnp.bfloat16))
         coded = ((direct * AMP_UNIT).astype(jnp.int32) << 16) | (mirror * AMP_UNIT).astype(jnp.int32)
         for r in range(2):
             rows = slice(CHIPS * r, CHIPS * (r + 1))
@@ -154,30 +155,9 @@
             out[pl.ds(8 + slot, CHIPS, stride=16), :] = coded[rows]
 
 
-def first_kernel(core_ref, rho_hbm, amp_hbm, tx_hbm, ty_hbm, pick_hbm, rev_hbm,
-                 out, tx, ty, pick, rev, rho, amp, sems):
-    core = core_ref[0]
-    copies = {}
-    for i, (name, source, target) in enumerate((
-        ("rho", rho_hbm, rho),
-        ("tx", tx_hbm.at[core], tx),
-        ("ty", ty_hbm, ty),
-        ("amp", amp_hbm, amp),
-        ("pick", pick_hbm.at[core], pick),
-        ("rev", rev_hbm, rev),
-    )):
-        copies[name] = pltpu.make_async_copy(source, target, sems.at[i])
-        copies[name].start()
-
-    def ready(*names):
-        for name in names:
-            copies[name].wait()
-
-    forward_planes(0, rho, amp, tx, ty, pick, rev, out, ready)
-
-
-def second_kernel(sent, rho, amp, tx, ty, pick, rev, out):
-    forward_planes(2, rho, amp, tx, ty, pick, rev, out, lambda *names: None)
+def forward_kernel(own, rho_other, amp_other, table, out):
+    forward_planes(0, own.at[:2], own.at[2:], table, out)
+    forward_planes(2, rho_other, amp_other, table, out)
 
 
 def middle_kernel(core_ref, msg, tzh, tzl, tzih, tzil, rev, out):
@@ -246,13 +226,13 @@
 HBM = pl.BlockSpec(memory_space=pltpu.HBM)
 
 
-def call(kernel, out_shape, operands, in_specs, flops, **more):
+def call(kernel, out_shape, operands, in_specs, flops, vmem=40 * 2**20, **more):
     return pl.pallas_call(
         kernel,
         out_shape=out_shape,
         in_specs=in_specs,
         out_specs=jax.tree.map(lambda _: VMEM, out_shape),
-        compiler_params=pltpu.CompilerParams(vmem_limit_bytes=40 * 2**20),
+        compiler_params=pltpu.CompilerParams(vmem_limit_bytes=vmem),
         cost_estimate=pl.CostEstimate(
             flops=int(flops), bytes_accessed=2 * 2**20, transcendentals=0
         ),
@@ -263,7 +243,7 @@
 def shards(density, amplitudes, support):
     c = {k: jax.tree.map(jnp.asarray, v) for k, v in constants().items()}
     swap = [(i, i ^ 1) for i in range(2 * CHIPS)]
-    same_core = [list(range(core, 2 * CHIPS, 2)) for core in range(2)]
+    same_core = [[int(2 * chip + core) for chip in ORDER] for core in range(2)]
     core = (lax.axis_index("slab") % 2).astype(jnp.int32).reshape(1)
 
     def exchange(x):
@@ -276,32 +256,14 @@
 
     density_other = lax.ppermute(density, "slab", swap)
     amplitudes_other = lax.ppermute(amplitudes, "slab", swap)
-    message = shape((CHIPS * 16, HALF), jnp.int32)
-    kept = [
-        shape(c["tx"].shape[1:], jnp.bfloat16),
-        shape(c["ty"].shape, jnp.bfloat16),
-        shape(c["pick"].shape[1:], jnp.bfloat16),
-        shape(c["rev_half"].shape, jnp.bfloat16),
-    ]
-    sent, *tables = call(
-        first_kernel,
-        [message, *kept],
-        (core, density, amplitudes, c["tx"], c["ty"], c["pick"], c["rev_half"]),
-        [SMEM] + [HBM] * 6,
-        400e6,
-        scratch_shapes=[
-            pltpu.VMEM(density.shape, jnp.bfloat16),
-            pltpu.VMEM(density.shape, jnp.bfloat16),
-            pltpu.SemaphoreType.DMA((6,)),
-        ],
-    )
+    table = lax.dynamic_index_in_dim(c["first"], core[0], 0, keepdims=False)
+    own = jnp.concatenate([density, amplitudes], 0)
     sent = call(
-        second_kernel,
-        message,
-        (sent, density_other, amplitudes_other, *tables),
-        [VMEM] * 7,
-        400e6,
-        input_output_aliases={0: 0},
+        forward_kernel,
+        shape((CHIPS * 16, HALF), jnp.int32),
+        (own, density_other, amplitudes_other, table),
+        [VMEM] * 4,
+        800e6,
     )
     lines = exchange(sent.reshape(CHIPS, 16, HALF)).reshape(CHIPS * 16, HALF)
     sent = call(

time: 64.6 us -> 55.3 us (0.86)
  local copies, waits for them, and re-layouts: 5 us -> 1.29 us
  blocking collectives: 44.7 us -> 41 us
  starting transfers between devices: 6.82 us -> 5.05 us
  Pallas kernels: 7.22 us -> 6.1 us
  other arithmetic: 0 us -> 1.08 us
    unnamed x34 -> x22, local copies, waits for them, and re-layouts: 5 us -> 0.07 us
    all_to_all x2, blocking collectives: 44.7 us -> 41 us  [exchange(): lax.all_to_all(x, 'slab', split_axis=0, concat_axis=0, tiled=True, axis_i...]
    ppermute x1, starting transfers between devices: 3.58 us -> 1.8 us  [shards(): planes_other = lax.ppermute(planes, 'slab', swap)]
    squeeze x0 -> x1, local copies, waits for them, and re-layouts: none -> 1.22 us  [shards(): table = lax.dynamic_index_in_dim(c['first'], core[0], 0, keepdims=False)]
    pallas_call x5 -> x4, Pallas kernels: 7.22 us -> 6.1 us  [call(): pl.pallas_call(kernel, out_shape=out_shape, in_specs=in_specs, out_specs=...]
    concatenate x0 -> x1, other arithmetic: none -> 1.08 us  [shards(): own = jnp.concatenate([density, amplitudes], 0)]
  transfers between devices with their start and end apart: 3 -> 3, of which waited for: 1 -> 1; matrix products, arithmetic and copies ran while one was open for 0% -> 4% of each run, Pallas kernels for 4% -> 2%
where the time goes in v3:
time: 55.3 us; the launch traced here: 55 us
  blocking collectives  41 us (74%)
  Pallas kernels  6.1 us (11%)
  starting transfers between devices  5.05 us (9%)
  local copies, waits for them, and re-layouts  1.29 us (2%)
  other arithmetic  1.08 us (2%)
    all_to_all x2, blocking collectives, exchange(): lax.all_to_all(x, 'slab', split_axis=0, concat_axis=0, tiled=True, axis_i...  41 us
    pallas_call x4, Pallas kernels, call(): pl.pallas_call(kernel, out_shape=out_shape, in_specs=in_specs, out_specs=...  6.1 us
    ppermute x1, starting transfers between devices, shards(): amplitudes_other = lax.ppermute(amplitudes, 'slab', swap)  3.24 us
    ppermute x1, starting transfers between devices, shards(): planes_other = lax.ppermute(planes, 'slab', swap)  1.8 us
    squeeze x1, local copies, waits for them, and re-layouts, shards(): table = lax.dynamic_index_in_dim(c['first'], core[0], 0, keepdims=False)  1.22 us
  transfers between devices with their start and end apart: 3, of which 1 were waited for; matrix products, arithmetic and copies ran while one was open for 4% of the time, Pallas kernels for 2%

profile of v3, /device:TPU:1, one launch (start us, length us, event | category | flops | bytes accessed | tf_op | source)
XLA Modules:
  0.0 55.0 jit_solution(2152512345047605142)
XLA Ops:
  0.0 3.2 %collective-permute-start.1 = (bf16[2,256,256]{2,1,0:T(8,128)(2,1)}, bf16[2,256,256]{2,1,0:T(8,128)(2,1)S(1)}, u32[]{:S(2)}, u32[]{:S(2)}) collective-permute-start(bf16[2,256,256]{2,1,0:T(8,128)(2,1)} %param.14), channel_id=1, source_target_pairs={{0,2},{2,0},{4,6},{6,4},{8,10},{10,8},{12,14},{14,12},{16,18},{18,... | collective-permute-start | bytes 786440 | tf_op jit(solution)/shard_map/ppermute | solution.py:258
  3.2 0.0 collective-permute-start
  3.2 1.1 %pad_maximum_fusion.own = bf16[4,256,256]{2,1,0:T(8,128)(2,1)S(1)} fusion(bf16[2,256,256]{2,1,0:T(8,128)(2,1)} %param.14, bf16[2,256,256]{2,1,0:T(8,128)(2,1)} %rho_ref.1), kind=kLoop, calls=%fused_computation.1 | loop fusion | flops 262144 | bytes 1048576 | tf_op jit(solution)/shard_map/concatenate | solution.py:260
  4.3 1.2 %dynamic-slice_bitcast_fusion.table = bf16[1664,256]{1,0:T(8,128)(2,1)S(1)} fusion(bf16[2,1664,256]{2,1,0:T(8,128)(2,1)} %constant.51.clone, s32[]{:T(128)S(6)} %select_n.12), kind=kLoop, calls=%fused_computation | loop fusion | bytes 1703940 | tf_op jit(solution)/shard_map/jit(dynamic_index_in_dim)/squeeze | solution.py:259
  5.6 0.0 copy-start.3
  5.6 0.0 copy-start.4
  5.6 0.0 copy-start.5
  5.6 0.0 copy-start.6
  5.6 0.0 copy-start.10
  5.6 0.0 collective-permute-done.1.amp_other
  5.6 0.0 collective-permute-done.rho_other
  5.6 1.7 %shard_map.127 = s32[1024,128]{1,0:T(8,128)S(1)} custom-call(bf16[4,256,256]{2,1,0:T(8,128)(2,1)S(1)} %pad_maximum_fusion.own, bf16[2,256,256]{2,1,0:T(8,128)(2,1)S(1)} %collective-permute-done.rho_other, bf16[2,256,256]{2,1,0:T(8,128)(2,1)S(1)} %collective-permute-done.1.amp_other, bf16[1664,256]{1,0:T(8,128)(2,1)S(1)} %dynamic-slice_bitcast_fusion.table), custom_call_target="tpu_custom_call" | custom-call | flops 800000000 | bytes 2097152 | tf_op jit(solution)/shard_map/pallas_call | solution.py:230
  7.3 24.1 %all_to_all.10 = s32[64,16,128]{2,1,0:T(8,128)S(1)} all-to-all(s32[64,16,128]{2,1,0:T(8,128)S(1)} %bitcast.11), channel_id=1, replica_groups={{176,180,184,188,160,164,168,172,144,148,152,156,128,132,136,140,240,24..., dimensions={0} | all-to-all | bytes 1048576 | tf_op jit(solution)/shard_map/all_to_all | solution.py:250
  31.5 0.0 copy-done.3
  31.5 0.0 copy-done.4
  31.5 0.0 copy-done.5
  31.5 0.0 copy-done.6
  31.5 0.0 copy-done.10
  31.5 0.0 copy-start.1
  31.5 0.0 copy-start.2
  31.5 0.0 copy-start.7
  31.5 0.0 copy-start.8
  31.5 1.9 %shard_map.128 = s32[512,128]{1,0:T(8,128)S(1)} custom-call(s32[1]{0:T(128)} %bitcast.core_ref, s32[1024,128]{1,0:T(8,128)S(1)} %bitcast.7, bf16[2,512,256]{2,1,0:T(8,128)(2,1)S(1)} %copy-done.6, bf16[2,512,256]{2,1,0:T(8,128)(2,1)S(1)} %copy-done.5, bf16[2,512,256]{2,1,0:T(8,128)(2,1)S(1)} %copy-done.4, bf16[2,512,256]{2,1,0:T(8,128)(2,1)S(1)} %copy-done.3, ...), custom_call_target="tpu_custom_call" | custom-call | flops 800000000 | bytes 2097152 | tf_op jit(solution)/shard_map/pallas_call | solution.py:230
  33.5 0.0 copy-start
  33.5 0.0 copy-start.9
  33.5 16.9 %all_to_all.11 = s32[64,8,128]{2,1,0:T(8,128)S(1)} all-to-all(s32[64,8,128]{2,1,0:T(8,128)S(1)} %bitcast.8), channel_id=1, replica_groups={{176,180,184,188,160,164,168,172,144,148,152,156,128,132,136,140,240,24..., dimensions={0} | all-to-all | bytes 524288 | tf_op jit(solution)/shard_map/all_to_all | solution.py:250
  50.4 1.8 %collective-permute-start.2 = (s32[512,128]{1,0:T(8,128)S(1)}, s32[512,128]{1,0:T(8,128)S(1)}, u32[]{:S(2)}, u32[]{:S(2)}) collective-permute-start(s32[512,128]{1,0:T(8,128)S(1)} %bitcast.9), channel_id=1, source_target_pairs={{0,2},{2,0},{4,6},{6,4},{8,10},{10,8},{12,14},{14,12},{16,18},{18,... | collective-permute-start | bytes 786440 | tf_op jit(solution)/shard_map/ppermute | solution.py:277
  52.2 0.0 copy-done.2
  52.3 0.8 %shard_map.129.partial = f32[2,256,256]{2,1,0:T(8,128)S(1)} custom-call(s32[1]{0:T(128)} %bitcast.core_ref, s32[512,128]{1,0:T(8,128)S(1)} %bitcast.10, bf16[256,256]{1,0:T(8,128)(2,1)S(1)} %copy-done.8, bf16[256,256]{1,0:T(8,128)(2,1)S(1)} %copy-done.7, bf16[2,256,256]{2,1,0:T(8,128)(2,1)S(1)} %copy-done.2, bf16[2,256,256]{2,1,0:T(8,128)(2,1)S(1)} %copy-done.1), custom_call_target="tpu_custom_call" | custom-call | flops 400000000 | bytes 2097152 | tf_op jit(solution)/shard_map/pallas_call | solution.py:230
  53.1 0.3 collective-permute-done.2.other
  53.4 0.0 copy-done
  53.4 1.6 %shard_map.130 = bf16[2,256,256]{2,1,0:T(8,128)(2,1)} custom-call(s32[1]{0:T(128)} %bitcast.core_ref, f32[2,256,256]{2,1,0:T(8,128)S(1)} %shard_map.129.partial, s32[512,128]{1,0:T(8,128)S(1)} %collective-permute-done.2.other, bf16[2,256,256]{2,1,0:T(8,128)(2,1)S(1)} %copy-done, s32[2,256,256]{2,1,0:T(8,128)S(1)} %copy-done.9, ...), custom_call_target="tpu_custom_call" | custom-call | flops 400000000 | bytes 2097152 | tf_op jit(solution)/shard_map/pallas_call | solution.py:230
  (4 shorter events, 0.0 us)
Async XLA Ops:
  0.0 5.6 %collective-permute-start.1 = (bf16[2,256,256]{2,1,0:T(8,128)(2,1)}, bf16[2,256,256]{2,1,0:T(8,128)(2,1)S(1)}, u32[]{:S(2)}, u32[]{:S(2)}) collective-permute-start(bf16[2,256,256]{2,1,0:T(8,128)(2,1)} %param.14), channel_id=1, source_target_pairs={{0,2},{2,0},{4,6},{6,4},{8,10},{10,8},{12,14},{14,12},{16,18},{18,... | collective-permute-start | bytes 786440 | tf_op jit(solution)/shard_map/ppermute | solution.py:258
  3.2 2.4 %collective-permute-start = (bf16[2,256,256]{2,1,0:T(8,128)(2,1)}, bf16[2,256,256]{2,1,0:T(8,128)(2,1)S(1)}, u32[]{:S(2)}, u32[]{:S(2)}) collective-permute-start(bf16[2,256,256]{2,1,0:T(8,128)(2,1)} %rho_ref.1), channel_id=1, source_target_pairs={{0,2},{2,0},{4,6},{6,4},{8,10},{10,8},{12,14},{14,12},{16,18},{18,... | collective-permute-start | bytes 786440 | tf_op jit(solution)/shard_map/ppermute | solution.py:257
  5.6 25.9 %copy-start.3 = (bf16[2,512,256]{2,1,0:T(8,128)(2,1)S(1)}, bf16[2,512,256]{2,1,0:T(8,128)(2,1)}, u32[]{:S(2)}) copy-start(bf16[2,512,256]{2,1,0:T(8,128)(2,1)} %constant.50.clone.tzil) | copy-start | bytes 1572868
  5.6 25.9 %copy-start.4 = (bf16[2,512,256]{2,1,0:T(8,128)(2,1)S(1)}, bf16[2,512,256]{2,1,0:T(8,128)(2,1)}, u32[]{:S(2)}) copy-start(bf16[2,512,256]{2,1,0:T(8,128)(2,1)} %constant.49.clone.tzih) | copy-start | bytes 1572868
  5.6 25.9 %copy-start.5 = (bf16[2,512,256]{2,1,0:T(8,128)(2,1)S(1)}, bf16[2,512,256]{2,1,0:T(8,128)(2,1)}, u32[]{:S(2)}) copy-start(bf16[2,512,256]{2,1,0:T(8,128)(2,1)} %constant.48.clone.tzl) | copy-start | bytes 1572868
  5.6 25.9 %copy-start.6 = (bf16[2,512,256]{2,1,0:T(8,128)(2,1)S(1)}, bf16[2,512,256]{2,1,0:T(8,128)(2,1)}, u32[]{:S(2)}) copy-start(bf16[2,512,256]{2,1,0:T(8,128)(2,1)} %constant.47.clone.tzh) | copy-start | bytes 1572868
  5.6 25.9 %copy-start.10 = (bf16[256,256]{1,0:T(8,128)(2,1)S(1)}, bf16[256,256]{1,0:T(8,128)(2,1)}, u32[]{:S(2)}) copy-start(bf16[256,256]{1,0:T(8,128)(2,1)} %constant.52.clone.rev) | copy-start | bytes 393220
  31.5 20.8 %copy-start.1 = (bf16[2,256,256]{2,1,0:T(8,128)(2,1)S(1)}, bf16[2,256,256]{2,1,0:T(8,128)(2,1)}, u32[]{:S(2)}) copy-start(bf16[2,256,256]{2,1,0:T(8,128)(2,1)} %constant.44.clone.txl) | copy-start | bytes 786436
  31.5 20.7 %copy-start.2 = (bf16[2,256,256]{2,1,0:T(8,128)(2,1)S(1)}, bf16[2,256,256]{2,1,0:T(8,128)(2,1)}, u32[]{:S(2)}) copy-start(bf16[2,256,256]{2,1,0:T(8,128)(2,1)} %constant.43.clone.txh) | copy-start | bytes 786436
  31.5 20.7 %copy-start.7 = (bf16[256,256]{1,0:T(8,128)(2,1)S(1)}, bf16[256,256]{1,0:T(8,128)(2,1)}, u32[]{:S(2)}) copy-start(bf16[256,256]{1,0:T(8,128)(2,1)} %constant.46.clone.tyl) | copy-start | bytes 393220
  31.5 20.7 %copy-start.8 = (bf16[256,256]{1,0:T(8,128)(2,1)S(1)}, bf16[256,256]{1,0:T(8,128)(2,1)}, u32[]{:S(2)}) copy-start(bf16[256,256]{1,0:T(8,128)(2,1)} %constant.45.clone.tyh) | copy-start | bytes 393220
  33.5 19.9 %copy-start = (bf16[2,256,256]{2,1,0:T(8,128)(2,1)S(1)}, bf16[2,256,256]{2,1,0:T(8,128)(2,1)}, u32[]{:S(2)}) copy-start(bf16[2,256,256]{2,1,0:T(8,128)(2,1)} %rho_ref.1) | copy-start | bytes 786436
  33.5 19.9 %copy-start.9 = (s32[2,256,256]{2,1,0:T(8,128)S(1)}, s32[2,256,256]{2,1,0:T(8,128)}, u32[]{:S(2)}) copy-start(s32[2,256,256]{2,1,0:T(8,128)} %support.1) | copy-start | bytes 1572868
  50.4 3.0 %collective-permute-start.2 = (s32[512,128]{1,0:T(8,128)S(1)}, s32[512,128]{1,0:T(8,128)S(1)}, u32[]{:S(2)}, u32[]{:S(2)}) collective-permute-start(s32[512,128]{1,0:T(8,128)S(1)} %bitcast.9), channel_id=1, source_target_pairs={{0,2},{2,0},{4,6},{6,4},{8,10},{10,8},{12,14},{14,12},{16,18},{18,... | collective-permute-start | bytes 786440 | tf_op jit(solution)/shard_map/ppermute | solution.py:277

commit v4 on v3

v4 whole, which is shorter than its diff:
```python
import functools

import jax
import jax.numpy as jnp
import ml_dtypes
import numpy as np
from jax import lax
from jax.experimental import pallas as pl
from jax.experimental.pallas import tpu as pltpu
from jax.sharding import PartitionSpec as P

N = 256
CHIPS = 64
HALF = N // 2
QUARTER = N // 4
FLOOR = 0.25
FULL = 16380.0
FORWARD_LOW = -20
INVERSE_LOW = -25
AMP_UNIT = 512.0
ORDER = np.arange(CHIPS) ^ 44


def angles(k, position):
    turns = np.outer(2 * np.asarray(k) - (N - 1), np.asarray(position)) % (2 * N)
    return turns * (np.pi / N)


def split(table):
    high = table.astype(ml_dtypes.bfloat16)
    low = (table - high.astype(np.float64)).astype(ml_dtypes.bfloat16)
    return high, low


def two(tables):
    highs, lows = zip(*(split(t) for t in tables))
    return np.stack(highs), np.stack(lows)


def turned(c, s):
    return np.concatenate([np.concatenate([c, -s], 1), np.concatenate([s, c], 1)], 0)


@functools.cache
def constants():
    out = {}
    scale = 1.0 / np.sqrt(N)
    every = np.arange(N)
    half = np.arange(HALF)
    a = angles(half, 2 * half)
    ty = turned(np.cos(a), -np.sin(a)) * scale
    out["tyi"] = split(turned(np.cos(a.T), np.sin(a.T)) * scale)
    lanes = np.repeat([0, 1], QUARTER)
    a = angles(half, lanes)
    out["tw"] = np.stack([np.cos(a), np.sin(a)]).astype(np.float32)
    first, inverse = [], []
    rev = np.zeros((HALF, N))
    rev[:, :HALF] = np.eye(HALF)[::-1]
    for core in range(2):
        kx = np.arange(QUARTER) + QUARTER * core
        a = angles(kx, every)
        tx = np.concatenate([np.cos(a), -np.sin(a)], 0)
        inverse.append(tx * (2.0 * scale))
        pick = np.zeros((N, N))
        for h in range(2):
            pick[kx, QUARTER * h + np.arange(QUARTER)] = 1
            pick[N - 1 - kx, HALF + QUARTER * h + np.arange(QUARTER)] = 1
        parts = [np.concatenate(split(tx.T * scale), 1), *split(ty), pick, rev]
        first.append(np.concatenate([p.astype(ml_dtypes.bfloat16) for p in parts], 0))
    out["first"] = np.stack(first)
    out["txi"] = two(inverse)
    forward, inverse, twist = [], [], []
    for core in range(2):
        planes = [0, 1, 2, 3] if core == 0 else [2, 3, 0, 1]
        kz = np.concatenate([4 * ORDER[CHIPS // 2 :] + p for p in planes])
        z = np.concatenate([4 * ORDER + p for p in planes[::2]])
        a = angles(kz, z)
        forward.append(turned(np.cos(a), -np.sin(a)) * scale)
        inverse.append(turned(np.cos(a.T), np.sin(a.T)) * scale)
        a = angles(kz, np.ones(HALF, int))
        twist.append(np.stack([np.cos(a), np.sin(a)]))
        kz = np.concatenate([kz, kz + HALF])
        out["rev_all"] = (kz[:, None] + kz[None, :] == N - 1).astype(ml_dtypes.bfloat16)
    out["tz"] = two(forward)
    out["tzi"] = two(inverse)
    out["tzw"] = np.stack(twist).astype(np.float32)
    return out


def mm(a, b):
    return jnp.dot(a, b, preferred_element_type=jnp.float32)


def cut(x):
    high = x.astype(jnp.bfloat16)
    return high, (x - high.astype(jnp.float32)).astype(jnp.bfloat16)


def left3(high, low, x):
    xh, xl = cut(x)
    return mm(high, xh) + (mm(high, xl) + mm(low, xh))


def pack(re0, im0, re1, im1, low):
    m = jnp.maximum(jnp.maximum(jnp.abs(re0), jnp.abs(im0)), jnp.maximum(jnp.abs(re1), jnp.abs(im1)))
    e = jnp.clip(jnp.floor(jnp.log2(jnp.maximum(m, 1e-30))) + (1.0 - low), 0.0, 31.0)
    s = jnp.exp2(-(e + low)) * FULL
    e = e.astype(jnp.int32)

    def code(x, factor):
        return jnp.floor(x * factor + 0.5).astype(jnp.int32)

    word0 = (code(re0, s) << 17) | ((code(im0, s) & 0x7FFF) << 2) | (e & 3)
    word1 = (code(re1, s) << 17) | ((code(im1, 0.5 * s) & 0x3FFF) << 3) | (e >> 2)
    return word0, word1


def unpack(word0, word1, low):
    e = (word0 & 3) | ((word1 & 7) << 2)
    s = jnp.exp2(e.astype(jnp.float32) + low) * (1.0 / FULL)
    re0 = (word0 >> 17).astype(jnp.float32) * s
    im0 = ((word0 << 15) >> 17).astype(jnp.float32) * s
    re1 = (word1 >> 17).astype(jnp.float32) * s
    im1 = ((word1 << 15) >> 18).astype(jnp.float32) * (2.0 * s)
    return re0, im0, re1, im1


def roll(x):
    return pltpu.roll(x, QUARTER, 1)


def lower(rows):
    return lax.broadcasted_iota(jnp.int32, (rows, HALF), 1) < QUARTER


def butterfly(x, low):
    return roll(x) + jnp.where(low, x, -x)


def square(x):
    return jnp.concatenate(
        [jnp.concatenate([x[0], x[2]], 1), jnp.concatenate([x[1], x[3]], 1)], 0
    )


def forward_planes(first, rho_ref, amp_ref, table, tw, out, scratch):
    low = lower(HALF)
    c, s = tw[0], tw[1]
    stack = []
    for q in range(2):
        a = mm(rho_ref[q], table[:N])
        scratch[q] = a[:, :HALF] + a[:, HALF:]
        even = scratch[q, pl.ds(0, HALF, stride=2), :]
        odd = scratch[q, pl.ds(1, HALF, stride=2), :]
        stack += [jnp.where(low, even, roll(odd)), jnp.where(low, roll(even), odd)]
    u = left3(table[N : 2 * N], table[2 * N : 3 * N], square(stack))
    parts = []
    for q in range(2):
        re, im = u[:HALF, HALF * q : HALF * (q + 1)], u[HALF:, HALF * q : HALF * (q + 1)]
        parts += [butterfly(re * c + im * s, low), butterfly(im * c - re * s, low)]
    words = pack(*parts, FORWARD_LOW)
    mirrors = []
    directs = []
    for q in range(2):
        both = mm(amp_ref[q], table[3 * N : 4 * N])
        directs.append(jnp.where(low, both[:HALF, :HALF], both[HALF:, :HALF]))
        mirrors.append(jnp.where(low, both[HALF:, HALF:], both[:HALF, HALF:]))
    mirrors = mm(table[4 * N :, :HALF], jnp.concatenate(mirrors, 1).astype(jnp.bfloat16))
    for q in range(2):
        mirror = mirrors[:, HALF * q : HALF * (q + 1)]
        coded = ((directs[q] * AMP_UNIT).astype(jnp.int32) << 16) | (mirror * AMP_UNIT).astype(jnp.int32)
        for r in range(2):
            rows = slice(CHIPS * r, CHIPS * (r + 1))
            slot = 2 * (first + q) + r
            out[pl.ds(slot, CHIPS, stride=16), :] = words[q][rows]
            out[pl.ds(8 + slot, CHIPS, stride=16), :] = coded[rows]


def forward_kernel(rho, amp, rho_other, amp_other, table, tw, out, scratch):
    forward_planes(0, rho, amp, table, tw, out, scratch.at[:2])
    forward_planes(2, rho_other, amp_other, table, tw, out, scratch.at[2:])


def middle_kernel(core_ref, msg, tzh, tzl, tzih, tzil, tzw, rev, out):
    core = core_ref[0]
    c, s = tzw[core, 0], tzw[core, 1]
    half = CHIPS // 2
    spectra, mirrors, directs = [], [], []
    for r in range(2):
        parts = []
        for p in (0, 2):
            pair = [msg[pl.ds(2 * (p + i) + r, CHIPS, stride=16), :] for i in range(2)]
            parts.append(unpack(*pair, FORWARD_LOW))
        lines = square([jnp.concatenate(x, 0) for x in zip(*parts)])
        u = left3(tzh[core], tzl[core], lines)
        even_re, odd_re = u[:HALF, :HALF], u[:HALF, HALF:]
        even_im, odd_im = u[HALF:, :HALF], u[HALF:, HALF:]
        odd_re, odd_im = odd_re * c + odd_im * s, odd_im * c - odd_re * s
        spectra.append(
            (
                jnp.concatenate([even_re + odd_re, even_re - odd_re], 0),
                jnp.concatenate([even_im + odd_im, even_im - odd_im], 0),
            )
        )
        coded = jnp.concatenate(
            [
                msg[pl.ds(16 * chip + 8 + 2 * p + r, half, stride=16), :]
                for chip in (half, 0)
                for p in range(4)
            ],
            0,
        )
        directs.append((coded >> 16).astype(jnp.float32))
        mirrors.append((coded & 0xFFFF).astype(jnp.float32).astype(jnp.bfloat16))
    mirrors = mm(rev[...], jnp.concatenate(mirrors, 1))
    for r in range(2):
        re, im = spectra[r]
        target = (directs[r] + mirrors[:, HALF * r : HALF * (r + 1)]) * (0.5 / AMP_UNIT)
        ratio = target / jnp.maximum(jnp.sqrt(re * re + im * im), FLOOR)
        re, im = re * ratio, im * ratio
        odd_re, odd_im = re[:HALF] - re[HALF:], im[:HALF] - im[HALF:]
        lines = square(
            [
                re[:HALF] + re[HALF:],
                im[:HALF] + im[HALF:],
                odd_re * c - odd_im * s,
                odd_im * c + odd_re * s,
            ]
        )
        u = left3(tzih[core], tzil[core], lines)
        for i in range(2):
            re, im = u[CHIPS * i : CHIPS * (i + 1)], u[HALF + CHIPS * i : HALF + CHIPS * (i + 1)]
            words = pack(re[:, :HALF], im[:, :HALF], re[:, HALF:], im[:, HALF:], INVERSE_LOW)
            for o in range(2):
                out[pl.ds(2 * (2 * i + o) + r, CHIPS, stride=8), :] = words[o]


def half_planes(ref, first, tyh, tyl, tw, txh, txl):
    low = lower(HALF)
    c, s = tw[0], tw[1]
    words = [
        jnp.concatenate([ref[pl.ds(2 * p + r, CHIPS, stride=8), :] for r in range(2)], 0)
        for p in (first, first + 1)
    ]
    parts = unpack(*words, INVERSE_LOW)
    stack = []
    for q in range(2):
        re, im = (butterfly(x, low) for x in parts[2 * q : 2 * q + 2])
        stack += [re * c - im * s, im * c + re * s]
    u = left3(tyh[...], tyl[...], square(stack))
    out = []
    for q in range(2):
        re, im = u[:HALF, HALF * q : HALF * (q + 1)], u[HALF:, HALF * q : HALF * (q + 1)]
        lines = jnp.concatenate(
            [jnp.where(low, re, roll(im)), jnp.where(low, roll(re), im)], 0
        )
        lh, ll = cut(lines)
        out.append(
            mm(jnp.concatenate([lh, ll], 1), jnp.concatenate([txh, txh], 0)) + mm(lh, txl)
        )
    return out


def own_kernel(core_ref, own, tyh, tyl, tw, txh, txl, out):
    core = core_ref[0]
    for q, term in enumerate(half_planes(own, 0, tyh, tyl, tw, txh[core], txl[core])):
        out[q] = term


def update_kernel(core_ref, partial, other, rho_ref, support, tyh, tyl, tw, txh, txl, out, scratch):
    core = 1 - core_ref[0]
    for q, term in enumerate(half_planes(other, 2, tyh, tyl, tw, txh[core], txl[core])):
        moduled = partial[q] + term
        for side in range(2):
            lanes = slice(HALF * side, HALF * (side + 1))
            for o in range(2):
                rows = moduled[HALF * o : HALF * (o + 1), lanes]
                scratch[2 * q + side, pl.ds(o, HALF, stride=2), :] = rows
            rho = rho_ref[q, :, lanes].astype(jnp.float32)
            mask = support[q, :, lanes].astype(jnp.float32)
            m = scratch[2 * q + side]
            out[q, :, lanes] = (rho + mask * (2.0 * m - rho) - m).astype(jnp.bfloat16)


SMEM = pl.BlockSpec(memory_space=pltpu.SMEM)
VMEM = pl.BlockSpec(memory_space=pltpu.VMEM)
HBM = pl.BlockSpec(memory_space=pltpu.HBM)


def call(kernel, out_shape, operands, in_specs, flops, vmem=40 * 2**20, **more):
    return pl.pallas_call(
        kernel,
        out_shape=out_shape,
        in_specs=in_specs,
        out_specs=jax.tree.map(lambda _: VMEM, out_shape),
        compiler_params=pltpu.CompilerParams(vmem_limit_bytes=vmem),
        cost_estimate=pl.CostEstimate(
            flops=int(flops), bytes_accessed=2 * 2**20, transcendentals=0
        ),
        **more,
    )(*operands)


def shards(density, amplitudes, support):
    c = {k: jax.tree.map(jnp.asarray, v) for k, v in constants().items()}
    swap = [(i, i ^ 1) for i in range(2 * CHIPS)]
    same_core = [[int(2 * chip + core) for chip in ORDER] for core in range(2)]
    core = (lax.axis_index("slab") % 2).astype(jnp.int32).reshape(1)

    def exchange(x):
        return lax.all_to_all(
            x, "slab", split_axis=0, concat_axis=0, tiled=True, axis_index_groups=same_core
        )

    def shape(dims, kind):
        return jax.ShapeDtypeStruct(dims, kind)

    density_other = lax.ppermute(density, "slab", swap)
    amplitudes_other = lax.ppermute(amplitudes, "slab", swap)
    table = lax.dynamic_index_in_dim(c["first"], core[0], 0, keepdims=False)
    sent = call(
        forward_kernel,
        shape((CHIPS * 16, HALF), jnp.int32),
        (density, amplitudes, density_other, amplitudes_other, table, c["tw"]),
        [VMEM] * 6,
        800e6,
        scratch_shapes=[pltpu.VMEM((4, N, HALF), jnp.float32)],
    )
    lines = exchange(sent.reshape(CHIPS, 16, HALF)).reshape(CHIPS * 16, HALF)
    sent = call(
        middle_kernel,
        shape((CHIPS * 8, HALF), jnp.int32),
        (core, lines, *c["tz"], *c["tzi"], c["tzw"], c["rev_all"]),
        [SMEM] + [VMEM] * 7,
        800e6,
    )
    planes = exchange(sent.reshape(CHIPS, 8, HALF)).reshape(CHIPS * 8, HALF)
    planes_other = lax.ppermute(planes, "slab", swap)
    tables = (*c["tyi"], c["tw"], *c["txi"])
    partial = call(
        own_kernel,
        shape(density.shape, jnp.float32),
        (core, planes, *tables),
        [SMEM] + [VMEM] * 6,
        400e6,
    )
    return call(
        update_kernel,
        shape(density.shape, jnp.bfloat16),
        (core, partial, planes_other, density, support, *tables),
        [SMEM] + [VMEM] * 9,
        400e6,
        scratch_shapes=[pltpu.VMEM((4, N, HALF), jnp.float32)],
    )


def solution(mesh):
    spec = P("slab", "member", None)
    return jax.shard_map(
        shards, mesh=mesh, in_specs=(spec, spec, spec), out_specs=spec, check_vma=False
    )
```

time: 55.3 us -> 53.8 us (0.973)
  other arithmetic: 1.08 us -> 0 us
  Pallas kernels: 6.1 us -> 5.31 us
    concatenate x1 -> x0, other arithmetic: 1.08 us -> none  [shards(): own = jnp.concatenate([density, amplitudes], 0)]
    pallas_call x4, Pallas kernels: 6.1 us -> 5.31 us  [call(): pl.pallas_call(kernel, out_shape=out_shape, in_specs=in_specs, out_specs=...]
  transfers between devices with their start and end apart: 3 -> 3, of which waited for: 1 -> 3; matrix products, arithmetic and copies ran while one was open for 4% -> 2% of each run, Pallas kernels for 2% -> 2%
where the time goes in v4:
time: 53.8 us; the launch traced here: 53.6 us
  blocking collectives  41.2 us (77%)
  Pallas kernels  5.31 us (10%)
  starting transfers between devices  5.12 us (10%)
  local copies, waits for them, and re-layouts  1.19 us (2%)
  waiting for transfers between devices  0.7 us (1%)
    all_to_all x2, blocking collectives, exchange(): lax.all_to_all(x, 'slab', split_axis=0, concat_axis=0, tiled=True, axis_i...  41.2 us
    pallas_call x4, Pallas kernels, call(): pl.pallas_call(kernel, out_shape=out_shape, in_specs=in_specs, out_specs=...  5.31 us
    ppermute x1, starting transfers between devices, shards(): amplitudes_other = lax.ppermute(amplitudes, 'slab', swap)  3.24 us
    ppermute x1, starting transfers between devices, shards(): planes_other = lax.ppermute(planes, 'slab', swap)  1.79 us
    squeeze x1, local copies, waits for them, and re-layouts, shards(): table = lax.dynamic_index_in_dim(c['first'], core[0], 0, keepdims=False)  1.1 us
  transfers between devices with their start and end apart: 3, of which 3 were waited for; matrix products, arithmetic and copies ran while one was open for 2% of the time, Pallas kernels for 2%

profile of v4, /device:TPU:1, one launch (start us, length us, event | category | flops | bytes accessed | tf_op | source)
XLA Modules:
  0.0 53.6 jit_solution(9893347189635536140)
XLA Ops:
  0.0 3.2 %collective-permute-start.1 = (bf16[2,256,256]{2,1,0:T(8,128)(2,1)}, bf16[2,256,256]{2,1,0:T(8,128)(2,1)S(1)}, u32[]{:S(2)}, u32[]{:S(2)}) collective-permute-start(bf16[2,256,256]{2,1,0:T(8,128)(2,1)} %amp.1), channel_id=1, source_target_pairs={{0,2},{2,0},{4,6},{6,4},{8,10},{10,8},{12,14},{14,12},{16,18},{18,... | collective-permute-start | bytes 786440 | tf_op jit(solution)/shard_map/ppermute | solution.py:319
  3.2 0.1 collective-permute-start
  3.3 1.1 %dynamic-slice_bitcast_fusion.table = bf16[1152,256]{1,0:T(8,128)(2,1)S(1)} fusion(bf16[2,1152,256]{2,1,0:T(8,128)(2,1)} %constant.50.clone, s32[]{:T(128)S(6)} %select_n.12), kind=kLoop, calls=%fused_computation | loop fusion | bytes 1179652 | tf_op jit(solution)/shard_map/jit(dynamic_index_in_dim)/squeeze | solution.py:320
  4.4 0.0 copy-start.8
  4.5 0.0 copy-start.9
  4.5 0.0 copy-start.10
  4.5 0.0 copy-start.11
  4.5 0.0 copy-start.12
  4.5 0.0 copy-start.13
  4.5 0.1 collective-permute-done.1.amp_other
  4.6 0.4 collective-permute-done.rho_other
  5.0 0.0 copy-done.2
  5.0 0.0 copy-done.7
  5.0 0.0 copy-done.1
  5.0 1.4 %shard_map.145 = s32[1024,128]{1,0:T(8,128)S(1)} custom-call(bf16[2,256,256]{2,1,0:T(8,128)(2,1)S(1)} %copy-done.1, bf16[2,256,256]{2,1,0:T(8,128)(2,1)S(1)} %copy-done.7, bf16[2,256,256]{2,1,0:T(8,128)(2,1)S(1)} %collective-permute-done.rho_other, bf16[2,256,256]{2,1,0:T(8,128)(2,1)S(1)} %collective-permute-done.1.amp_other, ...), custom_call_target="tpu_custom_call" | custom-call | flops 800000000 | bytes 2097152 | tf_op jit(solution)/shard_map/pallas_call | solution.py:291
  6.4 24.2 %all_to_all.10 = s32[64,16,128]{2,1,0:T(8,128)S(1)} all-to-all(s32[64,16,128]{2,1,0:T(8,128)S(1)} %bitcast.8), channel_id=1, replica_groups={{176,180,184,188,160,164,168,172,144,148,152,156,128,132,136,140,240,24..., dimensions={0} | all-to-all | bytes 1048576 | tf_op jit(solution)/shard_map/all_to_all | solution.py:311
  30.7 0.0 copy-done.8
  30.7 0.0 copy-done.9
  30.7 0.0 copy-done.10
  30.7 0.0 copy-done.11
  30.7 0.0 copy-start.3
  30.7 0.0 copy-start.4
  30.7 0.0 copy-start.5
  30.8 0.0 copy-start.6
  30.8 1.3 %shard_map.146 = s32[512,128]{1,0:T(8,128)S(1)} custom-call(s32[1]{0:T(128)} %bitcast.core_ref, s32[1024,128]{1,0:T(8,128)S(1)} %bitcast.7, bf16[2,256,256]{2,1,0:T(8,128)(2,1)S(1)} %copy-done.12, bf16[2,256,256]{2,1,0:T(8,128)(2,1)S(1)} %copy-done.11, bf16[2,256,256]{2,1,0:T(8,128)(2,1)S(1)} %copy-done.10, bf16[2,256,256]{2,1,0:T(8,128)(2,1)S(1)} %copy-done.9, ...), custom_call_target="tpu_custom_call" | custom-call | flops 800000000 | bytes 2097152 | tf_op jit(solution)/shard_map/pallas_call | solution.py:291
  32.0 0.0 copy-start
  32.1 16.9 %all_to_all.11 = s32[64,8,128]{2,1,0:T(8,128)S(1)} all-to-all(s32[64,8,128]{2,1,0:T(8,128)S(1)} %bitcast.9), channel_id=1, replica_groups={{176,180,184,188,160,164,168,172,144,148,152,156,128,132,136,140,240,24..., dimensions={0} | all-to-all | bytes 524288 | tf_op jit(solution)/shard_map/all_to_all | solution.py:311
  49.0 1.8 %collective-permute-start.2 = (s32[512,128]{1,0:T(8,128)S(1)}, s32[512,128]{1,0:T(8,128)S(1)}, u32[]{:S(2)}, u32[]{:S(2)}) collective-permute-start(s32[512,128]{1,0:T(8,128)S(1)} %bitcast.10), channel_id=1, source_target_pairs={{0,2},{2,0},{4,6},{6,4},{8,10},{10,8},{12,14},{14,12},{16,18},{18,... | collective-permute-start | bytes 786440 | tf_op jit(solution)/shard_map/ppermute | solution.py:338
  50.8 0.0 copy-done.3
  50.8 0.9 %shard_map.147.partial = f32[2,256,256]{2,1,0:T(8,128)S(1)} custom-call(s32[1]{0:T(128)} %bitcast.core_ref, s32[512,128]{1,0:T(8,128)S(1)} %bitcast.11, bf16[256,256]{1,0:T(8,128)(2,1)S(1)} %copy-done.6, bf16[256,256]{1,0:T(8,128)(2,1)S(1)} %copy-done.5, f32[2,128,128]{2,1,0:T(8,128)S(1)} %copy-done.2, bf16[2,128,256]{2,1,0:T(8,128)(2,1)S(1)} %copy-done.4, ...), custom_call_target="tpu_custom_call" | custom-call | flops 400000000 | bytes 2097152 | tf_op jit(solution)/shard_map/pallas_call | solution.py:291
  51.7 0.2 collective-permute-done.2.other
  51.9 1.7 %shard_map.148 = bf16[2,256,256]{2,1,0:T(8,128)(2,1)} custom-call(s32[1]{0:T(128)} %bitcast.core_ref, f32[2,256,256]{2,1,0:T(8,128)S(1)} %shard_map.147.partial, s32[512,128]{1,0:T(8,128)S(1)} %collective-permute-done.2.other, bf16[2,256,256]{2,1,0:T(8,128)(2,1)S(1)} %copy-done.1, s32[2,256,256]{2,1,0:T(8,128)S(1)} %copy-done, ...), custom_call_target="tpu_custom_call" | custom-call | flops 400000000 | bytes 2097152 | tf_op jit(solution)/shard_map/pallas_call | solution.py:291
  (9 shorter events, 0.0 us)
Async XLA Ops:
  0.0 5.0 %copy-start.2 = (f32[2,128,128]{2,1,0:T(8,128)S(1)}, f32[2,128,128]{2,1,0:T(8,128)}, u32[]{:S(2)}) copy-start(f32[2,128,128]{2,1,0:T(8,128)} %constant.49.clone.tw) | copy-start | bytes 393220
  0.0 5.0 %copy-start.7 = (bf16[2,256,256]{2,1,0:T(8,128)(2,1)S(1)}, bf16[2,256,256]{2,1,0:T(8,128)(2,1)}, u32[]{:S(2)}) copy-start(bf16[2,256,256]{2,1,0:T(8,128)(2,1)} %amp.1) | copy-start | bytes 786436
  0.0 5.0 %copy-start.1 = (bf16[2,256,256]{2,1,0:T(8,128)(2,1)S(1)}, bf16[2,256,256]{2,1,0:T(8,128)(2,1)}, u32[]{:S(2)}) copy-start(bf16[2,256,256]{2,1,0:T(8,128)(2,1)} %rho_ref.1) | copy-start | bytes 786436
  0.0 4.6 %collective-permute-start.1 = (bf16[2,256,256]{2,1,0:T(8,128)(2,1)}, bf16[2,256,256]{2,1,0:T(8,128)(2,1)S(1)}, u32[]{:S(2)}, u32[]{:S(2)}) collective-permute-start(bf16[2,256,256]{2,1,0:T(8,128)(2,1)} %amp.1), channel_id=1, source_target_pairs={{0,2},{2,0},{4,6},{6,4},{8,10},{10,8},{12,14},{14,12},{16,18},{18,... | collective-permute-start | bytes 786440 | tf_op jit(solution)/shard_map/ppermute | solution.py:319
  3.2 1.7 %collective-permute-start = (bf16[2,256,256]{2,1,0:T(8,128)(2,1)}, bf16[2,256,256]{2,1,0:T(8,128)(2,1)S(1)}, u32[]{:S(2)}, u32[]{:S(2)}) collective-permute-start(bf16[2,256,256]{2,1,0:T(8,128)(2,1)} %rho_ref.1), channel_id=1, source_target_pairs={{0,2},{2,0},{4,6},{6,4},{8,10},{10,8},{12,14},{14,12},{16,18},{18,... | collective-permute-start | bytes 786440 | tf_op jit(solution)/shard_map/ppermute | solution.py:318
  4.4 26.2 %copy-start.8 = (f32[2,2,128,128]{3,2,1,0:T(8,128)S(1)}, f32[2,2,128,128]{3,2,1,0:T(8,128)}, u32[]{:S(2)}) copy-start(f32[2,2,128,128]{3,2,1,0:T(8,128)} %constant.58.clone.tzw) | copy-start | bytes 786436
  4.5 26.2 %copy-start.9 = (bf16[2,256,256]{2,1,0:T(8,128)(2,1)S(1)}, bf16[2,256,256]{2,1,0:T(8,128)(2,1)}, u32[]{:S(2)}) copy-start(bf16[2,256,256]{2,1,0:T(8,128)(2,1)} %constant.57.clone.tzil) | copy-start | bytes 786436
  4.5 26.2 %copy-start.10 = (bf16[2,256,256]{2,1,0:T(8,128)(2,1)S(1)}, bf16[2,256,256]{2,1,0:T(8,128)(2,1)}, u32[]{:S(2)}) copy-start(bf16[2,256,256]{2,1,0:T(8,128)(2,1)} %constant.56.clone.tzih) | copy-start | bytes 786436
  4.5 26.2 %copy-start.11 = (bf16[2,256,256]{2,1,0:T(8,128)(2,1)S(1)}, bf16[2,256,256]{2,1,0:T(8,128)(2,1)}, u32[]{:S(2)}) copy-start(bf16[2,256,256]{2,1,0:T(8,128)(2,1)} %constant.55.clone.tzl) | copy-start | bytes 786436
  4.5 26.2 %copy-start.12 = (bf16[2,256,256]{2,1,0:T(8,128)(2,1)S(1)}, bf16[2,256,256]{2,1,0:T(8,128)(2,1)}, u32[]{:S(2)}) copy-start(bf16[2,256,256]{2,1,0:T(8,128)(2,1)} %constant.54.clone.tzh) | copy-start | bytes 786436
  4.5 26.2 %copy-start.13 = (bf16[256,256]{1,0:T(8,128)(2,1)S(1)}, bf16[256,256]{1,0:T(8,128)(2,1)}, u32[]{:S(2)}) copy-start(bf16[256,256]{1,0:T(8,128)(2,1)} %constant.53.clone.rev) | copy-start | bytes 393220
  30.7 20.0 %copy-start.3 = (bf16[2,128,256]{2,1,0:T(8,128)(2,1)S(1)}, bf16[2,128,256]{2,1,0:T(8,128)(2,1)}, u32[]{:S(2)}) copy-start(bf16[2,128,256]{2,1,0:T(8,128)(2,1)} %constant.52.clone.txl) | copy-start | bytes 393220
  30.7 20.0 %copy-start.4 = (bf16[2,128,256]{2,1,0:T(8,128)(2,1)S(1)}, bf16[2,128,256]{2,1,0:T(8,128)(2,1)}, u32[]{:S(2)}) copy-start(bf16[2,128,256]{2,1,0:T(8,128)(2,1)} %constant.51.clone.txh) | copy-start | bytes 393220
  30.7 20.0 %copy-start.5 = (bf16[256,256]{1,0:T(8,128)(2,1)S(1)}, bf16[256,256]{1,0:T(8,128)(2,1)}, u32[]{:S(2)}) copy-start(bf16[256,256]{1,0:T(8,128)(2,1)} %constant.48.clone.tyl) | copy-start | bytes 393220
  30.8 20.0 %copy-start.6 = (bf16[256,256]{1,0:T(8,128)(2,1)S(1)}, bf16[256,256]{1,0:T(8,128)(2,1)}, u32[]{:S(2)}) copy-start(bf16[256,256]{1,0:T(8,128)(2,1)} %constant.47.clone.tyh) | copy-start | bytes 393220
  32.0 19.9 %copy-start = (s32[2,256,256]{2,1,0:T(8,128)S(1)}, s32[2,256,256]{2,1,0:T(8,128)}, u32[]{:S(2)}) copy-start(s32[2,256,256]{2,1,0:T(8,128)} %support.1) | copy-start | bytes 1572868
  49.0 3.0 %collective-permute-start.2 = (s32[512,128]{1,0:T(8,128)S(1)}, s32[512,128]{1,0:T(8,128)S(1)}, u32[]{:S(2)}, u32[]{:S(2)}) collective-permute-start(s32[512,128]{1,0:T(8,128)S(1)} %bitcast.10), channel_id=1, source_target_pairs={{0,2},{2,0},{4,6},{6,4},{8,10},{10,8},{12,14},{14,12},{16,18},{18,... | collective-permute-start | bytes 786440 | tf_op jit(solution)/shard_map/ppermute | solution.py:338

commit v5 on v4

--- a/solution.py
+++ b/solution.py
@@ -107,21 +107,25 @@
     s = jnp.exp2(-(e + low)) * FULL
     e = e.astype(jnp.int32)
 
-    def code(x, factor):
-        return jnp.floor(x * factor + 0.5).astype(jnp.int32)
-
-    word0 = (code(re0, s) << 17) | ((code(im0, s) & 0x7FFF) << 2) | (e & 3)
-    word1 = (code(re1, s) << 17) | ((code(im1, 0.5 * s) & 0x3FFF) << 3) | (e >> 2)
+    def code(x, factor, middle):
+        return (x * factor + (middle + 0.5)).astype(jnp.int32)
+
+    word0 = (code(re0, s, 16384) << 17) | (code(im0, s, 16384) << 2) | (e & 3)
+    word1 = (code(re1, s, 16384) << 17) | (code(im1, 0.5 * s, 8192) << 3) | (e >> 2)
     return word0, word1
 
 
 def unpack(word0, word1, low):
     e = (word0 & 3) | ((word1 & 7) << 2)
     s = jnp.exp2(e.astype(jnp.float32) + low) * (1.0 / FULL)
-    re0 = (word0 >> 17).astype(jnp.float32) * s
-    im0 = ((word0 << 15) >> 17).astype(jnp.float32) * s
-    re1 = (word1 >> 17).astype(jnp.float32) * s
-    im1 = ((word1 << 15) >> 18).astype(jnp.float32) * (2.0 * s)
+
+    def value(code, factor, middle):
+        return (code - middle).astype(jnp.float32) * factor
+
+    re0 = value(lax.shift_right_logical(word0, 17), s, 16384)
+    im0 = value((word0 >> 2) & 0x7FFF, s, 16384)
+    re1 = value(lax.shift_right_logical(word1, 17), s, 16384)
+    im1 = value((word1 >> 3) & 0x3FFF, 2.0 * s, 8192)
     return re0, im0, re1, im1
 
 
@@ -143,42 +147,48 @@
     )
 
 
-def forward_planes(first, rho_ref, amp_ref, table, tw, out, scratch):
+def forward_kernel(rho_own, amp_own, rho_other, amp_other, table, tw, out, scratch):
     low = lower(HALF)
     c, s = tw[0], tw[1]
-    stack = []
-    for q in range(2):
-        a = mm(rho_ref[q], table[:N])
-        scratch[q] = a[:, :HALF] + a[:, HALF:]
-        even = scratch[q, pl.ds(0, HALF, stride=2), :]
-        odd = scratch[q, pl.ds(1, HALF, stride=2), :]
-        stack += [jnp.where(low, even, roll(odd)), jnp.where(low, roll(even), odd)]
-    u = left3(table[N : 2 * N], table[2 * N : 3 * N], square(stack))
-    parts = []
-    for q in range(2):
-        re, im = u[:HALF, HALF * q : HALF * (q + 1)], u[HALF:, HALF * q : HALF * (q + 1)]
-        parts += [butterfly(re * c + im * s, low), butterfly(im * c - re * s, low)]
-    words = pack(*parts, FORWARD_LOW)
-    mirrors = []
-    directs = []
-    for q in range(2):
-        both = mm(amp_ref[q], table[3 * N : 4 * N])
-        directs.append(jnp.where(low, both[:HALF, :HALF], both[HALF:, :HALF]))
-        mirrors.append(jnp.where(low, both[HALF:, HALF:], both[:HALF, HALF:]))
+    rho = [rho_own[0], rho_own[1], rho_other[0], rho_other[1]]
+    amp = [amp_own[0], amp_own[1], amp_other[0], amp_other[1]]
+
+    def along_x(p):
+        a = mm(rho[p], table[:N])
+        scratch[p] = a[:, :HALF] + a[:, HALF:]
+        even = scratch[p, pl.ds(0, HALF, stride=2), :]
+        odd = scratch[p, pl.ds(1, HALF, stride=2), :]
+        return [jnp.where(low, even, roll(odd)), jnp.where(low, roll(even), odd)]
+
+    def along_y(stack):
+        u = left3(table[N : 2 * N], table[2 * N : 3 * N], square(stack))
+        parts = []
+        for q in range(2):
+            re, im = u[:HALF, HALF * q : HALF * (q + 1)], u[HALF:, HALF * q : HALF * (q + 1)]
+            parts += [butterfly(re * c + im * s, low), butterfly(im * c - re * s, low)]
+        return parts
+
+    def picked(p):
+        both = mm(amp[p], table[3 * N : 4 * N])
+        direct = jnp.where(low, both[:HALF, :HALF], both[HALF:, :HALF])
+        return direct, jnp.where(low, both[HALF:, HALF:], both[:HALF, HALF:])
+
+    def store(slot, words):
+        for r in range(2):
+            out[pl.ds(slot + r, CHIPS, stride=16), :] = words[CHIPS * r : CHIPS * (r + 1)]
+
+    lines = [along_x(p) for p in range(4)]
+    first = along_y(lines[0] + lines[1])
+    directs, mirrors = zip(*(picked(p) for p in range(4)))
+    second = along_y(lines[2] + lines[3])
+    for q, words in enumerate(pack(*first, FORWARD_LOW)):
+        store(2 * q, words)
     mirrors = mm(table[4 * N :, :HALF], jnp.concatenate(mirrors, 1).astype(jnp.bfloat16))
-    for q in range(2):
-        mirror = mirrors[:, HALF * q : HALF * (q + 1)]
-        coded = ((directs[q] * AMP_UNIT).astype(jnp.int32) << 16) | (mirror * AMP_UNIT).astype(jnp.int32)
-        for r in range(2):
-            rows = slice(CHIPS * r, CHIPS * (r + 1))
-            slot = 2 * (first + q) + r
-            out[pl.ds(slot, CHIPS, stride=16), :] = words[q][rows]
-            out[pl.ds(8 + slot, CHIPS, stride=16), :] = coded[rows]
-
-
-def forward_kernel(rho, amp, rho_other, amp_other, table, tw, out, scratch):
-    forward_planes(0, rho, amp, table, tw, out, scratch.at[:2])
-    forward_planes(2, rho_other, amp_other, table, tw, out, scratch.at[2:])
+    for p in range(4):
+        mirror = (mirrors[:, HALF * p : HALF * (p + 1)] * AMP_UNIT).astype(jnp.int32)
+        store(8 + 2 * p, ((directs[p] * AMP_UNIT).astype(jnp.int32) << 16) | mirror)
+    for q, words in enumerate(pack(*second, FORWARD_LOW)):
+        store(4 + 2 * q, words)
 
 
 def middle_kernel(core_ref, msg, tzh, tzl, tzih, tzil, tzw, rev, out):
@@ -216,7 +226,7 @@
     for r in range(2):
         re, im = spectra[r]
         target = (directs[r] + mirrors[:, HALF * r : HALF * (r + 1)]) * (0.5 / AMP_UNIT)
-        ratio = target / jnp.maximum(jnp.sqrt(re * re + im * im), FLOOR)
+        ratio = target * lax.rsqrt(jnp.maximum(re * re + im * im, FLOOR * FLOOR))
         re, im = re * ratio, im * ratio
         odd_re, odd_im = re[:HALF] - re[HALF:], im[:HALF] - im[HALF:]
         lines = square(
@@ -261,25 +271,38 @@
     return out
 
 
-def own_kernel(core_ref, own, tyh, tyl, tw, txh, txl, out):
+def interleave(rows, side, scratch):
+    for o in range(2):
+        scratch[pl.ds(o, HALF, stride=2), :] = rows[
+            HALF * o : HALF * (o + 1), HALF * side : HALF * (side + 1)
+        ]
+    return scratch[...]
+
+
+def own_kernel(core_ref, own, rho_ref, support, tyh, tyl, tw, txh, txl, out, scratch):
     core = core_ref[0]
     for q, term in enumerate(half_planes(own, 0, tyh, tyl, tw, txh[core], txl[core])):
-        out[q] = term
-
-
-def update_kernel(core_ref, partial, other, rho_ref, support, tyh, tyl, tw, txh, txl, out, scratch):
-    core = 1 - core_ref[0]
-    for q, term in enumerate(half_planes(other, 2, tyh, tyl, tw, txh[core], txl[core])):
-        moduled = partial[q] + term
         for side in range(2):
             lanes = slice(HALF * side, HALF * (side + 1))
-            for o in range(2):
-                rows = moduled[HALF * o : HALF * (o + 1), lanes]
-                scratch[2 * q + side, pl.ds(o, HALF, stride=2), :] = rows
+            m = interleave(term, side, scratch.at[2 * q + side])
             rho = rho_ref[q, :, lanes].astype(jnp.float32)
             mask = support[q, :, lanes].astype(jnp.float32)
-            m = scratch[2 * q + side]
-            out[q, :, lanes] = (rho + mask * (2.0 * m - rho) - m).astype(jnp.bfloat16)
+            out[q, :, lanes] = rho + mask * (2.0 * m - rho) - m
+
+
+def update_kernel(core_ref, partial, other, support, tyh, tyl, tw, txh, txl, out, scratch, done, sems):
+    core = 1 - core_ref[0]
+    copies = []
+    for q, term in enumerate(half_planes(other, 2, tyh, tyl, tw, txh[core], txl[core])):
+        for side in range(2):
+            lanes = slice(HALF * side, HALF * (side + 1))
+            m = interleave(term, side, scratch.at[2 * q + side])
+            mask = support[q, :, lanes].astype(jnp.float32)
+            done[q, :, lanes] = (partial[q, :, lanes] + (2.0 * mask - 1.0) * m).astype(jnp.bfloat16)
+        copies.append(pltpu.make_async_copy(done.at[q], out.at[q], sems.at[q]))
+        copies[q].start()
+    for copy in copies:
+        copy.wait()
 
 
 SMEM = pl.BlockSpec(memory_space=pltpu.SMEM)
@@ -287,13 +310,13 @@
 HBM = pl.BlockSpec(memory_space=pltpu.HBM)
 
 
-def call(kernel, out_shape, operands, in_specs, flops, vmem=40 * 2**20, **more):
+def call(kernel, out_shape, operands, in_specs, flops, out_specs=VMEM, **more):
     return pl.pallas_call(
         kernel,
         out_shape=out_shape,
         in_specs=in_specs,
-        out_specs=jax.tree.map(lambda _: VMEM, out_shape),
-        compiler_params=pltpu.CompilerParams(vmem_limit_bytes=vmem),
+        out_specs=out_specs,
+        compiler_params=pltpu.CompilerParams(vmem_limit_bytes=40 * 2**20),
         cost_estimate=pl.CostEstimate(
             flops=int(flops), bytes_accessed=2 * 2**20, transcendentals=0
         ),
@@ -340,17 +363,23 @@
     partial = call(
         own_kernel,
         shape(density.shape, jnp.float32),
-        (core, planes, *tables),
-        [SMEM] + [VMEM] * 6,
+        (core, planes, density, support, *tables),
+        [SMEM] + [VMEM] * 8,
         400e6,
+        scratch_shapes=[pltpu.VMEM((4, N, HALF), jnp.float32)],
     )
     return call(
         update_kernel,
         shape(density.shape, jnp.bfloat16),
-        (core, partial, planes_other, density, support, *tables),
-        [SMEM] + [VMEM] * 9,
+        (core, partial, planes_other, support, *tables),
+        [SMEM] + [VMEM] * 8,
         400e6,
-        scratch_shapes=[pltpu.VMEM((4, N, HALF), jnp.float32)],
+        out_specs=HBM,
+        scratch_shapes=[
+            pltpu.VMEM((4, N, HALF), jnp.float32),
+            pltpu.VMEM(density.shape, jnp.bfloat16),
+            pltpu.SemaphoreType.DMA((2,)),
+        ],
     )
 
 

time: 53.8 us -> 53.3 us (level)
  no operation moved by 1% of the time
where the time goes in v5:
time: 53.3 us; the launch traced here: 53.1 us
  blocking collectives  41 us (77%)
  starting transfers between devices  5.12 us (10%)
  Pallas kernels  5.01 us (9%)
  local copies, waits for them, and re-layouts  1.19 us (2%)
  waiting for transfers between devices  0.62 us (1%)
    all_to_all x2, blocking collectives, exchange(): lax.all_to_all(x, 'slab', split_axis=0, concat_axis=0, tiled=True, axis_i...  41 us
    pallas_call x4, Pallas kernels, call(): pl.pallas_call(kernel, out_shape=out_shape, in_specs=in_specs, out_specs=...  5.01 us
    ppermute x1, starting transfers between devices, shards(): amplitudes_other = lax.ppermute(amplitudes, 'slab', swap)  3.24 us
    ppermute x1, starting transfers between devices, shards(): planes_other = lax.ppermute(planes, 'slab', swap)  1.79 us
    squeeze x1, local copies, waits for them, and re-layouts, shards(): table = lax.dynamic_index_in_dim(c['first'], core[0], 0, keepdims=False)  1.1 us
  transfers between devices with their start and end apart: 3, of which 3 were waited for; matrix products, arithmetic and copies ran while one was open for 2% of the time, Pallas kernels for 2%

profile of v5, /device:TPU:1, one launch (start us, length us, event | category | flops | bytes accessed | tf_op | source)
XLA Modules:
  0.0 53.1 jit_solution(2049291123595489436)
XLA Ops:
  0.0 3.2 %collective-permute-start.1 = (bf16[2,256,256]{2,1,0:T(8,128)(2,1)}, bf16[2,256,256]{2,1,0:T(8,128)(2,1)S(1)}, u32[]{:S(2)}, u32[]{:S(2)}) collective-permute-start(bf16[2,256,256]{2,1,0:T(8,128)(2,1)} %amp_own.1), channel_id=1, source_target_pairs={{0,2},{2,0},{4,6},{6,4},{8,10},{10,8},{12,14},{14,12},{16,18},{18,... | collective-permute-start | bytes 786440 | tf_op jit(solution)/shard_map/ppermute | solution.py:342
  3.2 0.1 collective-permute-start
  3.3 1.1 %dynamic-slice_bitcast_fusion.table = bf16[1152,256]{1,0:T(8,128)(2,1)S(1)} fusion(bf16[2,1152,256]{2,1,0:T(8,128)(2,1)} %constant.50.clone, s32[]{:T(128)S(6)} %select_n.12), kind=kLoop, calls=%fused_computation | loop fusion | bytes 1179652 | tf_op jit(solution)/shard_map/jit(dynamic_index_in_dim)/squeeze | solution.py:343
  4.4 0.0 copy-start.8
  4.5 0.0 copy-start.9
  4.5 0.0 copy-start.10
  4.5 0.0 copy-start.11
  4.5 0.0 copy-start.12
  4.5 0.0 copy-start.13
  4.5 0.1 collective-permute-done.1.amp_other
  4.6 0.4 collective-permute-done.rho_other
  5.0 0.0 copy-done.1
  5.0 0.0 copy-done.7
  5.0 0.0 copy-done.6
  5.0 1.2 %shard_map.145 = s32[1024,128]{1,0:T(8,128)S(1)} custom-call(bf16[2,256,256]{2,1,0:T(8,128)(2,1)S(1)} %copy-done.6, bf16[2,256,256]{2,1,0:T(8,128)(2,1)S(1)} %copy-done.7, bf16[2,256,256]{2,1,0:T(8,128)(2,1)S(1)} %collective-permute-done.rho_other, bf16[2,256,256]{2,1,0:T(8,128)(2,1)S(1)} %collective-permute-done.1.amp_other, ...), custom_call_target="tpu_custom_call" | custom-call | flops 800000000 | bytes 2097152 | tf_op jit(solution)/shard_map/pallas_call | solution.py:314
  6.2 24.2 %all_to_all.10 = s32[64,16,128]{2,1,0:T(8,128)S(1)} all-to-all(s32[64,16,128]{2,1,0:T(8,128)S(1)} %bitcast.10), channel_id=1, replica_groups={{176,180,184,188,160,164,168,172,144,148,152,156,128,132,136,140,240,24..., dimensions={0} | all-to-all | bytes 1048576 | tf_op jit(solution)/shard_map/all_to_all | solution.py:334
  30.4 0.0 copy-done.8
  30.4 0.0 copy-done.9
  30.4 0.0 copy-done.10
  30.4 0.0 copy-start
  30.5 0.0 copy-start.2
  30.5 0.0 copy-start.3
  30.5 0.0 copy-start.4
  30.5 0.0 copy-start.5
  30.5 1.2 %shard_map.146 = s32[512,128]{1,0:T(8,128)S(1)} custom-call(s32[1]{0:T(128)} %bitcast.core_ref, s32[1024,128]{1,0:T(8,128)S(1)} %bitcast.9, bf16[2,256,256]{2,1,0:T(8,128)(2,1)S(1)} %copy-done.12, bf16[2,256,256]{2,1,0:T(8,128)(2,1)S(1)} %copy-done.11, bf16[2,256,256]{2,1,0:T(8,128)(2,1)S(1)} %copy-done.10, bf16[2,256,256]{2,1,0:T(8,128)(2,1)S(1)} %copy-done.9, ...), custom_call_target="tpu_custom_call" | custom-call | flops 800000000 | bytes 2097152 | tf_op jit(solution)/shard_map/pallas_call | solution.py:314
  31.7 16.8 %all_to_all.11 = s32[64,8,128]{2,1,0:T(8,128)S(1)} all-to-all(s32[64,8,128]{2,1,0:T(8,128)S(1)} %bitcast.11), channel_id=1, replica_groups={{176,180,184,188,160,164,168,172,144,148,152,156,128,132,136,140,240,24..., dimensions={0} | all-to-all | bytes 524288 | tf_op jit(solution)/shard_map/all_to_all | solution.py:334
  48.5 1.8 %collective-permute-start.2 = (s32[512,128]{1,0:T(8,128)S(1)}, s32[512,128]{1,0:T(8,128)S(1)}, u32[]{:S(2)}, u32[]{:S(2)}) collective-permute-start(s32[512,128]{1,0:T(8,128)S(1)} %bitcast.7), channel_id=1, source_target_pairs={{0,2},{2,0},{4,6},{6,4},{8,10},{10,8},{12,14},{14,12},{16,18},{18,... | collective-permute-start | bytes 786440 | tf_op jit(solution)/shard_map/ppermute | solution.py:361
  50.3 0.0 copy-done.2
  50.3 0.0 copy-done.4
  50.3 1.0 %shard_map.147.partial = f32[2,256,256]{2,1,0:T(8,128)S(1)} custom-call(s32[1]{0:T(128)} %bitcast.core_ref, s32[512,128]{1,0:T(8,128)S(1)} %bitcast.8, bf16[2,256,256]{2,1,0:T(8,128)(2,1)S(1)} %copy-done.6, s32[2,256,256]{2,1,0:T(8,128)S(1)} %copy-done, bf16[256,256]{1,0:T(8,128)(2,1)S(1)} %copy-done.5, bf16[256,256]{1,0:T(8,128)(2,1)S(1)} %copy-done.4, ...), custom_call_target="tpu_custom_call" | custom-call | flops 400000000 | bytes 2097152 | tf_op jit(solution)/shard_map/pallas_call | solution.py:314
  51.3 0.1 collective-permute-done.2.other
  51.5 1.6 %shard_map.148 = bf16[2,256,256]{2,1,0:T(8,128)(2,1)} custom-call(s32[1]{0:T(128)} %bitcast.core_ref, f32[2,256,256]{2,1,0:T(8,128)S(1)} %shard_map.147.partial, s32[512,128]{1,0:T(8,128)S(1)} %collective-permute-done.2.other, s32[2,256,256]{2,1,0:T(8,128)S(1)} %copy-done, bf16[256,256]{1,0:T(8,128)(2,1)S(1)} %copy-done.5, bf16[256,256]{1,0:T(8,128)(2,1)S(1)} %copy-done.4, ...), custom_call_target="tpu_custom_call" | custom-call | flops 400000000 | bytes 2097152 | tf_op jit(solution)/shard_map/pallas_call | solution.py:314
  (9 shorter events, 0.0 us)
Async XLA Ops:
  0.0 5.0 %copy-start.1 = (f32[2,128,128]{2,1,0:T(8,128)S(1)}, f32[2,128,128]{2,1,0:T(8,128)}, u32[]{:S(2)}) copy-start(f32[2,128,128]{2,1,0:T(8,128)} %constant.49.clone.tw) | copy-start | bytes 393220
  0.0 5.0 %copy-start.7 = (bf16[2,256,256]{2,1,0:T(8,128)(2,1)S(1)}, bf16[2,256,256]{2,1,0:T(8,128)(2,1)}, u32[]{:S(2)}) copy-start(bf16[2,256,256]{2,1,0:T(8,128)(2,1)} %amp_own.1) | copy-start | bytes 786436
  0.0 5.0 %copy-start.6 = (bf16[2,256,256]{2,1,0:T(8,128)(2,1)S(1)}, bf16[2,256,256]{2,1,0:T(8,128)(2,1)}, u32[]{:S(2)}) copy-start(bf16[2,256,256]{2,1,0:T(8,128)(2,1)} %rho_ref.1) | copy-start | bytes 786436
  0.0 4.6 %collective-permute-start.1 = (bf16[2,256,256]{2,1,0:T(8,128)(2,1)}, bf16[2,256,256]{2,1,0:T(8,128)(2,1)S(1)}, u32[]{:S(2)}, u32[]{:S(2)}) collective-permute-start(bf16[2,256,256]{2,1,0:T(8,128)(2,1)} %amp_own.1), channel_id=1, source_target_pairs={{0,2},{2,0},{4,6},{6,4},{8,10},{10,8},{12,14},{14,12},{16,18},{18,... | collective-permute-start | bytes 786440 | tf_op jit(solution)/shard_map/ppermute | solution.py:342
  3.2 1.7 %collective-permute-start = (bf16[2,256,256]{2,1,0:T(8,128)(2,1)}, bf16[2,256,256]{2,1,0:T(8,128)(2,1)S(1)}, u32[]{:S(2)}, u32[]{:S(2)}) collective-permute-start(bf16[2,256,256]{2,1,0:T(8,128)(2,1)} %rho_ref.1), channel_id=1, source_target_pairs={{0,2},{2,0},{4,6},{6,4},{8,10},{10,8},{12,14},{14,12},{16,18},{18,... | collective-permute-start | bytes 786440 | tf_op jit(solution)/shard_map/ppermute | solution.py:341
  4.4 26.0 %copy-start.8 = (f32[2,2,128,128]{3,2,1,0:T(8,128)S(1)}, f32[2,2,128,128]{3,2,1,0:T(8,128)}, u32[]{:S(2)}) copy-start(f32[2,2,128,128]{3,2,1,0:T(8,128)} %constant.58.clone.tzw) | copy-start | bytes 786436
  4.5 26.0 %copy-start.9 = (bf16[2,256,256]{2,1,0:T(8,128)(2,1)S(1)}, bf16[2,256,256]{2,1,0:T(8,128)(2,1)}, u32[]{:S(2)}) copy-start(bf16[2,256,256]{2,1,0:T(8,128)(2,1)} %constant.57.clone.tzil) | copy-start | bytes 786436
  4.5 25.9 %copy-start.10 = (bf16[2,256,256]{2,1,0:T(8,128)(2,1)S(1)}, bf16[2,256,256]{2,1,0:T(8,128)(2,1)}, u32[]{:S(2)}) copy-start(bf16[2,256,256]{2,1,0:T(8,128)(2,1)} %constant.56.clone.tzih) | copy-start | bytes 786436
  4.5 25.9 %copy-start.11 = (bf16[2,256,256]{2,1,0:T(8,128)(2,1)S(1)}, bf16[2,256,256]{2,1,0:T(8,128)(2,1)}, u32[]{:S(2)}) copy-start(bf16[2,256,256]{2,1,0:T(8,128)(2,1)} %constant.55.clone.tzl) | copy-start | bytes 786436
  4.5 25.9 %copy-start.12 = (bf16[2,256,256]{2,1,0:T(8,128)(2,1)S(1)}, bf16[2,256,256]{2,1,0:T(8,128)(2,1)}, u32[]{:S(2)}) copy-start(bf16[2,256,256]{2,1,0:T(8,128)(2,1)} %constant.54.clone.tzh) | copy-start | bytes 786436
  4.5 25.9 %copy-start.13 = (bf16[256,256]{1,0:T(8,128)(2,1)S(1)}, bf16[256,256]{1,0:T(8,128)(2,1)}, u32[]{:S(2)}) copy-start(bf16[256,256]{1,0:T(8,128)(2,1)} %constant.53.clone.rev) | copy-start | bytes 393220
  30.4 19.9 %copy-start = (s32[2,256,256]{2,1,0:T(8,128)S(1)}, s32[2,256,256]{2,1,0:T(8,128)}, u32[]{:S(2)}) copy-start(s32[2,256,256]{2,1,0:T(8,128)} %support.3) | copy-start | bytes 1572868
  30.5 19.9 %copy-start.2 = (bf16[2,128,256]{2,1,0:T(8,128)(2,1)S(1)}, bf16[2,128,256]{2,1,0:T(8,128)(2,1)}, u32[]{:S(2)}) copy-start(bf16[2,128,256]{2,1,0:T(8,128)(2,1)} %constant.52.clone.txl) | copy-start | bytes 393220
  30.5 19.9 %copy-start.3 = (bf16[2,128,256]{2,1,0:T(8,128)(2,1)S(1)}, bf16[2,128,256]{2,1,0:T(8,128)(2,1)}, u32[]{:S(2)}) copy-start(bf16[2,128,256]{2,1,0:T(8,128)(2,1)} %constant.51.clone.txh) | copy-start | bytes 393220
  30.5 19.8 %copy-start.4 = (bf16[256,256]{1,0:T(8,128)(2,1)S(1)}, bf16[256,256]{1,0:T(8,128)(2,1)}, u32[]{:S(2)}) copy-start(bf16[256,256]{1,0:T(8,128)(2,1)} %constant.48.clone.tyl) | copy-start | bytes 393220
  30.5 19.8 %copy-start.5 = (bf16[256,256]{1,0:T(8,128)(2,1)S(1)}, bf16[256,256]{1,0:T(8,128)(2,1)}, u32[]{:S(2)}) copy-start(bf16[256,256]{1,0:T(8,128)(2,1)} %constant.47.clone.tyh) | copy-start | bytes 393220
  48.5 3.0 %collective-permute-start.2 = (s32[512,128]{1,0:T(8,128)S(1)}, s32[512,128]{1,0:T(8,128)S(1)}, u32[]{:S(2)}, u32[]{:S(2)}) collective-permute-start(s32[512,128]{1,0:T(8,128)S(1)} %bitcast.7), channel_id=1, source_target_pairs={{0,2},{2,0},{4,6},{6,4},{8,10},{10,8},{12,14},{14,12},{16,18},{18,... | collective-permute-start | bytes 786440 | tf_op jit(solution)/shard_map/ppermute | solution.py:361

commit v6 on v5

--- a/solution.py
+++ b/solution.py
@@ -245,7 +245,7 @@
                 out[pl.ds(2 * (2 * i + o) + r, CHIPS, stride=8), :] = words[o]
 
 
-def half_planes(ref, first, tyh, tyl, tw, txh, txl):
+def half_planes(ref, first, tyh, tyl, tw, txh, txl, scratch):
     low = lower(HALF)
     c, s = tw[0], tw[1]
     words = [
@@ -261,53 +261,34 @@
     out = []
     for q in range(2):
         re, im = u[:HALF, HALF * q : HALF * (q + 1)], u[HALF:, HALF * q : HALF * (q + 1)]
-        lines = jnp.concatenate(
-            [jnp.where(low, re, roll(im)), jnp.where(low, roll(re), im)], 0
-        )
-        lh, ll = cut(lines)
+        scratch[q, pl.ds(0, HALF, stride=2), :] = jnp.where(low, re, roll(im))
+        scratch[q, pl.ds(1, HALF, stride=2), :] = jnp.where(low, roll(re), im)
+        lh, ll = cut(scratch[q])
         out.append(
             mm(jnp.concatenate([lh, ll], 1), jnp.concatenate([txh, txh], 0)) + mm(lh, txl)
         )
     return out
 
 
-def interleave(rows, side, scratch):
-    for o in range(2):
-        scratch[pl.ds(o, HALF, stride=2), :] = rows[
-            HALF * o : HALF * (o + 1), HALF * side : HALF * (side + 1)
-        ]
-    return scratch[...]
-
-
 def own_kernel(core_ref, own, rho_ref, support, tyh, tyl, tw, txh, txl, out, scratch):
     core = core_ref[0]
-    for q, term in enumerate(half_planes(own, 0, tyh, tyl, tw, txh[core], txl[core])):
-        for side in range(2):
-            lanes = slice(HALF * side, HALF * (side + 1))
-            m = interleave(term, side, scratch.at[2 * q + side])
-            rho = rho_ref[q, :, lanes].astype(jnp.float32)
-            mask = support[q, :, lanes].astype(jnp.float32)
-            out[q, :, lanes] = rho + mask * (2.0 * m - rho) - m
-
-
-def update_kernel(core_ref, partial, other, support, tyh, tyl, tw, txh, txl, out, scratch, done, sems):
+    shares = half_planes(own, 0, tyh, tyl, tw, txh[core], txl[core], scratch)
+    for q, m in enumerate(shares):
+        rho = rho_ref[q].astype(jnp.float32)
+        mask = support[q].astype(jnp.float32)
+        out[q] = rho + mask * (2.0 * m - rho) - m
+
+
+def update_kernel(core_ref, partial, other, support, tyh, tyl, tw, txh, txl, out, scratch):
     core = 1 - core_ref[0]
-    copies = []
-    for q, term in enumerate(half_planes(other, 2, tyh, tyl, tw, txh[core], txl[core])):
-        for side in range(2):
-            lanes = slice(HALF * side, HALF * (side + 1))
-            m = interleave(term, side, scratch.at[2 * q + side])
-            mask = support[q, :, lanes].astype(jnp.float32)
-            done[q, :, lanes] = (partial[q, :, lanes] + (2.0 * mask - 1.0) * m).astype(jnp.bfloat16)
-        copies.append(pltpu.make_async_copy(done.at[q], out.at[q], sems.at[q]))
-        copies[q].start()
-    for copy in copies:
-        copy.wait()
+    shares = half_planes(other, 2, tyh, tyl, tw, txh[core], txl[core], scratch)
+    for q, m in enumerate(shares):
+        mask = support[q].astype(jnp.float32)
+        out[q] = (partial[q] + (2.0 * mask - 1.0) * m).astype(jnp.bfloat16)
 
 
 SMEM = pl.BlockSpec(memory_space=pltpu.SMEM)
 VMEM = pl.BlockSpec(memory_space=pltpu.VMEM)
-HBM = pl.BlockSpec(memory_space=pltpu.HBM)
 
 
 def call(kernel, out_shape, operands, in_specs, flops, out_specs=VMEM, **more):
@@ -366,7 +347,7 @@
         (core, planes, density, support, *tables),
         [SMEM] + [VMEM] * 8,
         400e6,
-        scratch_shapes=[pltpu.VMEM((4, N, HALF), jnp.float32)],
+        scratch_shapes=[pltpu.VMEM((2, N, HALF), jnp.float32)],
     )
     return call(
         update_kernel,
@@ -374,12 +355,7 @@
         (core, partial, planes_other, support, *tables),
         [SMEM] + [VMEM] * 8,
         400e6,
-        out_specs=HBM,
-        scratch_shapes=[
-            pltpu.VMEM((4, N, HALF), jnp.float32),
-            pltpu.VMEM(density.shape, jnp.bfloat16),
-            pltpu.SemaphoreType.DMA((2,)),
-        ],
+        scratch_shapes=[pltpu.VMEM((2, N, HALF), jnp.float32)],
     )
 
 

time: 53.3 us -> 53.3 us (level)
  no operation moved by 1% of the time
where the time goes in v6:
time: 53.3 us; the launch traced here: 53.1 us
  blocking collectives  41 us (77%)
  starting transfers between devices  5.12 us (10%)
  Pallas kernels  4.95 us (9%)
  local copies, waits for them, and re-layouts  1.19 us (2%)
  waiting for transfers between devices  0.66 us (1%)
    all_to_all x2, blocking collectives, exchange(): lax.all_to_all(x, 'slab', split_axis=0, concat_axis=0, tiled=True, axis_i...  41 us
    pallas_call x4, Pallas kernels, call(): pl.pallas_call(kernel, out_shape=out_shape, in_specs=in_specs, out_specs=...  4.95 us
    ppermute x1, starting transfers between devices, shards(): amplitudes_other = lax.ppermute(amplitudes, 'slab', swap)  3.24 us
    ppermute x1, starting transfers between devices, shards(): planes_other = lax.ppermute(planes, 'slab', swap)  1.79 us
    squeeze x1, local copies, waits for them, and re-layouts, shards(): table = lax.dynamic_index_in_dim(c['first'], core[0], 0, keepdims=False)  1.1 us
  transfers between devices with their start and end apart: 3, of which 3 were waited for; matrix products, arithmetic and copies ran while one was open for 2% of the time, Pallas kernels for 2%

profile of v6, /device:TPU:1, one launch (start us, length us, event | category | flops | bytes accessed | tf_op | source)
XLA Modules:
  0.0 53.1 jit_solution(2211986602330921196)
XLA Ops:
  0.0 3.2 %collective-permute-start.1 = (bf16[2,256,256]{2,1,0:T(8,128)(2,1)}, bf16[2,256,256]{2,1,0:T(8,128)(2,1)S(1)}, u32[]{:S(2)}, u32[]{:S(2)}) collective-permute-start(bf16[2,256,256]{2,1,0:T(8,128)(2,1)} %amp_own.1), channel_id=1, source_target_pairs={{0,2},{2,0},{4,6},{6,4},{8,10},{10,8},{12,14},{14,12},{16,18},{18,... | collective-permute-start | bytes 786440 | tf_op jit(solution)/shard_map/ppermute | solution.py:323
  3.2 0.1 collective-permute-start
  3.3 1.1 %dynamic-slice_bitcast_fusion.table = bf16[1152,256]{1,0:T(8,128)(2,1)S(1)} fusion(bf16[2,1152,256]{2,1,0:T(8,128)(2,1)} %constant.50.clone, s32[]{:T(128)S(6)} %select_n.12), kind=kLoop, calls=%fused_computation | loop fusion | bytes 1179652 | tf_op jit(solution)/shard_map/jit(dynamic_index_in_dim)/squeeze | solution.py:324
  4.4 0.0 copy-start.8
  4.5 0.0 copy-start.9
  4.5 0.0 copy-start.10
  4.5 0.0 copy-start.11
  4.5 0.0 copy-start.12
  4.5 0.0 copy-start.13
  4.5 0.1 collective-permute-done.1.amp_other
  4.6 0.4 collective-permute-done.rho_other
  5.0 0.0 copy-done.1
  5.0 0.0 copy-done.7
  5.0 0.0 copy-done.6
  5.0 1.2 %shard_map.145 = s32[1024,128]{1,0:T(8,128)S(1)} custom-call(bf16[2,256,256]{2,1,0:T(8,128)(2,1)S(1)} %copy-done.6, bf16[2,256,256]{2,1,0:T(8,128)(2,1)S(1)} %copy-done.7, bf16[2,256,256]{2,1,0:T(8,128)(2,1)S(1)} %collective-permute-done.rho_other, bf16[2,256,256]{2,1,0:T(8,128)(2,1)S(1)} %collective-permute-done.1.amp_other, ...), custom_call_target="tpu_custom_call" | custom-call | flops 800000000 | bytes 2097152 | tf_op jit(solution)/shard_map/pallas_call | solution.py:295
  6.2 24.2 %all_to_all.10 = s32[64,16,128]{2,1,0:T(8,128)S(1)} all-to-all(s32[64,16,128]{2,1,0:T(8,128)S(1)} %bitcast.10), channel_id=1, replica_groups={{176,180,184,188,160,164,168,172,144,148,152,156,128,132,136,140,240,24..., dimensions={0} | all-to-all | bytes 1048576 | tf_op jit(solution)/shard_map/all_to_all | solution.py:315
  30.4 0.0 copy-done.8
  30.4 0.0 copy-done.10
  30.4 0.0 copy-done.11
  30.4 0.0 copy-done.12
  30.4 0.0 copy-done.13
  30.4 0.0 copy-start
  30.5 0.0 copy-start.2
  30.5 0.0 copy-start.3
  30.5 0.0 copy-start.4
  30.5 0.0 copy-start.5
  30.5 1.2 %shard_map.146 = s32[512,128]{1,0:T(8,128)S(1)} custom-call(s32[1]{0:T(128)} %bitcast.core_ref, s32[1024,128]{1,0:T(8,128)S(1)} %bitcast.9, bf16[2,256,256]{2,1,0:T(8,128)(2,1)S(1)} %copy-done.12, bf16[2,256,256]{2,1,0:T(8,128)(2,1)S(1)} %copy-done.11, bf16[2,256,256]{2,1,0:T(8,128)(2,1)S(1)} %copy-done.10, bf16[2,256,256]{2,1,0:T(8,128)(2,1)S(1)} %copy-done.9, ...), custom_call_target="tpu_custom_call" | custom-call | flops 800000000 | bytes 2097152 | tf_op jit(solution)/shard_map/pallas_call | solution.py:295
  31.7 16.8 %all_to_all.11 = s32[64,8,128]{2,1,0:T(8,128)S(1)} all-to-all(s32[64,8,128]{2,1,0:T(8,128)S(1)} %bitcast.11), channel_id=1, replica_groups={{176,180,184,188,160,164,168,172,144,148,152,156,128,132,136,140,240,24..., dimensions={0} | all-to-all | bytes 524288 | tf_op jit(solution)/shard_map/all_to_all | solution.py:315
  48.5 1.8 %collective-permute-start.2 = (s32[512,128]{1,0:T(8,128)S(1)}, s32[512,128]{1,0:T(8,128)S(1)}, u32[]{:S(2)}, u32[]{:S(2)}) collective-permute-start(s32[512,128]{1,0:T(8,128)S(1)} %bitcast.7), channel_id=1, source_target_pairs={{0,2},{2,0},{4,6},{6,4},{8,10},{10,8},{12,14},{14,12},{16,18},{18,... | collective-permute-start | bytes 786440 | tf_op jit(solution)/shard_map/ppermute | solution.py:342
  50.3 0.9 %shard_map.147.partial = f32[2,256,256]{2,1,0:T(8,128)S(1)} custom-call(s32[1]{0:T(128)} %bitcast.core_ref, s32[512,128]{1,0:T(8,128)S(1)} %bitcast.8, bf16[2,256,256]{2,1,0:T(8,128)(2,1)S(1)} %copy-done.6, s32[2,256,256]{2,1,0:T(8,128)S(1)} %copy-done, bf16[256,256]{1,0:T(8,128)(2,1)S(1)} %copy-done.5, bf16[256,256]{1,0:T(8,128)(2,1)S(1)} %copy-done.4, ...), custom_call_target="tpu_custom_call" | custom-call | flops 400000000 | bytes 2097152 | tf_op jit(solution)/shard_map/pallas_call | solution.py:295
  51.3 0.2 collective-permute-done.2.other
  51.5 1.6 %shard_map.148 = bf16[2,256,256]{2,1,0:T(8,128)(2,1)} custom-call(s32[1]{0:T(128)} %bitcast.core_ref, f32[2,256,256]{2,1,0:T(8,128)S(1)} %shard_map.147.partial, s32[512,128]{1,0:T(8,128)S(1)} %collective-permute-done.2.other, s32[2,256,256]{2,1,0:T(8,128)S(1)} %copy-done, bf16[256,256]{1,0:T(8,128)(2,1)S(1)} %copy-done.5, bf16[256,256]{1,0:T(8,128)(2,1)S(1)} %copy-done.4, ...), custom_call_target="tpu_custom_call" | custom-call | flops 400000000 | bytes 2097152 | tf_op jit(solution)/shard_map/pallas_call | solution.py:295
  (9 shorter events, 0.0 us)
Async XLA Ops:
  0.0 5.0 %copy-start.1 = (f32[2,128,128]{2,1,0:T(8,128)S(1)}, f32[2,128,128]{2,1,0:T(8,128)}, u32[]{:S(2)}) copy-start(f32[2,128,128]{2,1,0:T(8,128)} %constant.49.clone.tw) | copy-start | bytes 393220
  0.0 5.0 %copy-start.7 = (bf16[2,256,256]{2,1,0:T(8,128)(2,1)S(1)}, bf16[2,256,256]{2,1,0:T(8,128)(2,1)}, u32[]{:S(2)}) copy-start(bf16[2,256,256]{2,1,0:T(8,128)(2,1)} %amp_own.1) | copy-start | bytes 786436
  0.0 5.0 %copy-start.6 = (bf16[2,256,256]{2,1,0:T(8,128)(2,1)S(1)}, bf16[2,256,256]{2,1,0:T(8,128)(2,1)}, u32[]{:S(2)}) copy-start(bf16[2,256,256]{2,1,0:T(8,128)(2,1)} %rho_ref.1) | copy-start | bytes 786436
  0.0 4.6 %collective-permute-start.1 = (bf16[2,256,256]{2,1,0:T(8,128)(2,1)}, bf16[2,256,256]{2,1,0:T(8,128)(2,1)S(1)}, u32[]{:S(2)}, u32[]{:S(2)}) collective-permute-start(bf16[2,256,256]{2,1,0:T(8,128)(2,1)} %amp_own.1), channel_id=1, source_target_pairs={{0,2},{2,0},{4,6},{6,4},{8,10},{10,8},{12,14},{14,12},{16,18},{18,... | collective-permute-start | bytes 786440 | tf_op jit(solution)/shard_map/ppermute | solution.py:323
  3.2 1.7 %collective-permute-start = (bf16[2,256,256]{2,1,0:T(8,128)(2,1)}, bf16[2,256,256]{2,1,0:T(8,128)(2,1)S(1)}, u32[]{:S(2)}, u32[]{:S(2)}) collective-permute-start(bf16[2,256,256]{2,1,0:T(8,128)(2,1)} %rho_ref.1), channel_id=1, source_target_pairs={{0,2},{2,0},{4,6},{6,4},{8,10},{10,8},{12,14},{14,12},{16,18},{18,... | collective-permute-start | bytes 786440 | tf_op jit(solution)/shard_map/ppermute | solution.py:322
  4.4 26.0 %copy-start.8 = (f32[2,2,128,128]{3,2,1,0:T(8,128)S(1)}, f32[2,2,128,128]{3,2,1,0:T(8,128)}, u32[]{:S(2)}) copy-start(f32[2,2,128,128]{3,2,1,0:T(8,128)} %constant.58.clone.tzw) | copy-start | bytes 786436
  4.5 26.0 %copy-start.9 = (bf16[2,256,256]{2,1,0:T(8,128)(2,1)S(1)}, bf16[2,256,256]{2,1,0:T(8,128)(2,1)}, u32[]{:S(2)}) copy-start(bf16[2,256,256]{2,1,0:T(8,128)(2,1)} %constant.57.clone.tzil) | copy-start | bytes 786436
  4.5 25.9 %copy-start.10 = (bf16[2,256,256]{2,1,0:T(8,128)(2,1)S(1)}, bf16[2,256,256]{2,1,0:T(8,128)(2,1)}, u32[]{:S(2)}) copy-start(bf16[2,256,256]{2,1,0:T(8,128)(2,1)} %constant.56.clone.tzih) | copy-start | bytes 786436
  4.5 25.9 %copy-start.11 = (bf16[2,256,256]{2,1,0:T(8,128)(2,1)S(1)}, bf16[2,256,256]{2,1,0:T(8,128)(2,1)}, u32[]{:S(2)}) copy-start(bf16[2,256,256]{2,1,0:T(8,128)(2,1)} %constant.55.clone.tzl) | copy-start | bytes 786436
  4.5 25.9 %copy-start.12 = (bf16[2,256,256]{2,1,0:T(8,128)(2,1)S(1)}, bf16[2,256,256]{2,1,0:T(8,128)(2,1)}, u32[]{:S(2)}) copy-start(bf16[2,256,256]{2,1,0:T(8,128)(2,1)} %constant.54.clone.tzh) | copy-start | bytes 786436
  4.5 25.9 %copy-start.13 = (bf16[256,256]{1,0:T(8,128)(2,1)S(1)}, bf16[256,256]{1,0:T(8,128)(2,1)}, u32[]{:S(2)}) copy-start(bf16[256,256]{1,0:T(8,128)(2,1)} %constant.53.clone.rev) | copy-start | bytes 393220
  30.4 19.9 %copy-start = (s32[2,256,256]{2,1,0:T(8,128)S(1)}, s32[2,256,256]{2,1,0:T(8,128)}, u32[]{:S(2)}) copy-start(s32[2,256,256]{2,1,0:T(8,128)} %support.3) | copy-start | bytes 1572868
  30.5 19.9 %copy-start.2 = (bf16[2,128,256]{2,1,0:T(8,128)(2,1)S(1)}, bf16[2,128,256]{2,1,0:T(8,128)(2,1)}, u32[]{:S(2)}) copy-start(bf16[2,128,256]{2,1,0:T(8,128)(2,1)} %constant.52.clone.txl) | copy-start | bytes 393220
  30.5 19.9 %copy-start.3 = (bf16[2,128,256]{2,1,0:T(8,128)(2,1)S(1)}, bf16[2,128,256]{2,1,0:T(8,128)(2,1)}, u32[]{:S(2)}) copy-start(bf16[2,128,256]{2,1,0:T(8,128)(2,1)} %constant.51.clone.txh) | copy-start | bytes 393220
  30.5 19.8 %copy-start.4 = (bf16[256,256]{1,0:T(8,128)(2,1)S(1)}, bf16[256,256]{1,0:T(8,128)(2,1)}, u32[]{:S(2)}) copy-start(bf16[256,256]{1,0:T(8,128)(2,1)} %constant.48.clone.tyl) | copy-start | bytes 393220
  30.5 19.8 %copy-start.5 = (bf16[256,256]{1,0:T(8,128)(2,1)S(1)}, bf16[256,256]{1,0:T(8,128)(2,1)}, u32[]{:S(2)}) copy-start(bf16[256,256]{1,0:T(8,128)(2,1)} %constant.47.clone.tyh) | copy-start | bytes 393220
  48.5 3.0 %collective-permute-start.2 = (s32[512,128]{1,0:T(8,128)S(1)}, s32[512,128]{1,0:T(8,128)S(1)}, u32[]{:S(2)}, u32[]{:S(2)}) collective-permute-start(s32[512,128]{1,0:T(8,128)S(1)} %bitcast.7), channel_id=1, source_target_pairs={{0,2},{2,0},{4,6},{6,4},{8,10},{10,8},{12,14},{14,12},{16,18},{18,... | collective-permute-start | bytes 786440 | tf_op jit(solution)/shard_map/ppermute | solution.py:342

commit v7 on v6

--- a/solution.py
+++ b/solution.py
@@ -245,12 +245,17 @@
                 out[pl.ds(2 * (2 * i + o) + r, CHIPS, stride=8), :] = words[o]
 
 
-def half_planes(ref, first, tyh, tyl, tw, txh, txl, scratch):
+def give_kernel(planes, out):
+    for slot in range(4):
+        out[pl.ds(slot, CHIPS, stride=4), :] = planes[pl.ds(4 + slot, CHIPS, stride=8), :]
+
+
+def half_planes(ref, stride, tyh, tyl, tw, txh, txl, scratch):
     low = lower(HALF)
     c, s = tw[0], tw[1]
     words = [
-        jnp.concatenate([ref[pl.ds(2 * p + r, CHIPS, stride=8), :] for r in range(2)], 0)
-        for p in (first, first + 1)
+        jnp.concatenate([ref[pl.ds(2 * p + r, CHIPS, stride=stride), :] for r in range(2)], 0)
+        for p in range(2)
     ]
     parts = unpack(*words, INVERSE_LOW)
     stack = []
@@ -272,7 +277,7 @@
 
 def own_kernel(core_ref, own, rho_ref, support, tyh, tyl, tw, txh, txl, out, scratch):
     core = core_ref[0]
-    shares = half_planes(own, 0, tyh, tyl, tw, txh[core], txl[core], scratch)
+    shares = half_planes(own, 8, tyh, tyl, tw, txh[core], txl[core], scratch)
     for q, m in enumerate(shares):
         rho = rho_ref[q].astype(jnp.float32)
         mask = support[q].astype(jnp.float32)
@@ -281,7 +286,7 @@
 
 def update_kernel(core_ref, partial, other, support, tyh, tyl, tw, txh, txl, out, scratch):
     core = 1 - core_ref[0]
-    shares = half_planes(other, 2, tyh, tyl, tw, txh[core], txl[core], scratch)
+    shares = half_planes(other, 4, tyh, tyl, tw, txh[core], txl[core], scratch)
     for q, m in enumerate(shares):
         mask = support[q].astype(jnp.float32)
         out[q] = (partial[q] + (2.0 * mask - 1.0) * m).astype(jnp.bfloat16)
@@ -339,7 +344,8 @@
         800e6,
     )
     planes = exchange(sent.reshape(CHIPS, 8, HALF)).reshape(CHIPS * 8, HALF)
-    planes_other = lax.ppermute(planes, "slab", swap)
+    given = call(give_kernel, shape((CHIPS * 4, HALF), jnp.int32), (planes,), [VMEM], 1e5)
+    planes_other = lax.ppermute(given, "slab", swap)
     tables = (*c["tyi"], c["tw"], *c["txi"])
     partial = call(
         own_kernel,

time: 53.3 us -> 53.4 us (level)
    pallas_call x4 -> x5, Pallas kernels: 4.95 us -> 4.99 us  [call(): pl.pallas_call(kernel, out_shape=out_shape, in_specs=in_specs, out_specs=...]
  transfers between devices with their start and end apart: 3 -> 3, of which waited for: 3 -> 2; matrix products, arithmetic and copies ran while one was open for 2% -> 2% of each run, Pallas kernels for 2% -> 2%
where the time goes in v7:
time: 53.4 us; the launch traced here: 53.2 us
  blocking collectives  41.1 us (77%)
  starting transfers between devices  5.21 us (10%)
  Pallas kernels  4.99 us (9%)
  local copies, waits for them, and re-layouts  1.19 us (2%)
    all_to_all x2, blocking collectives, exchange(): lax.all_to_all(x, 'slab', split_axis=0, concat_axis=0, tiled=True, axis_i...  41.1 us
    pallas_call x5, Pallas kernels, call(): pl.pallas_call(kernel, out_shape=out_shape, in_specs=in_specs, out_specs=...  4.99 us
    ppermute x1, starting transfers between devices, shards(): amplitudes_other = lax.ppermute(amplitudes, 'slab', swap)  3.24 us
    ppermute x1, starting transfers between devices, shards(): planes_other = lax.ppermute(given, 'slab', swap)  1.88 us
    squeeze x1, local copies, waits for them, and re-layouts, shards(): table = lax.dynamic_index_in_dim(c['first'], core[0], 0, keepdims=False)  1.1 us
  transfers between devices with their start and end apart: 3, of which 2 were waited for; matrix products, arithmetic and copies ran while one was open for 2% of the time, Pallas kernels for 2%

profile of v7, /device:TPU:1, one launch (start us, length us, event | category | flops | bytes accessed | tf_op | source)
XLA Modules:
  0.0 53.2 jit_solution(5525916296489155313)
XLA Ops:
  0.0 3.2 %collective-permute-start.1 = (bf16[2,256,256]{2,1,0:T(8,128)(2,1)}, bf16[2,256,256]{2,1,0:T(8,128)(2,1)S(1)}, u32[]{:S(2)}, u32[]{:S(2)}) collective-permute-start(bf16[2,256,256]{2,1,0:T(8,128)(2,1)} %amp_own.1), channel_id=1, source_target_pairs={{0,2},{2,0},{4,6},{6,4},{8,10},{10,8},{12,14},{14,12},{16,18},{18,... | collective-permute-start | bytes 786440 | tf_op jit(solution)/shard_map/ppermute | solution.py:328
  3.2 0.1 collective-permute-start
  3.3 1.1 %dynamic-slice_bitcast_fusion.table = bf16[1152,256]{1,0:T(8,128)(2,1)S(1)} fusion(bf16[2,1152,256]{2,1,0:T(8,128)(2,1)} %constant.50.clone, s32[]{:T(128)S(6)} %select_n.12), kind=kLoop, calls=%fused_computation | loop fusion | bytes 1179652 | tf_op jit(solution)/shard_map/jit(dynamic_index_in_dim)/squeeze | solution.py:329
  4.4 0.0 copy-start.8
  4.5 0.0 copy-start.9
  4.5 0.0 copy-start.10
  4.5 0.0 copy-start.11
  4.5 0.0 copy-start.12
  4.5 0.0 copy-start.13
  4.5 0.1 collective-permute-done.1.amp_other
  4.6 0.4 collective-permute-done.rho_other
  5.0 0.0 copy-done.1
  5.0 0.0 copy-done.7
  5.0 0.0 copy-done.6
  5.0 1.2 %shard_map.145 = s32[1024,128]{1,0:T(8,128)S(1)} custom-call(bf16[2,256,256]{2,1,0:T(8,128)(2,1)S(1)} %copy-done.6, bf16[2,256,256]{2,1,0:T(8,128)(2,1)S(1)} %copy-done.7, bf16[2,256,256]{2,1,0:T(8,128)(2,1)S(1)} %collective-permute-done.rho_other, bf16[2,256,256]{2,1,0:T(8,128)(2,1)S(1)} %collective-permute-done.1.amp_other, ...), custom_call_target="tpu_custom_call" | custom-call | flops 800000000 | bytes 2097152 | tf_op jit(solution)/shard_map/pallas_call | solution.py:300
  6.2 24.2 %all_to_all.10 = s32[64,16,128]{2,1,0:T(8,128)S(1)} all-to-all(s32[64,16,128]{2,1,0:T(8,128)S(1)} %bitcast.10), channel_id=1, replica_groups={{176,180,184,188,160,164,168,172,144,148,152,156,128,132,136,140,240,24..., dimensions={0} | all-to-all | bytes 1048576 | tf_op jit(solution)/shard_map/all_to_all | solution.py:320
  30.4 0.0 copy-done.8
  30.4 0.0 copy-done.9
  30.4 0.0 copy-done.10
  30.4 0.0 copy-start.2
  30.5 0.0 copy-start.3
  30.5 0.0 copy-start.4
  30.5 0.0 copy-start.5
  30.5 1.2 %shard_map.146 = s32[512,128]{1,0:T(8,128)S(1)} custom-call(s32[1]{0:T(128)} %bitcast.core_ref, s32[1024,128]{1,0:T(8,128)S(1)} %bitcast.9, bf16[2,256,256]{2,1,0:T(8,128)(2,1)S(1)} %copy-done.12, bf16[2,256,256]{2,1,0:T(8,128)(2,1)S(1)} %copy-done.11, bf16[2,256,256]{2,1,0:T(8,128)(2,1)S(1)} %copy-done.10, bf16[2,256,256]{2,1,0:T(8,128)(2,1)S(1)} %copy-done.9, ...), custom_call_target="tpu_custom_call" | custom-call | flops 800000000 | bytes 2097152 | tf_op jit(solution)/shard_map/pallas_call | solution.py:300
  31.7 0.0 copy-start
  31.7 16.9 %all_to_all.11 = s32[64,8,128]{2,1,0:T(8,128)S(1)} all-to-all(s32[64,8,128]{2,1,0:T(8,128)S(1)} %bitcast.11), channel_id=1, replica_groups={{176,180,184,188,160,164,168,172,144,148,152,156,128,132,136,140,240,24..., dimensions={0} | all-to-all | bytes 524288 | tf_op jit(solution)/shard_map/all_to_all | solution.py:320
  48.7 1.9 %collective-permute-start.2 = (s32[256,128]{1,0:T(8,128)S(1)}, s32[256,128]{1,0:T(8,128)S(1)}, u32[]{:S(2)}, u32[]{:S(2)}) collective-permute-start(s32[256,128]{1,0:T(8,128)S(1)} %shard_map.148), channel_id=1, source_target_pairs={{0,2},{2,0},{4,6},{6,4},{8,10},{10,8},{12,14},{14,12},{16,18},{18,... | collective-permute-start | bytes 393224 | tf_op jit(solution)/shard_map/ppermute | solution.py:348
  50.6 0.0 copy-done.5
  50.6 0.0 copy-done
  50.6 0.9 %shard_map.147.partial = f32[2,256,256]{2,1,0:T(8,128)S(1)} custom-call(s32[1]{0:T(128)} %bitcast.core_ref, s32[512,128]{1,0:T(8,128)S(1)} %bitcast.8, bf16[2,256,256]{2,1,0:T(8,128)(2,1)S(1)} %copy-done.6, s32[2,256,256]{2,1,0:T(8,128)S(1)} %copy-done, bf16[256,256]{1,0:T(8,128)(2,1)S(1)} %copy-done.5, bf16[256,256]{1,0:T(8,128)(2,1)S(1)} %copy-done.4, ...), custom_call_target="tpu_custom_call" | custom-call | flops 400000000 | bytes 2097152 | tf_op jit(solution)/shard_map/pallas_call | solution.py:300
  51.5 0.0 collective-permute-done.2.other
  51.6 1.6 %shard_map.149 = bf16[2,256,256]{2,1,0:T(8,128)(2,1)} custom-call(s32[1]{0:T(128)} %bitcast.core_ref, f32[2,256,256]{2,1,0:T(8,128)S(1)} %shard_map.147.partial, s32[256,128]{1,0:T(8,128)S(1)} %collective-permute-done.2.other, s32[2,256,256]{2,1,0:T(8,128)S(1)} %copy-done, bf16[256,256]{1,0:T(8,128)(2,1)S(1)} %copy-done.5, bf16[256,256]{1,0:T(8,128)(2,1)S(1)} %copy-done.4, ...), custom_call_target="tpu_custom_call" | custom-call | flops 400000000 | bytes 2097152 | tf_op jit(solution)/shard_map/pallas_call | solution.py:300
  (10 shorter events, 0.0 us)
Async XLA Ops:
  0.0 5.0 %copy-start.1 = (f32[2,128,128]{2,1,0:T(8,128)S(1)}, f32[2,128,128]{2,1,0:T(8,128)}, u32[]{:S(2)}) copy-start(f32[2,128,128]{2,1,0:T(8,128)} %constant.49.clone.tw) | copy-start | bytes 393220
  0.0 5.0 %copy-start.7 = (bf16[2,256,256]{2,1,0:T(8,128)(2,1)S(1)}, bf16[2,256,256]{2,1,0:T(8,128)(2,1)}, u32[]{:S(2)}) copy-start(bf16[2,256,256]{2,1,0:T(8,128)(2,1)} %amp_own.1) | copy-start | bytes 786436
  0.0 5.0 %copy-start.6 = (bf16[2,256,256]{2,1,0:T(8,128)(2,1)S(1)}, bf16[2,256,256]{2,1,0:T(8,128)(2,1)}, u32[]{:S(2)}) copy-start(bf16[2,256,256]{2,1,0:T(8,128)(2,1)} %rho_ref.1) | copy-start | bytes 786436
  0.0 4.6 %collective-permute-start.1 = (bf16[2,256,256]{2,1,0:T(8,128)(2,1)}, bf16[2,256,256]{2,1,0:T(8,128)(2,1)S(1)}, u32[]{:S(2)}, u32[]{:S(2)}) collective-permute-start(bf16[2,256,256]{2,1,0:T(8,128)(2,1)} %amp_own.1), channel_id=1, source_target_pairs={{0,2},{2,0},{4,6},{6,4},{8,10},{10,8},{12,14},{14,12},{16,18},{18,... | collective-permute-start | bytes 786440 | tf_op jit(solution)/shard_map/ppermute | solution.py:328
  3.2 1.7 %collective-permute-start = (bf16[2,256,256]{2,1,0:T(8,128)(2,1)}, bf16[2,256,256]{2,1,0:T(8,128)(2,1)S(1)}, u32[]{:S(2)}, u32[]{:S(2)}) collective-permute-start(bf16[2,256,256]{2,1,0:T(8,128)(2,1)} %rho_ref.1), channel_id=1, source_target_pairs={{0,2},{2,0},{4,6},{6,4},{8,10},{10,8},{12,14},{14,12},{16,18},{18,... | collective-permute-start | bytes 786440 | tf_op jit(solution)/shard_map/ppermute | solution.py:327
  4.4 26.0 %copy-start.8 = (f32[2,2,128,128]{3,2,1,0:T(8,128)S(1)}, f32[2,2,128,128]{3,2,1,0:T(8,128)}, u32[]{:S(2)}) copy-start(f32[2,2,128,128]{3,2,1,0:T(8,128)} %constant.58.clone.tzw) | copy-start | bytes 786436
  4.5 26.0 %copy-start.9 = (bf16[2,256,256]{2,1,0:T(8,128)(2,1)S(1)}, bf16[2,256,256]{2,1,0:T(8,128)(2,1)}, u32[]{:S(2)}) copy-start(bf16[2,256,256]{2,1,0:T(8,128)(2,1)} %constant.57.clone.tzil) | copy-start | bytes 786436
  4.5 25.9 %copy-start.10 = (bf16[2,256,256]{2,1,0:T(8,128)(2,1)S(1)}, bf16[2,256,256]{2,1,0:T(8,128)(2,1)}, u32[]{:S(2)}) copy-start(bf16[2,256,256]{2,1,0:T(8,128)(2,1)} %constant.56.clone.tzih) | copy-start | bytes 786436
  4.5 25.9 %copy-start.11 = (bf16[2,256,256]{2,1,0:T(8,128)(2,1)S(1)}, bf16[2,256,256]{2,1,0:T(8,128)(2,1)}, u32[]{:S(2)}) copy-start(bf16[2,256,256]{2,1,0:T(8,128)(2,1)} %constant.55.clone.tzl) | copy-start | bytes 786436
  4.5 25.9 %copy-start.12 = (bf16[2,256,256]{2,1,0:T(8,128)(2,1)S(1)}, bf16[2,256,256]{2,1,0:T(8,128)(2,1)}, u32[]{:S(2)}) copy-start(bf16[2,256,256]{2,1,0:T(8,128)(2,1)} %constant.54.clone.tzh) | copy-start | bytes 786436
  4.5 25.9 %copy-start.13 = (bf16[256,256]{1,0:T(8,128)(2,1)S(1)}, bf16[256,256]{1,0:T(8,128)(2,1)}, u32[]{:S(2)}) copy-start(bf16[256,256]{1,0:T(8,128)(2,1)} %constant.53.clone.rev) | copy-start | bytes 393220
  30.4 20.1 %copy-start.2 = (bf16[2,128,256]{2,1,0:T(8,128)(2,1)S(1)}, bf16[2,128,256]{2,1,0:T(8,128)(2,1)}, u32[]{:S(2)}) copy-start(bf16[2,128,256]{2,1,0:T(8,128)(2,1)} %constant.52.clone.txl) | copy-start | bytes 393220
  30.5 20.1 %copy-start.3 = (bf16[2,128,256]{2,1,0:T(8,128)(2,1)S(1)}, bf16[2,128,256]{2,1,0:T(8,128)(2,1)}, u32[]{:S(2)}) copy-start(bf16[2,128,256]{2,1,0:T(8,128)(2,1)} %constant.51.clone.txh) | copy-start | bytes 393220
  30.5 20.1 %copy-start.4 = (bf16[256,256]{1,0:T(8,128)(2,1)S(1)}, bf16[256,256]{1,0:T(8,128)(2,1)}, u32[]{:S(2)}) copy-start(bf16[256,256]{1,0:T(8,128)(2,1)} %constant.48.clone.tyl) | copy-start | bytes 393220
  30.5 20.1 %copy-start.5 = (bf16[256,256]{1,0:T(8,128)(2,1)S(1)}, bf16[256,256]{1,0:T(8,128)(2,1)}, u32[]{:S(2)}) copy-start(bf16[256,256]{1,0:T(8,128)(2,1)} %constant.47.clone.tyh) | copy-start | bytes 393220
  31.7 18.8 %copy-start = (s32[2,256,256]{2,1,0:T(8,128)S(1)}, s32[2,256,256]{2,1,0:T(8,128)}, u32[]{:S(2)}) copy-start(s32[2,256,256]{2,1,0:T(8,128)} %support.3) | copy-start | bytes 1572868
  48.7 2.9 %collective-permute-start.2 = (s32[256,128]{1,0:T(8,128)S(1)}, s32[256,128]{1,0:T(8,128)S(1)}, u32[]{:S(2)}, u32[]{:S(2)}) collective-permute-start(s32[256,128]{1,0:T(8,128)S(1)} %shard_map.148), channel_id=1, source_target_pairs={{0,2},{2,0},{4,6},{6,4},{8,10},{10,8},{12,14},{14,12},{16,18},{18,... | collective-permute-start | bytes 393224 | tf_op jit(solution)/shard_map/ppermute | solution.py:348

commit v8 on v5

--- a/solution.py
+++ b/solution.py
@@ -266,7 +266,7 @@
         )
         lh, ll = cut(lines)
         out.append(
-            mm(jnp.concatenate([lh, ll], 1), jnp.concatenate([txh, txh], 0)) + mm(lh, txl)
+            mm(jnp.concatenate([lh, ll, lh], 1), jnp.concatenate([txh, txh, txl], 0))
         )
     return out
 

time: 53.3 us -> 53.3 us (level)
  no operation moved by 1% of the time
where the time goes in v8:
time: 53.3 us; the launch traced here: 53.1 us
  blocking collectives  41 us (77%)
  starting transfers between devices  5.12 us (10%)
  Pallas kernels  4.89 us (9%)
  local copies, waits for them, and re-layouts  1.19 us (2%)
  waiting for transfers between devices  0.68 us (1%)
    all_to_all x2, blocking collectives, exchange(): lax.all_to_all(x, 'slab', split_axis=0, concat_axis=0, tiled=True, axis_i...  41 us
    pallas_call x4, Pallas kernels, call(): pl.pallas_call(kernel, out_shape=out_shape, in_specs=in_specs, out_specs=...  4.89 us
    ppermute x1, starting transfers between devices, shards(): amplitudes_other = lax.ppermute(amplitudes, 'slab', swap)  3.24 us
    ppermute x1, starting transfers between devices, shards(): planes_other = lax.ppermute(planes, 'slab', swap)  1.79 us
    squeeze x1, local copies, waits for them, and re-layouts, shards(): table = lax.dynamic_index_in_dim(c['first'], core[0], 0, keepdims=False)  1.1 us
  transfers between devices with their start and end apart: 3, of which 3 were waited for; matrix products, arithmetic and copies ran while one was open for 2% of the time, Pallas kernels for 2%

profile of v8, /device:TPU:1, one launch (start us, length us, event | category | flops | bytes accessed | tf_op | source)
XLA Modules:
  0.0 53.1 jit_solution(4560582827279938524)
XLA Ops:
  0.0 3.2 %collective-permute-start.1 = (bf16[2,256,256]{2,1,0:T(8,128)(2,1)}, bf16[2,256,256]{2,1,0:T(8,128)(2,1)S(1)}, u32[]{:S(2)}, u32[]{:S(2)}) collective-permute-start(bf16[2,256,256]{2,1,0:T(8,128)(2,1)} %amp_own.1), channel_id=1, source_target_pairs={{0,2},{2,0},{4,6},{6,4},{8,10},{10,8},{12,14},{14,12},{16,18},{18,... | collective-permute-start | bytes 786440 | tf_op jit(solution)/shard_map/ppermute | solution.py:342
  3.2 0.1 collective-permute-start
  3.3 1.1 %dynamic-slice_bitcast_fusion.table = bf16[1152,256]{1,0:T(8,128)(2,1)S(1)} fusion(bf16[2,1152,256]{2,1,0:T(8,128)(2,1)} %constant.50.clone, s32[]{:T(128)S(6)} %select_n.12), kind=kLoop, calls=%fused_computation | loop fusion | bytes 1179652 | tf_op jit(solution)/shard_map/jit(dynamic_index_in_dim)/squeeze | solution.py:343
  4.4 0.0 copy-start.8
  4.5 0.0 copy-start.9
  4.5 0.0 copy-start.10
  4.5 0.0 copy-start.11
  4.5 0.0 copy-start.12
  4.5 0.0 copy-start.13
  4.5 0.1 collective-permute-done.1.amp_other
  4.6 0.4 collective-permute-done.rho_other
  5.0 0.0 copy-done.1
  5.0 0.0 copy-done.7
  5.0 0.0 copy-done.6
  5.0 1.2 %shard_map.145 = s32[1024,128]{1,0:T(8,128)S(1)} custom-call(bf16[2,256,256]{2,1,0:T(8,128)(2,1)S(1)} %copy-done.6, bf16[2,256,256]{2,1,0:T(8,128)(2,1)S(1)} %copy-done.7, bf16[2,256,256]{2,1,0:T(8,128)(2,1)S(1)} %collective-permute-done.rho_other, bf16[2,256,256]{2,1,0:T(8,128)(2,1)S(1)} %collective-permute-done.1.amp_other, ...), custom_call_target="tpu_custom_call" | custom-call | flops 800000000 | bytes 2097152 | tf_op jit(solution)/shard_map/pallas_call | solution.py:314
  6.2 24.2 %all_to_all.10 = s32[64,16,128]{2,1,0:T(8,128)S(1)} all-to-all(s32[64,16,128]{2,1,0:T(8,128)S(1)} %bitcast.10), channel_id=1, replica_groups={{176,180,184,188,160,164,168,172,144,148,152,156,128,132,136,140,240,24..., dimensions={0} | all-to-all | bytes 1048576 | tf_op jit(solution)/shard_map/all_to_all | solution.py:334
  30.4 0.0 copy-done.8
  30.4 0.0 copy-done.9
  30.4 0.0 copy-done.10
  30.4 0.0 copy-start
  30.5 0.0 copy-start.2
  30.5 0.0 copy-start.3
  30.5 0.0 copy-start.4
  30.5 0.0 copy-start.5
  30.5 1.2 %shard_map.146 = s32[512,128]{1,0:T(8,128)S(1)} custom-call(s32[1]{0:T(128)} %bitcast.core_ref, s32[1024,128]{1,0:T(8,128)S(1)} %bitcast.9, bf16[2,256,256]{2,1,0:T(8,128)(2,1)S(1)} %copy-done.12, bf16[2,256,256]{2,1,0:T(8,128)(2,1)S(1)} %copy-done.11, bf16[2,256,256]{2,1,0:T(8,128)(2,1)S(1)} %copy-done.10, bf16[2,256,256]{2,1,0:T(8,128)(2,1)S(1)} %copy-done.9, ...), custom_call_target="tpu_custom_call" | custom-call | flops 800000000 | bytes 2097152 | tf_op jit(solution)/shard_map/pallas_call | solution.py:314
  31.7 16.8 %all_to_all.11 = s32[64,8,128]{2,1,0:T(8,128)S(1)} all-to-all(s32[64,8,128]{2,1,0:T(8,128)S(1)} %bitcast.11), channel_id=1, replica_groups={{176,180,184,188,160,164,168,172,144,148,152,156,128,132,136,140,240,24..., dimensions={0} | all-to-all | bytes 524288 | tf_op jit(solution)/shard_map/all_to_all | solution.py:334
  48.5 1.8 %collective-permute-start.2 = (s32[512,128]{1,0:T(8,128)S(1)}, s32[512,128]{1,0:T(8,128)S(1)}, u32[]{:S(2)}, u32[]{:S(2)}) collective-permute-start(s32[512,128]{1,0:T(8,128)S(1)} %bitcast.7), channel_id=1, source_target_pairs={{0,2},{2,0},{4,6},{6,4},{8,10},{10,8},{12,14},{14,12},{16,18},{18,... | collective-permute-start | bytes 786440 | tf_op jit(solution)/shard_map/ppermute | solution.py:361
  50.3 0.0 copy-done.2
  50.3 0.0 copy-done.4
  50.3 0.9 %shard_map.147.partial = f32[2,256,256]{2,1,0:T(8,128)S(1)} custom-call(s32[1]{0:T(128)} %bitcast.core_ref, s32[512,128]{1,0:T(8,128)S(1)} %bitcast.8, bf16[2,256,256]{2,1,0:T(8,128)(2,1)S(1)} %copy-done.6, s32[2,256,256]{2,1,0:T(8,128)S(1)} %copy-done, bf16[256,256]{1,0:T(8,128)(2,1)S(1)} %copy-done.5, bf16[256,256]{1,0:T(8,128)(2,1)S(1)} %copy-done.4, ...), custom_call_target="tpu_custom_call" | custom-call | flops 400000000 | bytes 2097152 | tf_op jit(solution)/shard_map/pallas_call | solution.py:314
  51.3 0.2 collective-permute-done.2.other
  51.5 1.6 %shard_map.148 = bf16[2,256,256]{2,1,0:T(8,128)(2,1)} custom-call(s32[1]{0:T(128)} %bitcast.core_ref, f32[2,256,256]{2,1,0:T(8,128)S(1)} %shard_map.147.partial, s32[512,128]{1,0:T(8,128)S(1)} %collective-permute-done.2.other, s32[2,256,256]{2,1,0:T(8,128)S(1)} %copy-done, bf16[256,256]{1,0:T(8,128)(2,1)S(1)} %copy-done.5, bf16[256,256]{1,0:T(8,128)(2,1)S(1)} %copy-done.4, ...), custom_call_target="tpu_custom_call" | custom-call | flops 400000000 | bytes 2097152 | tf_op jit(solution)/shard_map/pallas_call | solution.py:314
  (9 shorter events, 0.0 us)
Async XLA Ops:
  0.0 5.0 %copy-start.1 = (f32[2,128,128]{2,1,0:T(8,128)S(1)}, f32[2,128,128]{2,1,0:T(8,128)}, u32[]{:S(2)}) copy-start(f32[2,128,128]{2,1,0:T(8,128)} %constant.49.clone.tw) | copy-start | bytes 393220
  0.0 5.0 %copy-start.7 = (bf16[2,256,256]{2,1,0:T(8,128)(2,1)S(1)}, bf16[2,256,256]{2,1,0:T(8,128)(2,1)}, u32[]{:S(2)}) copy-start(bf16[2,256,256]{2,1,0:T(8,128)(2,1)} %amp_own.1) | copy-start | bytes 786436
  0.0 5.0 %copy-start.6 = (bf16[2,256,256]{2,1,0:T(8,128)(2,1)S(1)}, bf16[2,256,256]{2,1,0:T(8,128)(2,1)}, u32[]{:S(2)}) copy-start(bf16[2,256,256]{2,1,0:T(8,128)(2,1)} %rho_ref.1) | copy-start | bytes 786436
  0.0 4.6 %collective-permute-start.1 = (bf16[2,256,256]{2,1,0:T(8,128)(2,1)}, bf16[2,256,256]{2,1,0:T(8,128)(2,1)S(1)}, u32[]{:S(2)}, u32[]{:S(2)}) collective-permute-start(bf16[2,256,256]{2,1,0:T(8,128)(2,1)} %amp_own.1), channel_id=1, source_target_pairs={{0,2},{2,0},{4,6},{6,4},{8,10},{10,8},{12,14},{14,12},{16,18},{18,... | collective-permute-start | bytes 786440 | tf_op jit(solution)/shard_map/ppermute | solution.py:342
  3.2 1.7 %collective-permute-start = (bf16[2,256,256]{2,1,0:T(8,128)(2,1)}, bf16[2,256,256]{2,1,0:T(8,128)(2,1)S(1)}, u32[]{:S(2)}, u32[]{:S(2)}) collective-permute-start(bf16[2,256,256]{2,1,0:T(8,128)(2,1)} %rho_ref.1), channel_id=1, source_target_pairs={{0,2},{2,0},{4,6},{6,4},{8,10},{10,8},{12,14},{14,12},{16,18},{18,... | collective-permute-start | bytes 786440 | tf_op jit(solution)/shard_map/ppermute | solution.py:341
  4.4 26.0 %copy-start.8 = (f32[2,2,128,128]{3,2,1,0:T(8,128)S(1)}, f32[2,2,128,128]{3,2,1,0:T(8,128)}, u32[]{:S(2)}) copy-start(f32[2,2,128,128]{3,2,1,0:T(8,128)} %constant.58.clone.tzw) | copy-start | bytes 786436
  4.5 26.0 %copy-start.9 = (bf16[2,256,256]{2,1,0:T(8,128)(2,1)S(1)}, bf16[2,256,256]{2,1,0:T(8,128)(2,1)}, u32[]{:S(2)}) copy-start(bf16[2,256,256]{2,1,0:T(8,128)(2,1)} %constant.57.clone.tzil) | copy-start | bytes 786436
  4.5 25.9 %copy-start.10 = (bf16[2,256,256]{2,1,0:T(8,128)(2,1)S(1)}, bf16[2,256,256]{2,1,0:T(8,128)(2,1)}, u32[]{:S(2)}) copy-start(bf16[2,256,256]{2,1,0:T(8,128)(2,1)} %constant.56.clone.tzih) | copy-start | bytes 786436
  4.5 25.9 %copy-start.11 = (bf16[2,256,256]{2,1,0:T(8,128)(2,1)S(1)}, bf16[2,256,256]{2,1,0:T(8,128)(2,1)}, u32[]{:S(2)}) copy-start(bf16[2,256,256]{2,1,0:T(8,128)(2,1)} %constant.55.clone.tzl) | copy-start | bytes 786436
  4.5 25.9 %copy-start.12 = (bf16[2,256,256]{2,1,0:T(8,128)(2,1)S(1)}, bf16[2,256,256]{2,1,0:T(8,128)(2,1)}, u32[]{:S(2)}) copy-start(bf16[2,256,256]{2,1,0:T(8,128)(2,1)} %constant.54.clone.tzh) | copy-start | bytes 786436
  4.5 25.9 %copy-start.13 = (bf16[256,256]{1,0:T(8,128)(2,1)S(1)}, bf16[256,256]{1,0:T(8,128)(2,1)}, u32[]{:S(2)}) copy-start(bf16[256,256]{1,0:T(8,128)(2,1)} %constant.53.clone.rev) | copy-start | bytes 393220
  30.4 19.9 %copy-start = (s32[2,256,256]{2,1,0:T(8,128)S(1)}, s32[2,256,256]{2,1,0:T(8,128)}, u32[]{:S(2)}) copy-start(s32[2,256,256]{2,1,0:T(8,128)} %support.3) | copy-start | bytes 1572868
  30.5 19.9 %copy-start.2 = (bf16[2,128,256]{2,1,0:T(8,128)(2,1)S(1)}, bf16[2,128,256]{2,1,0:T(8,128)(2,1)}, u32[]{:S(2)}) copy-start(bf16[2,128,256]{2,1,0:T(8,128)(2,1)} %constant.52.clone.txl) | copy-start | bytes 393220
  30.5 19.9 %copy-start.3 = (bf16[2,128,256]{2,1,0:T(8,128)(2,1)S(1)}, bf16[2,128,256]{2,1,0:T(8,128)(2,1)}, u32[]{:S(2)}) copy-start(bf16[2,128,256]{2,1,0:T(8,128)(2,1)} %constant.51.clone.txh) | copy-start | bytes 393220
  30.5 19.8 %copy-start.4 = (bf16[256,256]{1,0:T(8,128)(2,1)S(1)}, bf16[256,256]{1,0:T(8,128)(2,1)}, u32[]{:S(2)}) copy-start(bf16[256,256]{1,0:T(8,128)(2,1)} %constant.48.clone.tyl) | copy-start | bytes 393220
  30.5 19.8 %copy-start.5 = (bf16[256,256]{1,0:T(8,128)(2,1)S(1)}, bf16[256,256]{1,0:T(8,128)(2,1)}, u32[]{:S(2)}) copy-start(bf16[256,256]{1,0:T(8,128)(2,1)} %constant.47.clone.tyh) | copy-start | bytes 393220
  48.5 3.0 %collective-permute-start.2 = (s32[512,128]{1,0:T(8,128)S(1)}, s32[512,128]{1,0:T(8,128)S(1)}, u32[]{:S(2)}, u32[]{:S(2)}) collective-permute-start(s32[512,128]{1,0:T(8,128)S(1)} %bitcast.7), channel_id=1, source_target_pairs={{0,2},{2,0},{4,6},{6,4},{8,10},{10,8},{12,14},{14,12},{16,18},{18,... | collective-permute-start | bytes 786440 | tf_op jit(solution)/shard_map/ppermute | solution.py:361

commit v9 on v8

--- a/solution.py
+++ b/solution.py
@@ -177,10 +177,10 @@
         for r in range(2):
             out[pl.ds(slot + r, CHIPS, stride=16), :] = words[CHIPS * r : CHIPS * (r + 1)]
 
-    lines = [along_x(p) for p in range(4)]
-    first = along_y(lines[0] + lines[1])
+    first = along_y(along_x(0) + along_x(1))
+    lines = along_x(2) + along_x(3)
     directs, mirrors = zip(*(picked(p) for p in range(4)))
-    second = along_y(lines[2] + lines[3])
+    second = along_y(lines)
     for q, words in enumerate(pack(*first, FORWARD_LOW)):
         store(2 * q, words)
     mirrors = mm(table[4 * N :, :HALF], jnp.concatenate(mirrors, 1).astype(jnp.bfloat16))

time: 53.3 us -> 53.3 us (level)
  no operation moved by 1% of the time
where the time goes in v9:
time: 53.3 us; the launch traced here: 53.1 us
  blocking collectives  41 us (77%)
  starting transfers between devices  5.12 us (10%)
  Pallas kernels  4.91 us (9%)
  local copies, waits for them, and re-layouts  1.19 us (2%)
  waiting for transfers between devices  0.68 us (1%)
    all_to_all x2, blocking collectives, exchange(): lax.all_to_all(x, 'slab', split_axis=0, concat_axis=0, tiled=True, axis_i...  41 us
    pallas_call x4, Pallas kernels, call(): pl.pallas_call(kernel, out_shape=out_shape, in_specs=in_specs, out_specs=...  4.91 us
    ppermute x1, starting transfers between devices, shards(): amplitudes_other = lax.ppermute(amplitudes, 'slab', swap)  3.24 us
    ppermute x1, starting transfers between devices, shards(): planes_other = lax.ppermute(planes, 'slab', swap)  1.79 us
    squeeze x1, local copies, waits for them, and re-layouts, shards(): table = lax.dynamic_index_in_dim(c['first'], core[0], 0, keepdims=False)  1.1 us
  transfers between devices with their start and end apart: 3, of which 3 were waited for; matrix products, arithmetic and copies ran while one was open for 2% of the time, Pallas kernels for 2%

profile of v9, /device:TPU:1, one launch (start us, length us, event | category | flops | bytes accessed | tf_op | source)
XLA Modules:
  0.0 53.1 jit_solution(646947944558313017)
XLA Ops:
  0.0 3.2 %collective-permute-start.1 = (bf16[2,256,256]{2,1,0:T(8,128)(2,1)}, bf16[2,256,256]{2,1,0:T(8,128)(2,1)S(1)}, u32[]{:S(2)}, u32[]{:S(2)}) collective-permute-start(bf16[2,256,256]{2,1,0:T(8,128)(2,1)} %amp_own.1), channel_id=1, source_target_pairs={{0,2},{2,0},{4,6},{6,4},{8,10},{10,8},{12,14},{14,12},{16,18},{18,... | collective-permute-start | bytes 786440 | tf_op jit(solution)/shard_map/ppermute | solution.py:342
  3.2 0.1 collective-permute-start
  3.3 1.1 %dynamic-slice_bitcast_fusion.table = bf16[1152,256]{1,0:T(8,128)(2,1)S(1)} fusion(bf16[2,1152,256]{2,1,0:T(8,128)(2,1)} %constant.50.clone, s32[]{:T(128)S(6)} %select_n.12), kind=kLoop, calls=%fused_computation | loop fusion | bytes 1179652 | tf_op jit(solution)/shard_map/jit(dynamic_index_in_dim)/squeeze | solution.py:343
  4.4 0.0 copy-start.8
  4.5 0.0 copy-start.9
  4.5 0.0 copy-start.10
  4.5 0.0 copy-start.11
  4.5 0.0 copy-start.12
  4.5 0.0 copy-start.13
  4.5 0.1 collective-permute-done.1.amp_other
  4.6 0.4 collective-permute-done.rho_other
  5.0 0.0 copy-done.1
  5.0 0.0 copy-done.7
  5.0 0.0 copy-done.6
  5.0 1.2 %shard_map.145 = s32[1024,128]{1,0:T(8,128)S(1)} custom-call(bf16[2,256,256]{2,1,0:T(8,128)(2,1)S(1)} %copy-done.6, bf16[2,256,256]{2,1,0:T(8,128)(2,1)S(1)} %copy-done.7, bf16[2,256,256]{2,1,0:T(8,128)(2,1)S(1)} %collective-permute-done.rho_other, bf16[2,256,256]{2,1,0:T(8,128)(2,1)S(1)} %collective-permute-done.1.amp_other, ...), custom_call_target="tpu_custom_call" | custom-call | flops 800000000 | bytes 2097152 | tf_op jit(solution)/shard_map/pallas_call | solution.py:314
  6.2 24.2 %all_to_all.10 = s32[64,16,128]{2,1,0:T(8,128)S(1)} all-to-all(s32[64,16,128]{2,1,0:T(8,128)S(1)} %bitcast.10), channel_id=1, replica_groups={{176,180,184,188,160,164,168,172,144,148,152,156,128,132,136,140,240,24..., dimensions={0} | all-to-all | bytes 1048576 | tf_op jit(solution)/shard_map/all_to_all | solution.py:334
  30.4 0.0 copy-done.10
  30.4 0.0 copy-done.11
  30.5 0.0 copy-done.12
  30.5 0.0 copy-done.13
  30.5 0.0 copy-start
  30.5 0.0 copy-start.2
  30.5 0.0 copy-start.3
  30.5 0.0 copy-start.4
  30.5 0.0 copy-start.5
  30.5 1.2 %shard_map.146 = s32[512,128]{1,0:T(8,128)S(1)} custom-call(s32[1]{0:T(128)} %bitcast.core_ref, s32[1024,128]{1,0:T(8,128)S(1)} %bitcast.9, bf16[2,256,256]{2,1,0:T(8,128)(2,1)S(1)} %copy-done.12, bf16[2,256,256]{2,1,0:T(8,128)(2,1)S(1)} %copy-done.11, bf16[2,256,256]{2,1,0:T(8,128)(2,1)S(1)} %copy-done.10, bf16[2,256,256]{2,1,0:T(8,128)(2,1)S(1)} %copy-done.9, ...), custom_call_target="tpu_custom_call" | custom-call | flops 800000000 | bytes 2097152 | tf_op jit(solution)/shard_map/pallas_call | solution.py:314
  31.8 16.8 %all_to_all.11 = s32[64,8,128]{2,1,0:T(8,128)S(1)} all-to-all(s32[64,8,128]{2,1,0:T(8,128)S(1)} %bitcast.11), channel_id=1, replica_groups={{176,180,184,188,160,164,168,172,144,148,152,156,128,132,136,140,240,24..., dimensions={0} | all-to-all | bytes 524288 | tf_op jit(solution)/shard_map/all_to_all | solution.py:334
  48.6 1.8 %collective-permute-start.2 = (s32[512,128]{1,0:T(8,128)S(1)}, s32[512,128]{1,0:T(8,128)S(1)}, u32[]{:S(2)}, u32[]{:S(2)}) collective-permute-start(s32[512,128]{1,0:T(8,128)S(1)} %bitcast.7), channel_id=1, source_target_pairs={{0,2},{2,0},{4,6},{6,4},{8,10},{10,8},{12,14},{14,12},{16,18},{18,... | collective-permute-start | bytes 786440 | tf_op jit(solution)/shard_map/ppermute | solution.py:361
  50.4 0.0 copy-done.2
  50.4 0.9 %shard_map.147.partial = f32[2,256,256]{2,1,0:T(8,128)S(1)} custom-call(s32[1]{0:T(128)} %bitcast.core_ref, s32[512,128]{1,0:T(8,128)S(1)} %bitcast.8, bf16[2,256,256]{2,1,0:T(8,128)(2,1)S(1)} %copy-done.6, s32[2,256,256]{2,1,0:T(8,128)S(1)} %copy-done, bf16[256,256]{1,0:T(8,128)(2,1)S(1)} %copy-done.5, bf16[256,256]{1,0:T(8,128)(2,1)S(1)} %copy-done.4, ...), custom_call_target="tpu_custom_call" | custom-call | flops 400000000 | bytes 2097152 | tf_op jit(solution)/shard_map/pallas_call | solution.py:314
  51.3 0.2 collective-permute-done.2.other
  51.5 1.6 %shard_map.148 = bf16[2,256,256]{2,1,0:T(8,128)(2,1)} custom-call(s32[1]{0:T(128)} %bitcast.core_ref, f32[2,256,256]{2,1,0:T(8,128)S(1)} %shard_map.147.partial, s32[512,128]{1,0:T(8,128)S(1)} %collective-permute-done.2.other, s32[2,256,256]{2,1,0:T(8,128)S(1)} %copy-done, bf16[256,256]{1,0:T(8,128)(2,1)S(1)} %copy-done.5, bf16[256,256]{1,0:T(8,128)(2,1)S(1)} %copy-done.4, ...), custom_call_target="tpu_custom_call" | custom-call | flops 400000000 | bytes 2097152 | tf_op jit(solution)/shard_map/pallas_call | solution.py:314
  (9 shorter events, 0.0 us)
Async XLA Ops:
  0.0 5.0 %copy-start.1 = (f32[2,128,128]{2,1,0:T(8,128)S(1)}, f32[2,128,128]{2,1,0:T(8,128)}, u32[]{:S(2)}) copy-start(f32[2,128,128]{2,1,0:T(8,128)} %constant.49.clone.tw) | copy-start | bytes 393220
  0.0 5.0 %copy-start.7 = (bf16[2,256,256]{2,1,0:T(8,128)(2,1)S(1)}, bf16[2,256,256]{2,1,0:T(8,128)(2,1)}, u32[]{:S(2)}) copy-start(bf16[2,256,256]{2,1,0:T(8,128)(2,1)} %amp_own.1) | copy-start | bytes 786436
  0.0 5.0 %copy-start.6 = (bf16[2,256,256]{2,1,0:T(8,128)(2,1)S(1)}, bf16[2,256,256]{2,1,0:T(8,128)(2,1)}, u32[]{:S(2)}) copy-start(bf16[2,256,256]{2,1,0:T(8,128)(2,1)} %rho_ref.1) | copy-start | bytes 786436
  0.0 4.6 %collective-permute-start.1 = (bf16[2,256,256]{2,1,0:T(8,128)(2,1)}, bf16[2,256,256]{2,1,0:T(8,128)(2,1)S(1)}, u32[]{:S(2)}, u32[]{:S(2)}) collective-permute-start(bf16[2,256,256]{2,1,0:T(8,128)(2,1)} %amp_own.1), channel_id=1, source_target_pairs={{0,2},{2,0},{4,6},{6,4},{8,10},{10,8},{12,14},{14,12},{16,18},{18,... | collective-permute-start | bytes 786440 | tf_op jit(solution)/shard_map/ppermute | solution.py:342
  3.2 1.7 %collective-permute-start = (bf16[2,256,256]{2,1,0:T(8,128)(2,1)}, bf16[2,256,256]{2,1,0:T(8,128)(2,1)S(1)}, u32[]{:S(2)}, u32[]{:S(2)}) collective-permute-start(bf16[2,256,256]{2,1,0:T(8,128)(2,1)} %rho_ref.1), channel_id=1, source_target_pairs={{0,2},{2,0},{4,6},{6,4},{8,10},{10,8},{12,14},{14,12},{16,18},{18,... | collective-permute-start | bytes 786440 | tf_op jit(solution)/shard_map/ppermute | solution.py:341
  4.4 26.0 %copy-start.8 = (f32[2,2,128,128]{3,2,1,0:T(8,128)S(1)}, f32[2,2,128,128]{3,2,1,0:T(8,128)}, u32[]{:S(2)}) copy-start(f32[2,2,128,128]{3,2,1,0:T(8,128)} %constant.58.clone.tzw) | copy-start | bytes 786436
  4.5 26.0 %copy-start.9 = (bf16[2,256,256]{2,1,0:T(8,128)(2,1)S(1)}, bf16[2,256,256]{2,1,0:T(8,128)(2,1)}, u32[]{:S(2)}) copy-start(bf16[2,256,256]{2,1,0:T(8,128)(2,1)} %constant.57.clone.tzil) | copy-start | bytes 786436
  4.5 26.0 %copy-start.10 = (bf16[2,256,256]{2,1,0:T(8,128)(2,1)S(1)}, bf16[2,256,256]{2,1,0:T(8,128)(2,1)}, u32[]{:S(2)}) copy-start(bf16[2,256,256]{2,1,0:T(8,128)(2,1)} %constant.56.clone.tzih) | copy-start | bytes 786436
  4.5 26.0 %copy-start.11 = (bf16[2,256,256]{2,1,0:T(8,128)(2,1)S(1)}, bf16[2,256,256]{2,1,0:T(8,128)(2,1)}, u32[]{:S(2)}) copy-start(bf16[2,256,256]{2,1,0:T(8,128)(2,1)} %constant.55.clone.tzl) | copy-start | bytes 786436
  4.5 26.0 %copy-start.12 = (bf16[2,256,256]{2,1,0:T(8,128)(2,1)S(1)}, bf16[2,256,256]{2,1,0:T(8,128)(2,1)}, u32[]{:S(2)}) copy-start(bf16[2,256,256]{2,1,0:T(8,128)(2,1)} %constant.54.clone.tzh) | copy-start | bytes 786436
  4.5 26.0 %copy-start.13 = (bf16[256,256]{1,0:T(8,128)(2,1)S(1)}, bf16[256,256]{1,0:T(8,128)(2,1)}, u32[]{:S(2)}) copy-start(bf16[256,256]{1,0:T(8,128)(2,1)} %constant.53.clone.rev) | copy-start | bytes 393220
  30.5 19.9 %copy-start = (s32[2,256,256]{2,1,0:T(8,128)S(1)}, s32[2,256,256]{2,1,0:T(8,128)}, u32[]{:S(2)}) copy-start(s32[2,256,256]{2,1,0:T(8,128)} %support.3) | copy-start | bytes 1572868
  30.5 19.9 %copy-start.2 = (bf16[2,128,256]{2,1,0:T(8,128)(2,1)S(1)}, bf16[2,128,256]{2,1,0:T(8,128)(2,1)}, u32[]{:S(2)}) copy-start(bf16[2,128,256]{2,1,0:T(8,128)(2,1)} %constant.52.clone.txl) | copy-start | bytes 393220
  30.5 19.9 %copy-start.3 = (bf16[2,128,256]{2,1,0:T(8,128)(2,1)S(1)}, bf16[2,128,256]{2,1,0:T(8,128)(2,1)}, u32[]{:S(2)}) copy-start(bf16[2,128,256]{2,1,0:T(8,128)(2,1)} %constant.51.clone.txh) | copy-start | bytes 393220
  30.5 19.8 %copy-start.4 = (bf16[256,256]{1,0:T(8,128)(2,1)S(1)}, bf16[256,256]{1,0:T(8,128)(2,1)}, u32[]{:S(2)}) copy-start(bf16[256,256]{1,0:T(8,128)(2,1)} %constant.48.clone.tyl) | copy-start | bytes 393220
  30.5 19.8 %copy-start.5 = (bf16[256,256]{1,0:T(8,128)(2,1)S(1)}, bf16[256,256]{1,0:T(8,128)(2,1)}, u32[]{:S(2)}) copy-start(bf16[256,256]{1,0:T(8,128)(2,1)} %constant.47.clone.tyh) | copy-start | bytes 393220
  48.6 3.0 %collective-permute-start.2 = (s32[512,128]{1,0:T(8,128)S(1)}, s32[512,128]{1,0:T(8,128)S(1)}, u32[]{:S(2)}, u32[]{:S(2)}) collective-permute-start(s32[512,128]{1,0:T(8,128)S(1)} %bitcast.7), channel_id=1, source_target_pairs={{0,2},{2,0},{4,6},{6,4},{8,10},{10,8},{12,14},{14,12},{16,18},{18,... | collective-permute-start | bytes 786440 | tf_op jit(solution)/shard_map/ppermute | solution.py:361
